TPU v7x, 128 devices: a whole 4x4x4 slice. The times are simulated.
128 devices in a mesh: dp: 32 (over z, y, core), mp: 4 (over x).
Axes of the slice: x: 4, y: 4, z: 4, core: 2. Of those that a mesh axis runs over, the one named last changes fastest.
Arguments:
- events: bfloat16 [98304, 1024], P('dp'), may hold values from -6 to 6
- upstream: bfloat16 [98304, 1024], P('dp'), may hold values from -1.5 to 1.5
- proj_weight: bfloat16 [1024, 4, 1024], P(None, None, 'mp'), may hold values from -0.1875 to 0.1875
- proj_bias: float32 [4, 1024], P(None, 'mp'), may hold values from -3 to 3
- norm_gain: float32 [1024], P('mp'), may hold values from 0.1 to 1.9
- out_weight: bfloat16 [1024, 1024], P('mp'), may hold values from -0.1875 to 0.1875
- lengths: int32 [32, 48], replicated, may hold values from 0 to 3, as said below
- owners: int32 [32, 48], replicated, may hold values from 0 to 31, as said below
Outputs:
- event_grads: bfloat16 [98304, 1024], P('dp', 'mp')
- proj_weight_grad: float32 [1024, 4, 1024], P(None, None, 'mp')
- proj_bias_grad: float32 [4, 1024], P(None, 'mp')
- norm_gain_grad: float32 [1024], P('mp')
- out_weight_grad: float32 [1024, 1024], P('mp')
Inputs may be any that keep to these rules, and one draw needn't show every extreme that they name: Each home's histories fill its tiles from the first tile on, zero lengths only after the last history; some home has all 48 tiles filled, and some history has exactly 3 tiles. The histories one home gives one dp index hold 0 or exactly 3 tiles, and every home gives itself 3; one dp index is given at most 21 tiles in all, and some dp index exactly that. `owners`: entries of zero-length histories carry no meaning. The result does not depend on this map.
All inputs are finite; a program needn't handle non-finite values.
Results may differ from a plain program's by a relative error of at most 0.004.
The roundings to bfloat16 on the way count: a program that leaves them out, or rounds other values in their place, can miss the bound.
Values may be sent and summed in bfloat16 or wider, within the bound.
No kernel may reach another device: no remote copies, remote signals or barrier semaphores. Data moves between devices by JAX's collectives and lax.ppermute only.
A program may use at most 192 MiB of HBM per device.

v0:
```python
import functools

import jax
import jax.numpy as jnp
from jax import lax
from jax.experimental import pallas as pl
from jax.experimental.pallas import tpu as pltpu
from jax.sharding import Mesh, PartitionSpec as P

HEADS = 8
TILE = 64
EPSILON = 1e-05
STEP = 512
PAIR = 128
HEAD = 128
WIDTH = 256
SPAN = 512
MODEL = 1024
COLUMNS = 5 * WIDTH + 128
PIECES = 8
ROW_PARTS = 3
F32 = jnp.float32
BF16 = jnp.bfloat16
NT = (((1,), (1,)), ((), ()))
TN = (((0,), (0,)), ((), ()))
DP = ("z", "y", "c")


def dot(a, b, dims=(((1,), (0,)), ((), ()))):
    return lax.dot_general(a, b, dims, preferred_element_type=F32)


def sigmoid(v):
    return 0.5 * jnp.tanh(0.5 * v) + 0.5


def tile_column(values, rows):
    ids = lax.broadcasted_iota(jnp.int32, (rows, 1), 0)
    column = jnp.full((rows, 1), values[0], jnp.int32)
    for i in range(1, len(values)):
        column = jnp.where(ids >= i * TILE, values[i], column)
    return column


def layer_kernel(
    steps, first_ref, core_ref, x_ref, g_ref, xp_ref, w_ref, wo_ref, b_ref, gain_ref, ones_ref,
    pg_out, sent_out, mine_out,
    kv, dkv, sl, pgq, gq, slgq, hg, hid, pgs, acc, sums, attn_s, dsl_s, mix_s, dm_s,
):
    j = pl.program_id(0)
    cur = pl.ds(STEP, STEP)
    old = pl.ds(0, STEP)
    pairs = STEP // PAIR
    chains = [(i, h) for i in range(pairs) for h in range(2)]

    @pl.when(j == 0)
    def _():
        kv[old] = jnp.zeros((STEP, SPAN), BF16)
        dkv[old] = jnp.zeros((STEP, SPAN), F32)
        sl[old] = jnp.zeros((STEP, SPAN), F32)
        pgq[...] = jnp.zeros((STEP, SPAN), BF16)
        pgs[...] = jnp.zeros(pgs.shape, BF16)
        acc[...] = jnp.zeros(acc.shape, F32)
        sums[...] = jnp.zeros(sums.shape, F32)

    def in_grad_piece(n):
        depth = MODEL // PIECES
        r = slice(n * depth, (n + 1) * depth)
        acc[r, 0 : 4 * WIDTH] += dot(xp_ref[:, r], pgs[...], TN)

    def finish():
        pg_out[:, 0:WIDTH] = pgq[:, 0:WIDTH]
        pg_out[:, WIDTH : 2 * WIDTH] = (dkv[old, 0:WIDTH] * sl[old, 0:WIDTH]).astype(BF16)
        pg_out[:, 2 * WIDTH : 3 * WIDTH] = pgq[:, WIDTH:]
        pg_out[:, 3 * WIDTH :] = (dkv[old, WIDTH:] * sl[old, WIDTH:]).astype(BF16)
        grads = pg_out[...]
        pgs[...] = grads
        sums[:, 0 : 4 * WIDTH] += jnp.sum(grads.astype(F32).reshape(STEP // 8, 8, 4 * WIDTH), axis=0)

    def rows_of(i):
        return slice(i * PAIR, (i + 1) * PAIR)

    def window(i):
        return pl.ds(STEP - PAIR + i * PAIR, 2 * PAIR)

    def first_cols(h):
        return slice(h * HEAD, (h + 1) * HEAD)

    def second_cols(h):
        return slice(WIDTH + h * HEAD, WIDTH + (h + 1) * HEAD)

    def query():
        t0 = j * (STEP // TILE)
        firsts = [first_ref[t0 + i] for i in range(STEP // TILE)]
        base = j * STEP
        starts = [jnp.where(f >= 0, f * TILE - base, STEP) for f in firsts]
        x = x_ref[...]
        used = tile_column(firsts, STEP) >= 0
        g = jnp.where(used, g_ref[...], jnp.zeros((), BF16))
        hg[...] = dot(g, wo_ref[...], NT)
        for part in range(4):
            cols = slice(part * WIDTH, (part + 1) * WIDTH)
            pre = dot(x, w_ref[:, cols]) + b_ref[:, cols]
            sig = sigmoid(pre)
            act = pre * sig
            slope = sig + act * (1.0 - sig)
            half = slice(0, WIDTH) if part < 2 else slice(WIDTH, SPAN)
            if part % 2 == 0:
                gq[:, half] = act.astype(BF16)
                slgq[:, half] = slope
            else:
                kv[cur, half] = act.astype(BF16)
                sl[cur, half] = slope
        scale = HEAD**-0.5
        row = lax.broadcasted_iota(jnp.int32, (PAIR, 2 * PAIR), 0)
        col = lax.broadcasted_iota(jnp.int32, (PAIR, 2 * PAIR), 1) - PAIR
        visible = []
        for i in range(pairs):
            begin = tile_column(starts[2 * i : 2 * i + 2], PAIR) - i * PAIR
            visible.append((col >= begin) & (col <= row))
        for n, (i, h) in enumerate(chains):
            s = dot(gq[rows_of(i), second_cols(h)], kv[window(i), second_cols(h)], NT) * scale
            sig = jnp.where(visible[i], sigmoid(s), 0.0)
            a = s * sig
            attn = a.astype(BF16)
            attn_s[i, h] = attn
            dsl_s[i, h] = (sig + a * (1.0 - sig)) * scale
            mix_s[rows_of(i), first_cols(h)] = dot(attn, kv[window(i), first_cols(h)])
            for t in range(n * PIECES // len(chains), (n + 1) * PIECES // len(chains)):
                in_grad_piece(t)
        ones = ones_ref[...]
        mix = mix_s[...]
        high = mix.astype(BF16)
        low = (mix - high.astype(F32)).astype(BF16)
        centered = mix - (dot(high, ones) + dot(low, ones))
        inverse = lax.rsqrt(dot((centered * centered).astype(BF16), ones) + EPSILON)
        normed = centered * inverse
        gate = gq[:, 0:WIDTH].astype(F32)
        gain = gain_ref[...]
        local = hg[...]
        scaled = normed * gain
        hid[...] = (scaled * gate).astype(BF16)
        gq[:, 0:WIDTH] = (local * scaled * slgq[:, 0:WIDTH]).astype(BF16)
        lg = local * gate
        gn = lg * normed
        sums[:, 4 * WIDTH :] += jnp.sum(gn.reshape(STEP // 8, 8, WIDTH), axis=0)
        ng = lg * gain
        mean_one = dot(ng.astype(BF16), ones)
        mean_two = dot((gn * gain).astype(BF16), ones)
        dm_s[...] = ((ng - mean_one - normed * mean_two) * inverse).astype(BF16)
        for i, h in chains:
            hc, kc = first_cols(h), second_cols(h)
            dm = dm_s[rows_of(i), hc]
            q = gq[rows_of(i), kc]
            da = dot(dm, kv[window(i), hc], NT)
            sg = (da * dsl_s[i, h]).astype(BF16)
            dq = dot(sg, kv[window(i), kc])
            dv = dot(attn_s[i, h], dm, TN)
            dk = dot(sg, q, TN)
            before = pl.ds(STEP - PAIR + i * PAIR, PAIR)
            here = pl.ds(STEP + i * PAIR, PAIR)
            dkv[before, hc] += dv[:PAIR]
            dkv[here, hc] = dv[PAIR:]
            dkv[before, kc] += dk[:PAIR]
            dkv[here, kc] = dk[PAIR:]
            gq[rows_of(i), kc] = (dq * slgq[rows_of(i), kc]).astype(BF16)
        acc[:, 4 * WIDTH : 5 * WIDTH] += dot(g, hid[...], TN)

    @pl.when(j < steps)
    def _():
        query()
        finish()
        kv[old] = kv[cur]
        dkv[old] = dkv[cur]
        sl[old] = sl[cur]
        pgq[...] = gq[...]

    @pl.when(j == steps)
    def _():
        for n in range(PIECES):
            in_grad_piece(n)
        finish()

    @pl.when(j == steps + 1)
    def _():
        for n in range(PIECES):
            in_grad_piece(n)
        total = jnp.sum(sums[...], axis=0, keepdims=True)
        for p in range(5 * WIDTH // 128):
            acc[pl.ds(32 * p, 8), 5 * WIDTH :] = jnp.broadcast_to(total[:, p * 128 : (p + 1) * 128], (8, 128))
        core = core_ref[0]
        half = MODEL // 2
        mine_out[...] = acc[pl.ds(pl.multiple_of(core * half, half), half), :]
        sent_out[...] = acc[pl.ds(pl.multiple_of((1 - core) * half, half), half), :].astype(BF16)


def layer(first_tile, core, x, g, w, wo, bias, gain):
    rows = x.shape[0]
    steps = rows // STEP
    half = MODEL // 2
    ones = jnp.kron(jnp.eye(2, dtype=F32), jnp.full((HEAD, HEAD), 1.0 / HEAD, F32)).astype(BF16)

    def in_block(j, *_):
        return (jnp.minimum(j, steps - 1), 0)

    def out_block(j, *_):
        return (jnp.clip(j - 1, 0, steps - 1), 0)

    def late_block(j, *_):
        return (jnp.maximum(j - 2, 0), 0)

    def whole(j, *_):
        return (0, 0)

    macs = rows * (MODEL * MODEL * 2 + 2 * WIDTH * MODEL + 6 * WIDTH * WIDTH)
    return pl.pallas_call(
        functools.partial(layer_kernel, steps),
        out_shape=[
            jax.ShapeDtypeStruct((rows, MODEL), BF16),
            jax.ShapeDtypeStruct((half, COLUMNS), BF16),
            jax.ShapeDtypeStruct((half, COLUMNS), F32),
        ],
        grid_spec=pltpu.PrefetchScalarGridSpec(
            num_scalar_prefetch=2,
            grid=(steps + 2,),
            in_specs=[
                pl.BlockSpec((STEP, MODEL), in_block),
                pl.BlockSpec((STEP, MODEL), in_block),
                pl.BlockSpec((STEP, MODEL), late_block),
                pl.BlockSpec(w.shape, whole),
                pl.BlockSpec(wo.shape, whole),
                pl.BlockSpec(bias.shape, whole),
                pl.BlockSpec(gain.shape, whole),
                pl.BlockSpec(ones.shape, whole),
            ],
            out_specs=[
                pl.BlockSpec((STEP, MODEL), out_block),
                pl.BlockSpec((half, COLUMNS), whole),
                pl.BlockSpec((half, COLUMNS), whole),
            ],
            scratch_shapes=[
                pltpu.VMEM((2 * STEP, SPAN), BF16),
                pltpu.VMEM((2 * STEP, SPAN), F32),
                pltpu.VMEM((2 * STEP, SPAN), F32),
                pltpu.VMEM((STEP, SPAN), BF16),
                pltpu.VMEM((STEP, SPAN), BF16),
                pltpu.VMEM((STEP, SPAN), F32),
                pltpu.VMEM((STEP, WIDTH), F32),
                pltpu.VMEM((STEP, WIDTH), BF16),
                pltpu.VMEM((STEP, MODEL), BF16),
                pltpu.VMEM((MODEL, COLUMNS), F32),
                pltpu.VMEM((8, 5 * WIDTH), F32),
                pltpu.VMEM((STEP // PAIR, 2, PAIR, 2 * PAIR), BF16),
                pltpu.VMEM((STEP // PAIR, 2, PAIR, 2 * PAIR), F32),
                pltpu.VMEM((STEP, WIDTH), F32),
                pltpu.VMEM((STEP, WIDTH), BF16),
            ],
        ),
        compiler_params=pltpu.CompilerParams(
            dimension_semantics=("arbitrary",), vmem_limit_bytes=56 * 1024 * 1024
        ),
        cost_estimate=pl.CostEstimate(flops=2 * macs, bytes_accessed=rows * 8000, transcendentals=rows * 2048),
        name="layer",
    )(first_tile, core, x, g, x, w, wo, bias, gain, ones)


def partial_kernel(pg_ref, w_ref, out_ref):
    grads = pg_ref[...]
    for d in range(4):
        out_ref[d] = dot(grads, w_ref[d * WIDTH : (d + 1) * WIDTH, :], NT).astype(BF16)


def partial_rows(grads, w, begin, count):
    block = 512
    return pl.pallas_call(
        partial_kernel,
        out_shape=jax.ShapeDtypeStruct((4, count, WIDTH), BF16),
        grid=(count // block,),
        in_specs=[
            pl.BlockSpec((block, MODEL), lambda i: (begin // block + i, 0)),
            pl.BlockSpec(w.shape, lambda i: (0, 0)),
        ],
        out_specs=pl.BlockSpec((4, block, WIDTH), lambda i: (0, i, 0)),
        compiler_params=pltpu.CompilerParams(
            dimension_semantics=("arbitrary",), vmem_limit_bytes=32 * 1024 * 1024
        ),
        cost_estimate=pl.CostEstimate(
            flops=2 * count * MODEL * MODEL, bytes_accessed=count * 4096 + w.size * 2, transcendentals=0
        ),
        name="partial_rows",
    )(grads, w)


def event_kernel(begin, block, first_ref, part_ref, got_ref, g_ref, *refs):
    out_ref = refs[-1]
    t0 = (begin + pl.program_id(0) * block) // TILE
    firsts = [first_ref[t0 + i] for i in range(block // TILE)]
    used = tile_column(firsts, block) >= 0
    g = jnp.where(used, g_ref[...], jnp.zeros((), BF16)).astype(F32)
    total = (got_ref[0].astype(F32) + got_ref[1].astype(F32)) + (got_ref[2].astype(F32) + got_ref[3].astype(F32))
    out_ref[...] = (total + g).astype(BF16)


def event_rows(first_tile, part, got, g, begin, out):
    block = 512
    count = got.shape[1]
    in_specs = [
        pl.BlockSpec((4, block, WIDTH), lambda i, f, p: (0, i, 0)),
        pl.BlockSpec((block, WIDTH), lambda i, f, p: (begin // block + i, p[0])),
    ]
    operands = [got, g]
    aliases = {}
    if out is not None:
        in_specs.append(pl.BlockSpec(memory_space=pl.ANY))
        operands.append(out)
        aliases = {4: 0}
    return pl.pallas_call(
        functools.partial(event_kernel, begin, block),
        out_shape=jax.ShapeDtypeStruct((g.shape[0], WIDTH), BF16),
        grid_spec=pltpu.PrefetchScalarGridSpec(
            num_scalar_prefetch=2,
            grid=(count // block,),
            in_specs=in_specs,
            out_specs=pl.BlockSpec((block, WIDTH), lambda i, f, p: (begin // block + i, 0)),
        ),
        input_output_aliases=aliases,
        compiler_params=pltpu.CompilerParams(
            dimension_semantics=("arbitrary",), vmem_limit_bytes=16 * 1024 * 1024
        ),
        cost_estimate=pl.CostEstimate(flops=count * 2048, bytes_accessed=count * 3072, transcendentals=0),
        name="event_rows",
    )(first_tile, part, *operands)


def weights_kernel(core_ref, mine_ref, other_ref, pw_out, ow_out, small_out):
    i = pl.program_id(0)
    half = MODEL // 2
    own = core_ref[0] == i

    def write(ref):
        values = ref[...].astype(F32) * (1.0 / 32.0)
        for p in range(4):
            pw_out[:, p, :] = values[:, p * WIDTH : (p + 1) * WIDTH]
        ow_out[...] = values[:, 4 * WIDTH : 5 * WIDTH].T

        @pl.when(i == 0)
        def _():
            for p in range(5 * WIDTH // 128):
                small_out[:, p * 128 : (p + 1) * 128] = values[32 * p : 32 * p + 1, 5 * WIDTH :]

    @pl.when(own)
    def _():
        write(mine_ref)

    @pl.when(jnp.logical_not(own))
    def _():
        write(other_ref)


def weights_out(core, mine, other):
    half = MODEL // 2
    return pl.pallas_call(
        weights_kernel,
        out_shape=[
            jax.ShapeDtypeStruct((MODEL, 4, WIDTH), F32),
            jax.ShapeDtypeStruct((WIDTH, MODEL), F32),
            jax.ShapeDtypeStruct((1, 5 * WIDTH), F32),
        ],
        grid_spec=pltpu.PrefetchScalarGridSpec(
            num_scalar_prefetch=1,
            grid=(2,),
            in_specs=[
                pl.BlockSpec((half, COLUMNS), lambda i, c: (0, 0)),
                pl.BlockSpec((half, COLUMNS), lambda i, c: (0, 0)),
            ],
            out_specs=[
                pl.BlockSpec((half, 4, WIDTH), lambda i, c: (i, 0, 0)),
                pl.BlockSpec((WIDTH, half), lambda i, c: (0, i)),
                pl.BlockSpec((1, 5 * WIDTH), lambda i, c: (0, 0)),
            ],
        ),
        compiler_params=pltpu.CompilerParams(
            dimension_semantics=("arbitrary",), vmem_limit_bytes=40 * 1024 * 1024
        ),
        cost_estimate=pl.CostEstimate(flops=4000000, bytes_accessed=8500000, transcendentals=0),
        name="weights_out",
    )(core, mine, other)


def body(events, upstream, proj_weight, proj_bias, norm_gain, out_weight, lengths, owners):
    rows = events.shape[0]
    home_tiles = lengths.shape[1]
    my_index = lax.axis_index(DP)
    my_core = lax.axis_index("c").astype(jnp.int32).reshape(1)
    my_part = lax.axis_index("mp").astype(jnp.int32).reshape(1)
    weight_in = proj_weight.reshape(MODEL, 4 * WIDTH)
    bias_in = proj_bias.reshape(1, 4 * WIDTH)
    gain = norm_gain.reshape(1, WIDTH)
    mine = lengths[my_index]
    ends = jnp.cumsum(mine, dtype=jnp.int32)
    begins = ends - mine
    tile_ids = jnp.arange(home_tiles, dtype=jnp.int32)[:, None]
    inside = (tile_ids >= begins[None]) & (tile_ids < ends[None])
    first_tile = jnp.max(jnp.where(inside, begins[None], -1), axis=1).astype(jnp.int32)

    grads, sent, kept = layer(first_tile, my_core, events, upstream, weight_in, out_weight, bias_in, gain)

    swap = [(0, 1), (1, 0)]
    half = MODEL // 2
    kept = kept + lax.ppermute(sent, "c", swap).astype(F32)
    pieces = lax.all_to_all(kept.astype(BF16).reshape(16, half // 16, COLUMNS), ("z", "y"), 0, 0, tiled=True)
    piece = jnp.sum(pieces.astype(F32), axis=0).astype(BF16)
    pieces = lax.all_to_all(
        jnp.broadcast_to(piece[None], (16,) + piece.shape), ("z", "y"), 0, 0, tiled=True
    ).reshape(half, COLUMNS)
    other = lax.ppermute(pieces, "c", swap)
    proj_grad, out_grad, small = weights_out(my_core, pieces, other)

    event_grads = None
    count = rows // ROW_PARTS
    for n in range(ROW_PARTS):
        shares = partial_rows(grads, weight_in, n * count, count)
        got = lax.all_to_all(shares, "mp", 0, 0, tiled=True)
        event_grads = event_rows(first_tile, my_part, got, upstream, n * count, event_grads)
    return (
        event_grads,
        proj_grad,
        small[0, : 4 * WIDTH].reshape(4, WIDTH),
        small[0, 4 * WIDTH :],
        out_grad,
    )


def solution(mesh):
    grid = Mesh(mesh.devices.reshape(4, 4, 2, 4), ("z", "y", "c", "mp"))
    placed = (
        P(DP, None),
        P(DP, None),
        P(None, None, "mp"),
        P(None, "mp"),
        P("mp"),
        P("mp", None),
        P(),
        P(),
    )
    return jax.shard_map(
        body,
        mesh=grid,
        in_specs=placed,
        out_specs=(P(DP, "mp"), P(None, None, "mp"), P(None, "mp"), P("mp"), P("mp", None)),
        check_vma=False,
    )
```

profile of v0, /device:TPU:1, one launch (start us, length us, event | category | flops | bytes accessed | tf_op | source)
XLA Modules:
  0.0 215.2 jit_solution(1951175752724442166)
XLA Ops:
  0.7 1.3 copy.18
  1.9 0.7 fusion.3
  2.6 0.1 copy.16
  2.7 0.1 reduce-window.4
  2.8 0.1 reduce.1
  2.9 0.7 fusion.2
  3.6 0.6 select_reduce_fusion.first_ref
  4.2 0.1 mul.33
  4.4 0.7 copy.21
  5.0 3.4 %copy.17 = bf16[128,8,4,256]{3,1,2,0:T(8,128)(2,1)} copy(bf16[128,8,4,256]{3,2,1,0:T(4,128)(2,1)} %bitcast.31) | data formatting | bytes 4194304
  8.5 0.0 copy-start.5
  8.5 44.3 %layer.1 = (bf16[3072,1024]{1,0:T(8,128)(2,1)}, bf16[512,1408]{1,0:T(8,128)(2,1)}, f32[512,1408]{1,0:T(8,128)}) custom-call(s32[48]{0:T(128)} %select_reduce_fusion.first_ref, s32[1]{0:T(128)} %bitcast.3.core_ref, bf16[3072,1024]{1,0:T(8,128)(2,1)} %xp_ref.1, bf16[3072,1024]{1,0:T(8,128)(2,1)} %g_ref.7, bf16[3072,1024]{1,0:T(8,128)(2,1)} %xp_ref.1, ...), custom_call_target="tpu_custom_call" | custom-call | flops 18522046464 | bytes 24576000 | tf_op jit(solution)/shard_map/layer/pallas_call | solution.py:216
  52.7 1.4 collective-permute-start
  54.2 0.0 copy-done.5
  54.2 0.0 copy-start.2
  54.2 2.8 %copy-done.2 = bf16[3072,1024]{1,0:T(8,128)(2,1)S(1)} copy-done((bf16[3072,1024]{1,0:T(8,128)(2,1)S(1)}, bf16[3072,1024]{1,0:T(8,128)(2,1)}, u32[]{:S(2)}) %copy-start.2) | copy-done | bytes 6291480
  57.0 2.7 %partial_rows.5 = bf16[4,1024,256]{2,1,0:T(8,128)(2,1)S(1)} custom-call(bf16[3072,1024]{1,0:T(8,128)(2,1)S(1)} %copy-done.2, bf16[1024,1024]{1,0:T(8,128)(2,1)S(1)} %bitcast.25), custom_call_target="tpu_custom_call" | custom-call | flops 2147483648 | bytes 6291456 | tf_op jit(solution)/shard_map/partial_rows/pallas_call | solution.py:275
  59.7 0.0 copy-start.7
  59.7 1.4 copy-done.7
  61.0 4.5 %all-to-all-start.2 = ((bf16[4,1024,256]{2,1,0:T(8,128)(2,1)}), bf16[4,1024,256]{2,1,0:T(8,128)(2,1)}, u32[]{:S(2)}, u32[]{:S(2)}) async-start(bf16[4,1024,256]{2,1,0:T(8,128)(2,1)} %copy-done.7), calls=%async_computation.2 | async-start | bytes 4194304 | tf_op jit(solution)/shard_map/all_to_all | solution.py:423
  65.5 0.0 collective-permute-done
  65.5 3.2 %add_convert_fusion = bf16[512,1408]{1,0:T(8,128)(2,1)} fusion(f32[512,1408]{1,0:T(8,128)} %get-tuple-element.12, bf16[512,1408]{1,0:T(8,128)(2,1)S(1)} %collective-permute-done), kind=kLoop, calls=%fused_computation | loop fusion | flops 2162688 | bytes 5767168 | tf_op jit(solution)/shard_map/convert_element_type | solution.py:411
  68.7 23.4 %all-to-all-done.2.got_ref = bf16[4,1024,256]{2,1,0:T(8,128)(2,1)} async-done(((bf16[4,1024,256]{2,1,0:T(8,128)(2,1)}), bf16[4,1024,256]{2,1,0:T(8,128)(2,1)}, u32[]{:S(2)}, u32[]{:S(2)}) %all-to-all-start.2) | async-done | bytes 2097184 | tf_op jit(solution)/shard_map/all_to_all | solution.py:423
  92.0 7.9 %all-to-all-start.3 = ((bf16[16,32,1408]{2,1,0:T(8,128)(2,1)}), bf16[16,32,1408]{2,1,0:T(8,128)(2,1)S(1)}, u32[]{:S(2)}, u32[]{:S(2)}) async-start(bf16[16,32,1408]{2,1,0:T(8,128)(2,1)} %bitcast.30), calls=%async_computation.3 | async-start | bytes 2883584 | tf_op jit(solution)/shard_map/all_to_all | solution.py:411
  99.9 0.0 copy-start.3
  99.9 2.8 %copy-done.3 = bf16[3072,1024]{1,0:T(8,128)(2,1)S(1)} copy-done((bf16[3072,1024]{1,0:T(8,128)(2,1)S(1)}, bf16[3072,1024]{1,0:T(8,128)(2,1)}, u32[]{:S(2)}) %copy-start.3) | copy-done | bytes 6291480
  102.7 2.7 %partial_rows.4 = bf16[4,1024,256]{2,1,0:T(8,128)(2,1)S(1)} custom-call(bf16[3072,1024]{1,0:T(8,128)(2,1)S(1)} %copy-done.3, bf16[1024,1024]{1,0:T(8,128)(2,1)S(1)} %bitcast.26), custom_call_target="tpu_custom_call" | custom-call | flops 2147483648 | bytes 6291456 | tf_op jit(solution)/shard_map/partial_rows/pallas_call | solution.py:275
  105.4 0.0 copy-start.8
  105.4 1.3 copy-done.8
  106.7 13.4 %all-to-all-done.3 = bf16[16,32,1408]{2,1,0:T(8,128)(2,1)S(1)} async-done(((bf16[16,32,1408]{2,1,0:T(8,128)(2,1)}), bf16[16,32,1408]{2,1,0:T(8,128)(2,1)S(1)}, u32[]{:S(2)}, u32[]{:S(2)}) %all-to-all-start.3) | async-done | bytes 1441824 | tf_op jit(solution)/shard_map/all_to_all | solution.py:411
  120.1 4.5 %all-to-all-start.1 = ((bf16[4,1024,256]{2,1,0:T(8,128)(2,1)}), bf16[4,1024,256]{2,1,0:T(8,128)(2,1)}, u32[]{:S(2)}, u32[]{:S(2)}) async-start(bf16[4,1024,256]{2,1,0:T(8,128)(2,1)} %copy-done.8), calls=%async_computation.1 | async-start | bytes 4194304 | tf_op jit(solution)/shard_map/all_to_all | solution.py:423
  124.6 0.9 reduce_sum.12
  125.5 22.3 %all-to-all-done.1.got_ref = bf16[4,1024,256]{2,1,0:T(8,128)(2,1)} async-done(((bf16[4,1024,256]{2,1,0:T(8,128)(2,1)}), bf16[4,1024,256]{2,1,0:T(8,128)(2,1)}, u32[]{:S(2)}, u32[]{:S(2)}) %all-to-all-start.1) | async-done | bytes 2097184 | tf_op jit(solution)/shard_map/all_to_all | solution.py:423
  147.8 2.1 broadcast_in_dim.17
  149.9 8.5 %all-to-all-start.4 = ((bf16[16,32,1408]{2,1,0:T(8,128)(2,1)}), bf16[16,32,1408]{2,1,0:T(8,128)(2,1)S(1)}, u32[]{:S(2)}, u32[]{:S(2)}) async-start(bf16[16,32,1408]{2,1,0:T(8,128)(2,1)} %broadcast_in_dim.17), calls=%async_computation.4 | async-start | bytes 2883584 | tf_op jit(solution)/shard_map/all_to_all | solution.py:413
  158.4 0.0 copy-start.4
  158.4 2.8 %copy-done.4 = bf16[3072,1024]{1,0:T(8,128)(2,1)S(1)} copy-done((bf16[3072,1024]{1,0:T(8,128)(2,1)S(1)}, bf16[3072,1024]{1,0:T(8,128)(2,1)}, u32[]{:S(2)}) %copy-start.4) | copy-done | bytes 6291480
  161.2 2.7 %partial_rows.3 = bf16[4,1024,256]{2,1,0:T(8,128)(2,1)S(1)} custom-call(bf16[3072,1024]{1,0:T(8,128)(2,1)S(1)} %copy-done.4, bf16[1024,1024]{1,0:T(8,128)(2,1)S(1)} %bitcast.27), custom_call_target="tpu_custom_call" | custom-call | flops 2147483648 | bytes 6291456 | tf_op jit(solution)/shard_map/partial_rows/pallas_call | solution.py:275
  163.9 0.0 copy-start.6
  163.9 1.3 copy-done.6
  165.2 0.0 copy-start.9
  165.2 12.7 %all-to-all-done.4 = bf16[16,32,1408]{2,1,0:T(8,128)(2,1)S(1)} async-done(((bf16[16,32,1408]{2,1,0:T(8,128)(2,1)}), bf16[16,32,1408]{2,1,0:T(8,128)(2,1)S(1)}, u32[]{:S(2)}, u32[]{:S(2)}) %all-to-all-start.4) | async-done | bytes 1441824 | tf_op jit(solution)/shard_map/all_to_all | solution.py:413
  177.9 3.6 %all-to-all-start = ((bf16[4,1024,256]{2,1,0:T(8,128)(2,1)}), bf16[4,1024,256]{2,1,0:T(8,128)(2,1)S(1)}, u32[]{:S(2)}, u32[]{:S(2)}) async-start(bf16[4,1024,256]{2,1,0:T(8,128)(2,1)} %copy-done.6), calls=%async_computation | async-start | bytes 4194304 | tf_op jit(solution)/shard_map/all_to_all | solution.py:423
  181.5 3.7 %collective-permute-start.1 = (bf16[512,1408]{1,0:T(8,128)(2,1)S(1)}, bf16[512,1408]{1,0:T(8,128)(2,1)}, u32[]{:S(2)}, u32[]{:S(2)}) collective-permute-start(bf16[512,1408]{1,0:T(8,128)(2,1)S(1)} %bitcast.28), channel_id=1, source_target_pairs={{0,4},{4,0},{1,5},{5,1},{2,6},{6,2},{3,7},{7,3},{8,12},{12,8},{9,1... | collective-permute-start | bytes 4325384 | tf_op jit(solution)/shard_map/ppermute | solution.py:416
  185.2 0.0 copy-done.9
  185.2 0.0 copy-start
  185.2 2.8 %copy-done = bf16[3072,1024]{1,0:T(8,128)(2,1)S(1)} copy-done((bf16[3072,1024]{1,0:T(8,128)(2,1)S(1)}, bf16[3072,1024]{1,0:T(8,128)(2,1)}, u32[]{:S(2)}) %copy-start) | copy-done | bytes 6291480
  188.0 3.0 %event_rows.3.refs_0_ = bf16[3072,256]{1,0:T(8,128)(2,1)} custom-call(s32[48]{0:T(128)S(1)} %copy-done.9, s32[1]{0:T(128)} %bitcast.2.part_ref, bf16[4,1024,256]{2,1,0:T(8,128)(2,1)} %all-to-all-done.2.got_ref, bf16[3072,1024]{1,0:T(8,128)(2,1)S(1)} %copy-done), custom_call_target="tpu_custom_call" | custom-call | flops 2097152 | bytes 3145728 | tf_op jit(solution)/shard_map/event_rows/pallas_call | solution.py:317
  191.0 3.0 %event_rows.4.refs_0_ = bf16[3072,256]{1,0:T(8,128)(2,1)} custom-call(s32[48]{0:T(128)S(1)} %copy-done.9, s32[1]{0:T(128)} %bitcast.2.part_ref, bf16[4,1024,256]{2,1,0:T(8,128)(2,1)} %all-to-all-done.1.got_ref, bf16[3072,1024]{1,0:T(8,128)(2,1)S(1)} %copy-done, bf16[3072,256]{1,0:T(8,128)(2,1)} %event_rows.3.refs_0_), custom_call_target="tpu_custom_call", output_to_operand_aliasing={{}: (4, {})} | custom-call | flops 2097152 | bytes 3145728 | tf_op jit(solution)/shard_map/event_rows/pallas_call | solution.py:317
  194.0 10.3 %all-to-all-done.got_ref = bf16[4,1024,256]{2,1,0:T(8,128)(2,1)S(1)} async-done(((bf16[4,1024,256]{2,1,0:T(8,128)(2,1)}), bf16[4,1024,256]{2,1,0:T(8,128)(2,1)S(1)}, u32[]{:S(2)}, u32[]{:S(2)}) %all-to-all-start) | async-done | bytes 2097184 | tf_op jit(solution)/shard_map/all_to_all | solution.py:423
  204.3 0.0 copy-start.1
  204.3 2.8 %copy-done.1 = bf16[3072,1024]{1,0:T(8,128)(2,1)S(1)} copy-done((bf16[3072,1024]{1,0:T(8,128)(2,1)S(1)}, bf16[3072,1024]{1,0:T(8,128)(2,1)}, u32[]{:S(2)}) %copy-start.1) | copy-done | bytes 6291480
  207.1 1.9 event_rows.5
  208.9 0.0 collective-permute-done.1.other_ref
  208.9 5.1 %weights_out.1 = (f32[1024,4,256]{2,1,0:T(4,128)}, f32[256,1024]{1,0:T(8,128)}, f32[1,1280]{1,0:T(1,128)S(1)}) custom-call(s32[1]{0:T(128)} %bitcast.3.core_ref, bf16[512,1408]{1,0:T(8,128)(2,1)S(1)} %bitcast.29, bf16[512,1408]{1,0:T(8,128)(2,1)} %collective-permute-done.1.other_ref), custom_call_target="tpu_custom_call" | custom-call | flops 4000000 | bytes 8500000 | tf_op jit(solution)/shard_map/weights_out/pallas_call | solution.py:362
  214.1 0.6 slice.7
  214.6 0.6 reshape_squeeze.3
  (2 shorter events, 0.0 us)
Async XLA Ops:
  8.5 45.7 %copy-start.5 = (bf16[128,8,4,256]{3,1,2,0:T(8,128)(2,1)S(1)}, bf16[128,8,4,256]{3,1,2,0:T(8,128)(2,1)}, u32[]{:S(2)}) copy-start(bf16[128,8,4,256]{3,1,2,0:T(8,128)(2,1)} %copy.17) | copy-start | bytes 6291460
  52.7 12.8 %collective-permute-start = (bf16[512,1408]{1,0:T(8,128)(2,1)}, bf16[512,1408]{1,0:T(8,128)(2,1)S(1)}, u32[]{:S(2)}, u32[]{:S(2)}) collective-permute-start(bf16[512,1408]{1,0:T(8,128)(2,1)} %get-tuple-element.13), channel_id=1, source_target_pairs={{0,4},{4,0},{1,5},{5,1},{2,6},{6,2},{3,7},{7,3},{8,12},{12,8},{9,1... | collective-permute-start | bytes 4325384 | tf_op jit(solution)/shard_map/ppermute | solution.py:410
  54.2 2.8 %copy-start.2 = (bf16[3072,1024]{1,0:T(8,128)(2,1)S(1)}, bf16[3072,1024]{1,0:T(8,128)(2,1)}, u32[]{:S(2)}) copy-start(bf16[3072,1024]{1,0:T(8,128)(2,1)} %get-tuple-element.11.pg_ref) | copy-start | bytes 18874372
  59.7 1.4 copy-start.7
  61.0 31.0 %all-to-all-start.2 = ((bf16[4,1024,256]{2,1,0:T(8,128)(2,1)}), bf16[4,1024,256]{2,1,0:T(8,128)(2,1)}, u32[]{:S(2)}, u32[]{:S(2)}) async-start(bf16[4,1024,256]{2,1,0:T(8,128)(2,1)} %copy-done.7), calls=%async_computation.2 | async-start | bytes 4194304 | tf_op jit(solution)/shard_map/all_to_all | solution.py:423
  92.0 28.1 %all-to-all-start.3 = ((bf16[16,32,1408]{2,1,0:T(8,128)(2,1)}), bf16[16,32,1408]{2,1,0:T(8,128)(2,1)S(1)}, u32[]{:S(2)}, u32[]{:S(2)}) async-start(bf16[16,32,1408]{2,1,0:T(8,128)(2,1)} %bitcast.30), calls=%async_computation.3 | async-start | bytes 2883584 | tf_op jit(solution)/shard_map/all_to_all | solution.py:411
  99.9 2.8 %copy-start.3 = (bf16[3072,1024]{1,0:T(8,128)(2,1)S(1)}, bf16[3072,1024]{1,0:T(8,128)(2,1)}, u32[]{:S(2)}) copy-start(bf16[3072,1024]{1,0:T(8,128)(2,1)} %get-tuple-element.11.pg_ref) | copy-start | bytes 18874372
  105.4 1.3 copy-start.8
  120.1 27.7 %all-to-all-start.1 = ((bf16[4,1024,256]{2,1,0:T(8,128)(2,1)}), bf16[4,1024,256]{2,1,0:T(8,128)(2,1)}, u32[]{:S(2)}, u32[]{:S(2)}) async-start(bf16[4,1024,256]{2,1,0:T(8,128)(2,1)} %copy-done.8), calls=%async_computation.1 | async-start | bytes 4194304 | tf_op jit(solution)/shard_map/all_to_all | solution.py:423
  149.9 28.0 %all-to-all-start.4 = ((bf16[16,32,1408]{2,1,0:T(8,128)(2,1)}), bf16[16,32,1408]{2,1,0:T(8,128)(2,1)S(1)}, u32[]{:S(2)}, u32[]{:S(2)}) async-start(bf16[16,32,1408]{2,1,0:T(8,128)(2,1)} %broadcast_in_dim.17), calls=%async_computation.4 | async-start | bytes 2883584 | tf_op jit(solution)/shard_map/all_to_all | solution.py:413
  158.4 2.8 %copy-start.4 = (bf16[3072,1024]{1,0:T(8,128)(2,1)S(1)}, bf16[3072,1024]{1,0:T(8,128)(2,1)}, u32[]{:S(2)}) copy-start(bf16[3072,1024]{1,0:T(8,128)(2,1)} %get-tuple-element.11.pg_ref) | copy-start | bytes 18874372
  163.9 1.3 copy-start.6
  165.2 20.0 %copy-start.9 = (s32[48]{0:T(128)S(1)}, s32[48]{0:T(128)}, u32[]{:S(2)}) copy-start(s32[48]{0:T(128)} %select_reduce_fusion.first_ref) | copy-start | bytes 580
  177.9 26.3 %all-to-all-start = ((bf16[4,1024,256]{2,1,0:T(8,128)(2,1)}), bf16[4,1024,256]{2,1,0:T(8,128)(2,1)S(1)}, u32[]{:S(2)}, u32[]{:S(2)}) async-start(bf16[4,1024,256]{2,1,0:T(8,128)(2,1)} %copy-done.6), calls=%async_computation | async-start | bytes 4194304 | tf_op jit(solution)/shard_map/all_to_all | solution.py:423
  181.5 27.4 %collective-permute-start.1 = (bf16[512,1408]{1,0:T(8,128)(2,1)S(1)}, bf16[512,1408]{1,0:T(8,128)(2,1)}, u32[]{:S(2)}, u32[]{:S(2)}) collective-permute-start(bf16[512,1408]{1,0:T(8,128)(2,1)S(1)} %bitcast.28), channel_id=1, source_target_pairs={{0,4},{4,0},{1,5},{5,1},{2,6},{6,2},{3,7},{7,3},{8,12},{12,8},{9,1... | collective-permute-start | bytes 4325384 | tf_op jit(solution)/shard_map/ppermute | solution.py:416
  185.2 2.8 %copy-start = (bf16[3072,1024]{1,0:T(8,128)(2,1)S(1)}, bf16[3072,1024]{1,0:T(8,128)(2,1)}, u32[]{:S(2)}) copy-start(bf16[3072,1024]{1,0:T(8,128)(2,1)} %g_ref.7) | copy-start | bytes 18874372
  204.3 2.8 %copy-start.1 = (bf16[3072,1024]{1,0:T(8,128)(2,1)S(1)}, bf16[3072,1024]{1,0:T(8,128)(2,1)}, u32[]{:S(2)}) copy-start(bf16[3072,1024]{1,0:T(8,128)(2,1)} %g_ref.7) | copy-start | bytes 18874372
where the time goes:
time: 219 us; the launch traced here: 215 us
  waiting for transfers between devices  82.1 us (37%)
  Pallas kernels  65.3 us (30%)
  starting transfers between devices  34 us (16%)
  local copies, waits for them, and re-layouts  27.5 us (13%)
  other arithmetic  5.51 us (3%)
    all_to_all x3, waiting for transfers between devices, body(): got = lax.all_to_all(shares, 'mp', 0, 0, tiled=True)  56 us
    pallas_call x1, Pallas kernels, layer(): pl.pallas_call(functools.partial(layer_kernel, steps), out_shape=[jax.Sha...  44.3 us
    unnamed x23, local copies, waits for them, and re-layouts  23.3 us
    all_to_all x1, waiting for transfers between devices, body(): lax.all_to_all(kept.astype(BF16).reshape(16, half // 16, COLUMNS), ('z',...  13.4 us
    all_to_all x1, waiting for transfers between devices, body(): lax.all_to_all(jnp.broadcast_to(piece[None], (16,) + piece.shape), ('z',...  12.7 us
    all_to_all x3, starting transfers between devices, body(): got = lax.all_to_all(shares, 'mp', 0, 0, tiled=True)  12.6 us
    all_to_all x1, starting transfers between devices, body(): lax.all_to_all(jnp.broadcast_to(piece[None], (16,) + piece.shape), ('z',...  8.49 us
    pallas_call x3, Pallas kernels, partial_rows(): pl.pallas_call(partial_kernel, out_shape=jax.ShapeDtypeStruct((4, count,...  8.07 us
  transfers between devices with their start and end apart: 7, of which 5 were waited for; matrix products, arithmetic and copies ran while one was open for 2% of the time, Pallas kernels for 7%

commit v1 on v0

--- a/solution.py
+++ b/solution.py
@@ -18,7 +18,8 @@
 MODEL = 1024
 COLUMNS = 5 * WIDTH + 128
 PIECES = 8
-ROW_PARTS = 3
+ROW_PARTS = 2
+HISTORY = 3
 F32 = jnp.float32
 BF16 = jnp.bfloat16
 NT = (((1,), (1,)), ((), ()))
@@ -43,9 +44,9 @@
 
 
 def layer_kernel(
-    steps, first_ref, core_ref, x_ref, g_ref, xp_ref, w_ref, wo_ref, b_ref, gain_ref, ones_ref,
-    pg_out, sent_out, mine_out,
-    kv, dkv, sl, pgq, gq, slgq, hg, hid, pgs, acc, sums, attn_s, dsl_s, mix_s, dm_s,
+    steps, lengths_ref, place_ref, x_ref, g_ref, xp_ref, wp_ref, wo_ref, b_ref, gain_ref,
+    pg_out, sent_out, mine_out, w_ref,
+    first_ref, ones_ref, kv, dkv, sl, pgq, gq, slgq, hg, hid, pgs, acc, sums, attn_s, dsl_s, mix_s, dm_s,
 ):
     j = pl.program_id(0)
     cur = pl.ds(STEP, STEP)
@@ -62,6 +63,29 @@
         pgs[...] = jnp.zeros(pgs.shape, BF16)
         acc[...] = jnp.zeros(acc.shape, F32)
         sums[...] = jnp.zeros(sums.shape, F32)
+        for p in range(4):
+            w_ref[:, p * WIDTH : (p + 1) * WIDTH] = wp_ref[:, p, :]
+        head_row = lax.broadcasted_iota(jnp.int32, (WIDTH, WIDTH), 0) >= HEAD
+        head_col = lax.broadcasted_iota(jnp.int32, (WIDTH, WIDTH), 1) >= HEAD
+        ones_ref[...] = jnp.where(head_row == head_col, 1.0 / HEAD, 0.0).astype(BF16)
+        home = place_ref[0]
+        tiles = steps * (STEP // TILE)
+
+        @pl.loop(0, tiles)
+        def _(t):
+            first_ref[t] = -1
+
+        def place(u, begin):
+            count = lengths_ref[home, u]
+            for t in range(HISTORY):
+
+                @pl.when(t < count)
+                def _():
+                    first_ref[begin + t] = begin
+
+            return begin + count
+
+        lax.fori_loop(0, lengths_ref.shape[1], place, jnp.int32(0))
 
     def in_grad_piece(n):
         depth = MODEL // PIECES
@@ -100,7 +124,7 @@
         hg[...] = dot(g, wo_ref[...], NT)
         for part in range(4):
             cols = slice(part * WIDTH, (part + 1) * WIDTH)
-            pre = dot(x, w_ref[:, cols]) + b_ref[:, cols]
+            pre = dot(x, w_ref[:, cols]) + b_ref[part : part + 1, :]
             sig = sigmoid(pre)
             act = pre * sig
             slope = sig + act * (1.0 - sig)
@@ -188,17 +212,16 @@
         total = jnp.sum(sums[...], axis=0, keepdims=True)
         for p in range(5 * WIDTH // 128):
             acc[pl.ds(32 * p, 8), 5 * WIDTH :] = jnp.broadcast_to(total[:, p * 128 : (p + 1) * 128], (8, 128))
-        core = core_ref[0]
+        core = place_ref[1]
         half = MODEL // 2
         mine_out[...] = acc[pl.ds(pl.multiple_of(core * half, half), half), :]
         sent_out[...] = acc[pl.ds(pl.multiple_of((1 - core) * half, half), half), :].astype(BF16)
 
 
-def layer(first_tile, core, x, g, w, wo, bias, gain):
+def layer(lengths, place, x, g, w, wo, bias, gain):
     rows = x.shape[0]
     steps = rows // STEP
     half = MODEL // 2
-    ones = jnp.kron(jnp.eye(2, dtype=F32), jnp.full((HEAD, HEAD), 1.0 / HEAD, F32)).astype(BF16)
 
     def in_block(j, *_):
         return (jnp.minimum(j, steps - 1), 0)
@@ -219,6 +242,7 @@
             jax.ShapeDtypeStruct((rows, MODEL), BF16),
             jax.ShapeDtypeStruct((half, COLUMNS), BF16),
             jax.ShapeDtypeStruct((half, COLUMNS), F32),
+            jax.ShapeDtypeStruct((MODEL, 4 * WIDTH), BF16),
         ],
         grid_spec=pltpu.PrefetchScalarGridSpec(
             num_scalar_prefetch=2,
@@ -227,18 +251,20 @@
                 pl.BlockSpec((STEP, MODEL), in_block),
                 pl.BlockSpec((STEP, MODEL), in_block),
                 pl.BlockSpec((STEP, MODEL), late_block),
-                pl.BlockSpec(w.shape, whole),
+                pl.BlockSpec(w.shape, lambda j, *_: (0, 0, 0)),
                 pl.BlockSpec(wo.shape, whole),
                 pl.BlockSpec(bias.shape, whole),
                 pl.BlockSpec(gain.shape, whole),
-                pl.BlockSpec(ones.shape, whole),
             ],
             out_specs=[
                 pl.BlockSpec((STEP, MODEL), out_block),
                 pl.BlockSpec((half, COLUMNS), whole),
                 pl.BlockSpec((half, COLUMNS), whole),
+                pl.BlockSpec((MODEL, 4 * WIDTH), whole),
             ],
             scratch_shapes=[
+                pltpu.SMEM((steps * (STEP // TILE),), jnp.int32),
+                pltpu.VMEM((WIDTH, WIDTH), BF16),
                 pltpu.VMEM((2 * STEP, SPAN), BF16),
                 pltpu.VMEM((2 * STEP, SPAN), F32),
                 pltpu.VMEM((2 * STEP, SPAN), F32),
@@ -261,59 +287,69 @@
         ),
         cost_estimate=pl.CostEstimate(flops=2 * macs, bytes_accessed=rows * 8000, transcendentals=rows * 2048),
         name="layer",
-    )(first_tile, core, x, g, x, w, wo, bias, gain, ones)
-
-
-def partial_kernel(pg_ref, w_ref, out_ref):
+    )(lengths, place, x, g, x, w, wo, bias, gain)
+
+
+def partial_kernel(place_ref, pg_ref, w_ref, own_out, ahead_out, across_out, behind_out):
     grads = pg_ref[...]
-    for d in range(4):
-        out_ref[d] = dot(grads, w_ref[d * WIDTH : (d + 1) * WIDTH, :], NT).astype(BF16)
-
-
-def partial_rows(grads, w, begin, count):
+    me = place_ref[2]
+
+    def chunk(shift):
+        start = pl.multiple_of(lax.rem(me + shift, 4) * WIDTH, WIDTH)
+        return dot(grads, w_ref[pl.ds(start, WIDTH), :], NT)
+
+    ahead_out[...] = chunk(1).astype(BF16)
+    across_out[...] = chunk(2).astype(BF16)
+    behind_out[...] = chunk(3).astype(BF16)
+    own_out[...] = chunk(0)
+
+
+def partial_rows(place, grads, w, begin, count):
     block = 512
+    here = pl.BlockSpec((block, WIDTH), lambda i, p: (i, 0))
     return pl.pallas_call(
         partial_kernel,
-        out_shape=jax.ShapeDtypeStruct((4, count, WIDTH), BF16),
-        grid=(count // block,),
-        in_specs=[
-            pl.BlockSpec((block, MODEL), lambda i: (begin // block + i, 0)),
-            pl.BlockSpec(w.shape, lambda i: (0, 0)),
-        ],
-        out_specs=pl.BlockSpec((4, block, WIDTH), lambda i: (0, i, 0)),
+        out_shape=[jax.ShapeDtypeStruct((count, WIDTH), F32)] + [jax.ShapeDtypeStruct((count, WIDTH), BF16)] * 3,
+        grid_spec=pltpu.PrefetchScalarGridSpec(
+            num_scalar_prefetch=1,
+            grid=(count // block,),
+            in_specs=[
+                pl.BlockSpec((block, MODEL), lambda i, p: (begin // block + i, 0)),
+                pl.BlockSpec(w.shape, lambda i, p: (0, 0)),
+            ],
+            out_specs=[here, here, here, here],
+        ),
         compiler_params=pltpu.CompilerParams(
-            dimension_semantics=("arbitrary",), vmem_limit_bytes=32 * 1024 * 1024
+            dimension_semantics=("arbitrary",), vmem_limit_bytes=56 * 1024 * 1024
         ),
         cost_estimate=pl.CostEstimate(
             flops=2 * count * MODEL * MODEL, bytes_accessed=count * 4096 + w.size * 2, transcendentals=0
         ),
         name="partial_rows",
-    )(grads, w)
-
-
-def event_kernel(begin, block, first_ref, part_ref, got_ref, g_ref, *refs):
+    )(place, grads, w)
+
+
+def event_kernel(begin, block, lengths_ref, place_ref, own_ref, a_ref, b_ref, c_ref, g_ref, *refs):
     out_ref = refs[-1]
-    t0 = (begin + pl.program_id(0) * block) // TILE
-    firsts = [first_ref[t0 + i] for i in range(block // TILE)]
-    used = tile_column(firsts, block) >= 0
-    g = jnp.where(used, g_ref[...], jnp.zeros((), BF16)).astype(F32)
-    total = (got_ref[0].astype(F32) + got_ref[1].astype(F32)) + (got_ref[2].astype(F32) + got_ref[3].astype(F32))
-    out_ref[...] = (total + g).astype(BF16)
-
-
-def event_rows(first_tile, part, got, g, begin, out):
+    home = place_ref[0]
+    tiles = lax.fori_loop(0, lengths_ref.shape[1], lambda u, t: t + lengths_ref[home, u], jnp.int32(0))
+    row = lax.broadcasted_iota(jnp.int32, (block, WIDTH), 0) + begin + pl.program_id(0) * block
+    g = jnp.where(row < tiles * TILE, g_ref[...].astype(F32), 0.0)
+    got = a_ref[...].astype(F32) + b_ref[...].astype(F32) + c_ref[...].astype(F32)
+    out_ref[...] = (own_ref[...] + got + g).astype(BF16)
+
+
+def event_rows(lengths, place, shares, g, begin, out):
     block = 512
-    count = got.shape[1]
-    in_specs = [
-        pl.BlockSpec((4, block, WIDTH), lambda i, f, p: (0, i, 0)),
-        pl.BlockSpec((block, WIDTH), lambda i, f, p: (begin // block + i, p[0])),
-    ]
-    operands = [got, g]
+    count = shares[0].shape[0]
+    here = pl.BlockSpec((block, WIDTH), lambda i, f, p: (i, 0))
+    in_specs = [here] * 4 + [pl.BlockSpec((block, WIDTH), lambda i, f, p: (begin // block + i, p[2]))]
+    operands = list(shares) + [g]
     aliases = {}
     if out is not None:
         in_specs.append(pl.BlockSpec(memory_space=pl.ANY))
         operands.append(out)
-        aliases = {4: 0}
+        aliases = {7: 0}
     return pl.pallas_call(
         functools.partial(event_kernel, begin, block),
         out_shape=jax.ShapeDtypeStruct((g.shape[0], WIDTH), BF16),
@@ -325,28 +361,48 @@
         ),
         input_output_aliases=aliases,
         compiler_params=pltpu.CompilerParams(
-            dimension_semantics=("arbitrary",), vmem_limit_bytes=16 * 1024 * 1024
+            dimension_semantics=("arbitrary",), vmem_limit_bytes=56 * 1024 * 1024
         ),
         cost_estimate=pl.CostEstimate(flops=count * 2048, bytes_accessed=count * 3072, transcendentals=0),
         name="event_rows",
-    )(first_tile, part, *operands)
-
-
-def weights_kernel(core_ref, mine_ref, other_ref, pw_out, ow_out, small_out):
-    i = pl.program_id(0)
-    half = MODEL // 2
-    own = core_ref[0] == i
+    )(lengths, place, *operands)
+
+
+def spread_kernel(got_ref, out_ref):
+    total = jnp.sum(got_ref[...].astype(F32), axis=0).astype(BF16)
+    out_ref[...] = jnp.broadcast_to(total[None], out_ref.shape)
+
+
+def spread(pieces):
+    return pl.pallas_call(
+        spread_kernel,
+        out_shape=jax.ShapeDtypeStruct(pieces.shape, BF16),
+        compiler_params=pltpu.CompilerParams(vmem_limit_bytes=32 * 1024 * 1024),
+        cost_estimate=pl.CostEstimate(flops=pieces.size, bytes_accessed=pieces.size * 4, transcendentals=0),
+        name="spread",
+    )(pieces)
+
+
+def weights_kernel(place_ref, mine_ref, other_ref, pw_out, ow_out, bias_out, gain_out):
+    i, k = pl.program_id(0), pl.program_id(1)
+    own = place_ref[1] == i
 
     def write(ref):
         values = ref[...].astype(F32) * (1.0 / 32.0)
         for p in range(4):
             pw_out[:, p, :] = values[:, p * WIDTH : (p + 1) * WIDTH]
         ow_out[...] = values[:, 4 * WIDTH : 5 * WIDTH].T
-
-        @pl.when(i == 0)
-        def _():
-            for p in range(5 * WIDTH // 128):
-                small_out[:, p * 128 : (p + 1) * 128] = values[32 * p : 32 * p + 1, 5 * WIDTH :]
+        for p in range(5 * WIDTH // 128):
+            block, at = divmod(32 * p, values.shape[0])
+
+            @pl.when((i == 0) & (k == block))
+            def _():
+                lanes = slice(p % 2 * 128, p % 2 * 128 + 128)
+                small = values[at : at + 1, 5 * WIDTH :]
+                if p < 8:
+                    bias_out[p // 2 : p // 2 + 1, lanes] = small
+                else:
+                    gain_out[:, lanes] = small
 
     @pl.when(own)
     def _():
@@ -357,78 +413,70 @@
         write(other_ref)
 
 
-def weights_out(core, mine, other):
+def weights_out(place, mine, other):
     half = MODEL // 2
+    block = 128
+    per = half // block
     return pl.pallas_call(
         weights_kernel,
         out_shape=[
             jax.ShapeDtypeStruct((MODEL, 4, WIDTH), F32),
             jax.ShapeDtypeStruct((WIDTH, MODEL), F32),
-            jax.ShapeDtypeStruct((1, 5 * WIDTH), F32),
+            jax.ShapeDtypeStruct((4, WIDTH), F32),
+            jax.ShapeDtypeStruct((1, WIDTH), F32),
         ],
         grid_spec=pltpu.PrefetchScalarGridSpec(
             num_scalar_prefetch=1,
-            grid=(2,),
+            grid=(2, per),
             in_specs=[
-                pl.BlockSpec((half, COLUMNS), lambda i, c: (0, 0)),
-                pl.BlockSpec((half, COLUMNS), lambda i, c: (0, 0)),
+                pl.BlockSpec((block, COLUMNS), lambda i, k, c: (k, 0)),
+                pl.BlockSpec((block, COLUMNS), lambda i, k, c: (k, 0)),
             ],
             out_specs=[
-                pl.BlockSpec((half, 4, WIDTH), lambda i, c: (i, 0, 0)),
-                pl.BlockSpec((WIDTH, half), lambda i, c: (0, i)),
-                pl.BlockSpec((1, 5 * WIDTH), lambda i, c: (0, 0)),
+                pl.BlockSpec((block, 4, WIDTH), lambda i, k, c: (i * per + k, 0, 0)),
+                pl.BlockSpec((WIDTH, block), lambda i, k, c: (0, i * per + k)),
+                pl.BlockSpec((4, WIDTH), lambda i, k, c: (0, 0)),
+                pl.BlockSpec((1, WIDTH), lambda i, k, c: (0, 0)),
             ],
         ),
         compiler_params=pltpu.CompilerParams(
-            dimension_semantics=("arbitrary",), vmem_limit_bytes=40 * 1024 * 1024
+            dimension_semantics=("arbitrary", "arbitrary"), vmem_limit_bytes=40 * 1024 * 1024
         ),
         cost_estimate=pl.CostEstimate(flops=4000000, bytes_accessed=8500000, transcendentals=0),
         name="weights_out",
-    )(core, mine, other)
+    )(place, mine, other)
+
+
+def ring(step):
+    return [(i, (i + step) % 4) for i in range(4)]
 
 
 def body(events, upstream, proj_weight, proj_bias, norm_gain, out_weight, lengths, owners):
     rows = events.shape[0]
-    home_tiles = lengths.shape[1]
-    my_index = lax.axis_index(DP)
-    my_core = lax.axis_index("c").astype(jnp.int32).reshape(1)
-    my_part = lax.axis_index("mp").astype(jnp.int32).reshape(1)
-    weight_in = proj_weight.reshape(MODEL, 4 * WIDTH)
-    bias_in = proj_bias.reshape(1, 4 * WIDTH)
+    place = jnp.stack([lax.axis_index(DP), lax.axis_index("c"), lax.axis_index("mp")]).astype(jnp.int32)
     gain = norm_gain.reshape(1, WIDTH)
-    mine = lengths[my_index]
-    ends = jnp.cumsum(mine, dtype=jnp.int32)
-    begins = ends - mine
-    tile_ids = jnp.arange(home_tiles, dtype=jnp.int32)[:, None]
-    inside = (tile_ids >= begins[None]) & (tile_ids < ends[None])
-    first_tile = jnp.max(jnp.where(inside, begins[None], -1), axis=1).astype(jnp.int32)
-
-    grads, sent, kept = layer(first_tile, my_core, events, upstream, weight_in, out_weight, bias_in, gain)
+    grads, sent, kept, weight_in = layer(lengths, place, events, upstream, proj_weight, out_weight, proj_bias, gain)
 
     swap = [(0, 1), (1, 0)]
     half = MODEL // 2
     kept = kept + lax.ppermute(sent, "c", swap).astype(F32)
     pieces = lax.all_to_all(kept.astype(BF16).reshape(16, half // 16, COLUMNS), ("z", "y"), 0, 0, tiled=True)
-    piece = jnp.sum(pieces.astype(F32), axis=0).astype(BF16)
-    pieces = lax.all_to_all(
-        jnp.broadcast_to(piece[None], (16,) + piece.shape), ("z", "y"), 0, 0, tiled=True
-    ).reshape(half, COLUMNS)
+    pieces = lax.all_to_all(spread(pieces), ("z", "y"), 0, 0, tiled=True).reshape(half, COLUMNS)
     other = lax.ppermute(pieces, "c", swap)
-    proj_grad, out_grad, small = weights_out(my_core, pieces, other)
+    proj_grad, out_grad, bias_grad, gain_grad = weights_out(place, pieces, other)
 
     event_grads = None
     count = rows // ROW_PARTS
     for n in range(ROW_PARTS):
-        shares = partial_rows(grads, weight_in, n * count, count)
-        got = lax.all_to_all(shares, "mp", 0, 0, tiled=True)
-        event_grads = event_rows(first_tile, my_part, got, upstream, n * count, event_grads)
-    return (
-        event_grads,
-        proj_grad,
-        small[0, : 4 * WIDTH].reshape(4, WIDTH),
-        small[0, 4 * WIDTH :],
-        out_grad,
-    )
+        own, ahead, across, behind = partial_rows(place, grads, weight_in, n * count, count)
+        shares = (
+            own,
+            lax.ppermute(ahead, "mp", ring(1)),
+            lax.ppermute(across, "mp", ring(2)),
+            lax.ppermute(behind, "mp", ring(3)),
+        )
+        event_grads = event_rows(lengths, place, shares, upstream, n * count, event_grads)
+    return event_grads, proj_grad, bias_grad, gain_grad.reshape(WIDTH), out_grad
 
 
 def solution(mesh):

time: 219 us -> 182 us (0.83)
  waiting for transfers between devices: 82.1 us -> 49.5 us
  blocking collectives: 0 us -> 28.4 us
  local copies, waits for them, and re-layouts: 27.5 us -> 1.8 us
  starting transfers between devices: 34 us -> 16.5 us
  Pallas kernels: 65.3 us -> 80.5 us
  other arithmetic: 5.51 us -> 2.76 us
    all_to_all x5 -> x1, waiting for transfers between devices: 82.1 us -> 8.29 us  [body(): lax.all_to_all(spread(pieces), ('z', 'y'), 0, 0, tiled=True)]
    ppermute x0 -> x6, waiting for transfers between devices: none -> 38.1 us  [the longest x2 22.4 us: body(): lax.ppermute(across, 'mp', ring(2))]
    all_to_all x0 -> x1, blocking collectives: none -> 28.4 us  [body(): lax.all_to_all(kept.astype(BF16).reshape(16, half // 16, COLUMNS), ('z',...]
    all_to_all x5 -> x1, starting transfers between devices: 28.9 us -> 3.71 us  [body(): lax.all_to_all(spread(pieces), ('z', 'y'), 0, 0, tiled=True)]
    unnamed x23 -> x14, local copies, waits for them, and re-layouts: 23.3 us -> 1.8 us
    pallas_call x3, Pallas kernels: 8.07 us -> 16.5 us  [the longest x2 15.2 us: partial_rows(): pl.pallas_call(partial_kernel, out_shape=[jax.ShapeDtypeStruct((count, WI...]
    ppermute x0 -> x6, starting transfers between devices: none -> 7.86 us  [the longest x2 4.16 us: body(): lax.ppermute(across, 'mp', ring(2))]
    pallas_call x1, Pallas kernels: 44.3 us -> 48.9 us  [layer(): pl.pallas_call(functools.partial(layer_kernel, steps), out_shape=[jax.Sha...]
  transfers between devices with their start and end apart: 7 -> 9, of which waited for: 5 -> 7; matrix products, arithmetic and copies ran while one was open for 2% -> 0% of each run, Pallas kernels for 7% -> 14%
where the time goes in v1:
time: 182 us; the launch traced here: 180 us
  Pallas kernels  80.5 us (44%)
  waiting for transfers between devices  49.5 us (27%)
  blocking collectives  28.4 us (16%)
  starting transfers between devices  16.5 us (9%)
  other arithmetic  2.76 us (2%)
    pallas_call x1, Pallas kernels, layer(): pl.pallas_call(functools.partial(layer_kernel, steps), out_shape=[jax.Sha...  48.9 us
    all_to_all x1, blocking collectives, body(): lax.all_to_all(kept.astype(BF16).reshape(16, half // 16, COLUMNS), ('z',...  28.4 us
    ppermute x2, waiting for transfers between devices, body(): lax.ppermute(across, 'mp', ring(2))  22.4 us
    pallas_call x2, Pallas kernels, partial_rows(): pl.pallas_call(partial_kernel, out_shape=[jax.ShapeDtypeStruct((count, WI...  15.2 us
    ppermute x2, waiting for transfers between devices, body(): lax.ppermute(ahead, 'mp', ring(1))  12.4 us
    pallas_call x2, Pallas kernels, event_rows(): pl.pallas_call(functools.partial(event_kernel, begin, block), out_shape=j...  9.98 us
    all_to_all x1, waiting for transfers between devices, body(): lax.all_to_all(spread(pieces), ('z', 'y'), 0, 0, tiled=True)  8.29 us
    pallas_call x1, Pallas kernels, weights_out(): pl.pallas_call(weights_kernel, out_shape=[jax.ShapeDtypeStruct((MODEL, 4,...  5.17 us
  transfers between devices with their start and end apart: 9, of which 7 were waited for; matrix products, arithmetic and copies ran while one was open for 0% of the time, Pallas kernels for 14%

profile of v1, /device:TPU:1, one launch (start us, length us, event | category | flops | bytes accessed | tf_op | source)
XLA Modules:
  0.0 180.2 jit_solution(8721279973568002856)
XLA Ops:
  0.6 0.6 pad_add_fusion.place_ref
  1.2 48.9 %layer.1 = (bf16[3072,1024]{1,0:T(8,128)(2,1)}, bf16[512,1408]{1,0:T(8,128)(2,1)}, f32[512,1408]{1,0:T(8,128)}, bf16[1024,1024]{1,0:T(8,128)(2,1)}) custom-call(s32[32,48]{1,0:T(8,128)} %lengths_ref.5, s32[3]{0:T(128)} %pad_add_fusion.place_ref, bf16[3072,1024]{1,0:T(8,128)(2,1)} %xp_ref.1, bf16[3072,1024]{1,0:T(8,128)(2,1)} %g_ref.5, ...), custom_call_target="tpu_custom_call" | custom-call | flops 18522046464 | bytes 24576000 | tf_op jit(solution)/shard_map/layer/pallas_call | solution.py:239
  50.1 1.4 collective-permute-start.6
  51.5 3.1 %collective-permute-done.6 = bf16[512,1408]{1,0:T(8,128)(2,1)S(1)} collective-permute-done((bf16[512,1408]{1,0:T(8,128)(2,1)}, bf16[512,1408]{1,0:T(8,128)(2,1)S(1)}, u32[]{:S(2)}, u32[]{:S(2)}) %collective-permute-start.6) | collective-permute-done | bytes 1441824 | tf_op jit(solution)/shard_map/ppermute | solution.py:462
  54.6 2.2 %add_convert_fusion = bf16[512,1408]{1,0:T(8,128)(2,1)S(1)} fusion(f32[512,1408]{1,0:T(8,128)} %get-tuple-element.31, bf16[512,1408]{1,0:T(8,128)(2,1)S(1)} %collective-permute-done.6), kind=kLoop, calls=%fused_computation | loop fusion | flops 2162688 | bytes 5767168 | tf_op jit(solution)/shard_map/convert_element_type | solution.py:463
  56.7 28.4 %all_to_all.10.got_ref = bf16[16,32,1408]{2,1,0:T(8,128)(2,1)S(1)} all-to-all(bf16[16,32,1408]{2,1,0:T(8,128)(2,1)S(1)} %bitcast.9), channel_id=1, replica_groups=mesh['z'=4,'y'=4,'c'=2,'mp'=4] {'z','y'}, dimensions={0} | all-to-all | bytes 2883584 | tf_op jit(solution)/shard_map/all_to_all | solution.py:463
  85.2 1.3 spread.1
  86.5 3.7 %all-to-all-start.1 = ((bf16[16,32,1408]{2,1,0:T(8,128)(2,1)}), bf16[16,32,1408]{2,1,0:T(8,128)(2,1)S(1)}, u32[]{:S(2)}, u32[]{:S(2)}) async-start(bf16[16,32,1408]{2,1,0:T(8,128)(2,1)} %spread.1), calls=%async_computation.1 | async-start | bytes 2883584 | tf_op jit(solution)/shard_map/all_to_all | solution.py:464
  90.2 7.6 %partial_rows.3 = (f32[1536,256]{1,0:T(8,128)}, bf16[1536,256]{1,0:T(8,128)(2,1)}, bf16[1536,256]{1,0:T(8,128)(2,1)}, bf16[1536,256]{1,0:T(8,128)(2,1)}) custom-call(s32[3]{0:T(128)} %pad_add_fusion.place_ref, bf16[3072,1024]{1,0:T(8,128)(2,1)} %get-tuple-element.21.pg_ref, bf16[1024,1024]{1,0:T(8,128)(2,1)} %get-tuple-element.22.w_ref), custom_call_target="tpu_custom_call" | custom-call | flops 3221225472 | bytes 8388608 | tf_op jit(solution)/shard_map/partial_rows/pallas_call | solution.py:310
  97.8 1.2 collective-permute-start.3
  99.0 2.4 %collective-permute-start.4 = (bf16[1536,256]{1,0:T(8,128)(2,1)}, bf16[1536,256]{1,0:T(8,128)(2,1)S(1)}, u32[]{:S(2)}, u32[]{:S(2)}) collective-permute-start(bf16[1536,256]{1,0:T(8,128)(2,1)} %get-tuple-element.29), channel_id=1, source_target_pairs={{0,2},{1,3},{2,0},{3,1},{4,6},{5,7},{6,4},{7,5},{8,10},{9,11},{10,... | collective-permute-start | bytes 2359304 | tf_op jit(solution)/shard_map/ppermute | solution.py:475
  101.5 8.3 %all-to-all-done.1 = bf16[16,32,1408]{2,1,0:T(8,128)(2,1)S(1)} async-done(((bf16[16,32,1408]{2,1,0:T(8,128)(2,1)}), bf16[16,32,1408]{2,1,0:T(8,128)(2,1)S(1)}, u32[]{:S(2)}, u32[]{:S(2)}) %all-to-all-start.1) | async-done | bytes 1441824 | tf_op jit(solution)/shard_map/all_to_all | solution.py:464
  109.8 3.6 %collective-permute-start.7 = (bf16[512,1408]{1,0:T(8,128)(2,1)S(1)}, bf16[512,1408]{1,0:T(8,128)(2,1)S(1)}, u32[]{:S(2)}, u32[]{:S(2)}) collective-permute-start(bf16[512,1408]{1,0:T(8,128)(2,1)S(1)} %bitcast.7), channel_id=1, source_target_pairs={{0,4},{4,0},{1,5},{5,1},{2,6},{6,2},{3,7},{7,3},{8,12},{12,8},{9,1... | collective-permute-start | bytes 4325384 | tf_op jit(solution)/shard_map/ppermute | solution.py:465
  113.3 2.5 %collective-permute-start.5 = (bf16[1536,256]{1,0:T(8,128)(2,1)}, bf16[1536,256]{1,0:T(8,128)(2,1)S(1)}, u32[]{:S(2)}, u32[]{:S(2)}) collective-permute-start(bf16[1536,256]{1,0:T(8,128)(2,1)} %get-tuple-element.30), channel_id=1, source_target_pairs={{0,3},{1,0},{2,1},{3,2},{4,7},{5,4},{6,5},{7,6},{8,11},{9,8},{10,9... | collective-permute-start | bytes 2359304 | tf_op jit(solution)/shard_map/ppermute | solution.py:476
  115.8 7.6 %partial_rows.2 = (f32[1536,256]{1,0:T(8,128)}, bf16[1536,256]{1,0:T(8,128)(2,1)}, bf16[1536,256]{1,0:T(8,128)(2,1)}, bf16[1536,256]{1,0:T(8,128)(2,1)}) custom-call(s32[3]{0:T(128)} %pad_add_fusion.place_ref, bf16[3072,1024]{1,0:T(8,128)(2,1)} %get-tuple-element.21.pg_ref, bf16[1024,1024]{1,0:T(8,128)(2,1)} %get-tuple-element.22.w_ref), custom_call_target="tpu_custom_call" | custom-call | flops 3221225472 | bytes 8388608 | tf_op jit(solution)/shard_map/partial_rows/pallas_call | solution.py:310
  123.4 0.0 collective-permute-start
  123.4 0.0 collective-permute-done.3.a_ref
  123.4 0.0 copy-start.1
  123.4 1.7 collective-permute-start.1
  125.2 9.5 %collective-permute-done.4.b_ref = bf16[1536,256]{1,0:T(8,128)(2,1)S(1)} collective-permute-done((bf16[1536,256]{1,0:T(8,128)(2,1)}, bf16[1536,256]{1,0:T(8,128)(2,1)S(1)}, u32[]{:S(2)}, u32[]{:S(2)}) %collective-permute-start.4) | collective-permute-done | bytes 786464 | tf_op jit(solution)/shard_map/ppermute | solution.py:475
  134.6 0.0 copy-start.2
  134.6 0.0 collective-permute-start.2
  134.6 2.6 %collective-permute-done.5.c_ref = bf16[1536,256]{1,0:T(8,128)(2,1)S(1)} collective-permute-done((bf16[1536,256]{1,0:T(8,128)(2,1)}, bf16[1536,256]{1,0:T(8,128)(2,1)S(1)}, u32[]{:S(2)}, u32[]{:S(2)}) %collective-permute-start.5) | collective-permute-done | bytes 786464 | tf_op jit(solution)/shard_map/ppermute | solution.py:476
  137.2 0.0 copy-start.3
  137.2 0.0 copy-done.1
  137.2 0.0 copy-done.2
  137.2 0.9 copy-done.3
  138.1 4.9 %event_rows.2.refs_0_ = bf16[3072,256]{1,0:T(8,128)(2,1)} custom-call(s32[32,48]{1,0:T(8,128)} %lengths_ref.5, s32[3]{0:T(128)} %pad_add_fusion.place_ref, f32[1536,256]{1,0:T(8,128)} %get-tuple-element.27.own_ref, bf16[1536,256]{1,0:T(8,128)(2,1)} %copy-done.1, bf16[1536,256]{1,0:T(8,128)(2,1)} %copy-done.2, bf16[1536,256]{1,0:T(8,128)(2,1)} %copy-done.3, ...), custom_call_target="tpu_custom_call" | custom-call | flops 3145728 | bytes 4718592 | tf_op jit(solution)/shard_map/event_rows/pallas_call | solution.py:353
  143.0 12.4 %collective-permute-done.a_ref = bf16[1536,256]{1,0:T(8,128)(2,1)S(1)} collective-permute-done((bf16[1536,256]{1,0:T(8,128)(2,1)}, bf16[1536,256]{1,0:T(8,128)(2,1)S(1)}, u32[]{:S(2)}, u32[]{:S(2)}) %collective-permute-start) | collective-permute-done | bytes 786464 | tf_op jit(solution)/shard_map/ppermute | solution.py:474
  155.4 0.0 copy-start.4
  155.4 13.0 %collective-permute-done.1.b_ref = bf16[1536,256]{1,0:T(8,128)(2,1)S(1)} collective-permute-done((bf16[1536,256]{1,0:T(8,128)(2,1)}, bf16[1536,256]{1,0:T(8,128)(2,1)S(1)}, u32[]{:S(2)}, u32[]{:S(2)}) %collective-permute-start.1) | collective-permute-done | bytes 786464 | tf_op jit(solution)/shard_map/ppermute | solution.py:475
  168.3 0.0 copy-start.5
  168.3 0.7 collective-permute-done.2.c_ref
  169.1 0.0 copy-start.6
  169.1 0.0 copy-done.4
  169.1 0.2 copy-done.5
  169.2 0.8 copy-done.6
  170.0 0.0 copy-start
  170.0 5.1 %event_rows.3 = bf16[3072,256]{1,0:T(8,128)(2,1)} custom-call(s32[32,48]{1,0:T(8,128)} %lengths_ref.5, s32[3]{0:T(128)} %pad_add_fusion.place_ref, f32[1536,256]{1,0:T(8,128)} %get-tuple-element.23.own_ref, bf16[1536,256]{1,0:T(8,128)(2,1)} %copy-done.4, bf16[1536,256]{1,0:T(8,128)(2,1)} %copy-done.5, ...), custom_call_target="tpu_custom_call", output_to_operand_aliasing={{}: (7, {})} | custom-call | flops 3145728 | bytes 4718592 | tf_op jit(solution)/shard_map/event_rows/pallas_call | solution.py:353
  175.0 0.0 collective-permute-done.7.other_ref
  175.1 0.0 copy-done
  175.1 5.2 %weights_out.1 = (f32[1024,4,256]{2,1,0:T(4,128)}, f32[256,1024]{1,0:T(8,128)}, f32[4,256]{1,0:T(4,128)}, f32[1,256]{1,0:T(1,128)}) custom-call(s32[3]{0:T(128)S(1)} %copy-done, bf16[512,1408]{1,0:T(8,128)(2,1)S(1)} %bitcast.8, bf16[512,1408]{1,0:T(8,128)(2,1)S(1)} %collective-permute-done.7.other_ref), custom_call_target="tpu_custom_call" | custom-call | flops 4000000 | bytes 8500000 | tf_op jit(solution)/shard_map/weights_out/pallas_call | solution.py:420
Async XLA Ops:
  50.1 4.5 %collective-permute-start.6 = (bf16[512,1408]{1,0:T(8,128)(2,1)}, bf16[512,1408]{1,0:T(8,128)(2,1)S(1)}, u32[]{:S(2)}, u32[]{:S(2)}) collective-permute-start(bf16[512,1408]{1,0:T(8,128)(2,1)} %get-tuple-element.32), channel_id=1, source_target_pairs={{0,4},{4,0},{1,5},{5,1},{2,6},{6,2},{3,7},{7,3},{8,12},{12,8},{9,1... | collective-permute-start | bytes 4325384 | tf_op jit(solution)/shard_map/ppermute | solution.py:462
  86.5 23.3 %all-to-all-start.1 = ((bf16[16,32,1408]{2,1,0:T(8,128)(2,1)}), bf16[16,32,1408]{2,1,0:T(8,128)(2,1)S(1)}, u32[]{:S(2)}, u32[]{:S(2)}) async-start(bf16[16,32,1408]{2,1,0:T(8,128)(2,1)} %spread.1), calls=%async_computation.1 | async-start | bytes 2883584 | tf_op jit(solution)/shard_map/all_to_all | solution.py:464
  97.8 25.6 %collective-permute-start.3 = (bf16[1536,256]{1,0:T(8,128)(2,1)}, bf16[1536,256]{1,0:T(8,128)(2,1)S(1)}, u32[]{:S(2)}, u32[]{:S(2)}) collective-permute-start(bf16[1536,256]{1,0:T(8,128)(2,1)} %get-tuple-element.28), channel_id=1, source_target_pairs={{0,1},{1,2},{2,3},{3,0},{4,5},{5,6},{6,7},{7,4},{8,9},{9,10},{10,1... | collective-permute-start | bytes 2359304 | tf_op jit(solution)/shard_map/ppermute | solution.py:474
  99.0 35.6 %collective-permute-start.4 = (bf16[1536,256]{1,0:T(8,128)(2,1)}, bf16[1536,256]{1,0:T(8,128)(2,1)S(1)}, u32[]{:S(2)}, u32[]{:S(2)}) collective-permute-start(bf16[1536,256]{1,0:T(8,128)(2,1)} %get-tuple-element.29), channel_id=1, source_target_pairs={{0,2},{1,3},{2,0},{3,1},{4,6},{5,7},{6,4},{7,5},{8,10},{9,11},{10,... | collective-permute-start | bytes 2359304 | tf_op jit(solution)/shard_map/ppermute | solution.py:475
  109.8 65.3 %collective-permute-start.7 = (bf16[512,1408]{1,0:T(8,128)(2,1)S(1)}, bf16[512,1408]{1,0:T(8,128)(2,1)S(1)}, u32[]{:S(2)}, u32[]{:S(2)}) collective-permute-start(bf16[512,1408]{1,0:T(8,128)(2,1)S(1)} %bitcast.7), channel_id=1, source_target_pairs={{0,4},{4,0},{1,5},{5,1},{2,6},{6,2},{3,7},{7,3},{8,12},{12,8},{9,1... | collective-permute-start | bytes 4325384 | tf_op jit(solution)/shard_map/ppermute | solution.py:465
  113.3 23.9 %collective-permute-start.5 = (bf16[1536,256]{1,0:T(8,128)(2,1)}, bf16[1536,256]{1,0:T(8,128)(2,1)S(1)}, u32[]{:S(2)}, u32[]{:S(2)}) collective-permute-start(bf16[1536,256]{1,0:T(8,128)(2,1)} %get-tuple-element.30), channel_id=1, source_target_pairs={{0,3},{1,0},{2,1},{3,2},{4,7},{5,4},{6,5},{7,6},{8,11},{9,8},{10,9... | collective-permute-start | bytes 2359304 | tf_op jit(solution)/shard_map/ppermute | solution.py:476
  123.4 32.0 %collective-permute-start = (bf16[1536,256]{1,0:T(8,128)(2,1)}, bf16[1536,256]{1,0:T(8,128)(2,1)S(1)}, u32[]{:S(2)}, u32[]{:S(2)}) collective-permute-start(bf16[1536,256]{1,0:T(8,128)(2,1)} %get-tuple-element.24), channel_id=1, source_target_pairs={{0,1},{1,2},{2,3},{3,0},{4,5},{5,6},{6,7},{7,4},{8,9},{9,10},{10,1... | collective-permute-start | bytes 2359304 | tf_op jit(solution)/shard_map/ppermute | solution.py:474
  123.4 13.8 %copy-start.1 = (bf16[1536,256]{1,0:T(8,128)(2,1)}, bf16[1536,256]{1,0:T(8,128)(2,1)S(1)}, u32[]{:S(2)}) copy-start(bf16[1536,256]{1,0:T(8,128)(2,1)S(1)} %collective-permute-done.3.a_ref) | copy-start | bytes 2359300
  123.4 44.9 %collective-permute-start.1 = (bf16[1536,256]{1,0:T(8,128)(2,1)}, bf16[1536,256]{1,0:T(8,128)(2,1)S(1)}, u32[]{:S(2)}, u32[]{:S(2)}) collective-permute-start(bf16[1536,256]{1,0:T(8,128)(2,1)} %get-tuple-element.25), channel_id=1, source_target_pairs={{0,2},{1,3},{2,0},{3,1},{4,6},{5,7},{6,4},{7,5},{8,10},{9,11},{10,... | collective-permute-start | bytes 2359304 | tf_op jit(solution)/shard_map/ppermute | solution.py:475
  134.6 2.6 %copy-start.2 = (bf16[1536,256]{1,0:T(8,128)(2,1)}, bf16[1536,256]{1,0:T(8,128)(2,1)S(1)}, u32[]{:S(2)}) copy-start(bf16[1536,256]{1,0:T(8,128)(2,1)S(1)} %collective-permute-done.4.b_ref) | copy-start | bytes 2359300
  134.6 34.4 %collective-permute-start.2 = (bf16[1536,256]{1,0:T(8,128)(2,1)}, bf16[1536,256]{1,0:T(8,128)(2,1)S(1)}, u32[]{:S(2)}, u32[]{:S(2)}) collective-permute-start(bf16[1536,256]{1,0:T(8,128)(2,1)} %get-tuple-element.26), channel_id=1, source_target_pairs={{0,3},{1,0},{2,1},{3,2},{4,7},{5,4},{6,5},{7,6},{8,11},{9,8},{10,9... | collective-permute-start | bytes 2359304 | tf_op jit(solution)/shard_map/ppermute | solution.py:476
  137.2 0.9 copy-start.3
  155.4 13.7 %copy-start.4 = (bf16[1536,256]{1,0:T(8,128)(2,1)}, bf16[1536,256]{1,0:T(8,128)(2,1)S(1)}, u32[]{:S(2)}) copy-start(bf16[1536,256]{1,0:T(8,128)(2,1)S(1)} %collective-permute-done.a_ref) | copy-start | bytes 2359300
  168.3 0.9 copy-start.5
  169.1 0.9 copy-start.6
  170.0 5.1 %copy-start = (s32[3]{0:T(128)S(1)}, s32[3]{0:T(128)}, u32[]{:S(2)}) copy-start(s32[3]{0:T(128)} %pad_add_fusion.place_ref) | copy-start | bytes 40

commit v2 on v1

--- a/solution.py
+++ b/solution.py
@@ -290,26 +290,35 @@
     )(lengths, place, x, g, x, w, wo, bias, gain)
 
 
-def partial_kernel(place_ref, pg_ref, w_ref, own_out, ahead_out, across_out, behind_out):
+def partial_kernel(place_ref, pg_ref, w_ref, own_out, s1f_out, s1b_out, r2f_out, r2b_out):
     grads = pg_ref[...]
     me = place_ref[2]
 
-    def chunk(shift):
+    def share(shift):
         start = pl.multiple_of(lax.rem(me + shift, 4) * WIDTH, WIDTH)
         return dot(grads, w_ref[pl.ds(start, WIDTH), :], NT)
 
-    ahead_out[...] = chunk(1).astype(BF16)
-    across_out[...] = chunk(2).astype(BF16)
-    behind_out[...] = chunk(3).astype(BF16)
-    own_out[...] = chunk(0)
+    across = share(2).astype(BF16)
+    s1f_out[:, :HEAD] = across[:, :HEAD]
+    s1b_out[:, HEAD:] = across[:, HEAD:]
+    ahead = share(1).astype(BF16)
+    r2f_out[...] = ahead[:, :HEAD]
+    s1f_out[:, HEAD:] = ahead[:, HEAD:]
+    behind = share(3).astype(BF16)
+    s1b_out[:, :HEAD] = behind[:, :HEAD]
+    r2b_out[...] = behind[:, HEAD:]
+    own_out[...] = share(0)
 
 
 def partial_rows(place, grads, w, begin, count):
     block = 512
-    here = pl.BlockSpec((block, WIDTH), lambda i, p: (i, 0))
+    wide = pl.BlockSpec((block, WIDTH), lambda i, p: (i, 0))
+    slim = pl.BlockSpec((block, HEAD), lambda i, p: (i, 0))
     return pl.pallas_call(
         partial_kernel,
-        out_shape=[jax.ShapeDtypeStruct((count, WIDTH), F32)] + [jax.ShapeDtypeStruct((count, WIDTH), BF16)] * 3,
+        out_shape=[jax.ShapeDtypeStruct((count, WIDTH), F32)]
+        + [jax.ShapeDtypeStruct((count, WIDTH), BF16)] * 2
+        + [jax.ShapeDtypeStruct((count, HEAD), BF16)] * 2,
         grid_spec=pltpu.PrefetchScalarGridSpec(
             num_scalar_prefetch=1,
             grid=(count // block,),
@@ -317,7 +326,7 @@
                 pl.BlockSpec((block, MODEL), lambda i, p: (begin // block + i, 0)),
                 pl.BlockSpec(w.shape, lambda i, p: (0, 0)),
             ],
-            out_specs=[here, here, here, here],
+            out_specs=[wide, wide, wide, slim, slim],
         ),
         compiler_params=pltpu.CompilerParams(
             dimension_semantics=("arbitrary",), vmem_limit_bytes=56 * 1024 * 1024
@@ -329,27 +338,31 @@
     )(place, grads, w)
 
 
-def event_kernel(begin, block, lengths_ref, place_ref, own_ref, a_ref, b_ref, c_ref, g_ref, *refs):
+def event_kernel(begin, block, lengths_ref, place_ref, own_ref, t1f_ref, t1b_ref, t2f_ref, t2b_ref, g_ref, *refs):
     out_ref = refs[-1]
     home = place_ref[0]
     tiles = lax.fori_loop(0, lengths_ref.shape[1], lambda u, t: t + lengths_ref[home, u], jnp.int32(0))
     row = lax.broadcasted_iota(jnp.int32, (block, WIDTH), 0) + begin + pl.program_id(0) * block
-    g = jnp.where(row < tiles * TILE, g_ref[...].astype(F32), 0.0)
-    got = a_ref[...].astype(F32) + b_ref[...].astype(F32) + c_ref[...].astype(F32)
-    out_ref[...] = (own_ref[...] + got + g).astype(BF16)
+    base = own_ref[...] + jnp.where(row < tiles * TILE, g_ref[...].astype(F32), 0.0)
+    left = t1b_ref[:, :HEAD].astype(F32) + t2f_ref[...].astype(F32)
+    right = t1f_ref[:, HEAD:].astype(F32) + t2b_ref[...].astype(F32)
+    out_ref[:, :HEAD] = (base[:, :HEAD] + left).astype(BF16)
+    out_ref[:, HEAD:] = (base[:, HEAD:] + right).astype(BF16)
 
 
 def event_rows(lengths, place, shares, g, begin, out):
     block = 512
     count = shares[0].shape[0]
-    here = pl.BlockSpec((block, WIDTH), lambda i, f, p: (i, 0))
-    in_specs = [here] * 4 + [pl.BlockSpec((block, WIDTH), lambda i, f, p: (begin // block + i, p[2]))]
+    wide = pl.BlockSpec((block, WIDTH), lambda i, f, p: (i, 0))
+    slim = pl.BlockSpec((block, HEAD), lambda i, f, p: (i, 0))
+    in_specs = [wide, wide, wide, slim, slim]
+    in_specs.append(pl.BlockSpec((block, WIDTH), lambda i, f, p: (begin // block + i, p[2])))
     operands = list(shares) + [g]
     aliases = {}
     if out is not None:
         in_specs.append(pl.BlockSpec(memory_space=pl.ANY))
         operands.append(out)
-        aliases = {7: 0}
+        aliases = {8: 0}
     return pl.pallas_call(
         functools.partial(event_kernel, begin, block),
         out_shape=jax.ShapeDtypeStruct((g.shape[0], WIDTH), BF16),
@@ -366,6 +379,29 @@
         cost_estimate=pl.CostEstimate(flops=count * 2048, bytes_accessed=count * 3072, transcendentals=0),
         name="event_rows",
     )(lengths, place, *operands)
+
+
+def relay_kernel(r2f_ref, r2b_ref, t1f_ref, t1b_ref, f_out, b_out):
+    f_out[...] = (r2f_ref[...].astype(F32) + t1f_ref[...].astype(F32)).astype(BF16)
+    b_out[...] = (r2b_ref[...].astype(F32) + t1b_ref[...].astype(F32)).astype(BF16)
+
+
+def relay(r2f, r2b, t1f, t1b):
+    block = 512
+    rows = r2f.shape[0]
+    slim = pl.BlockSpec((block, HEAD), lambda i: (i, 0))
+    return pl.pallas_call(
+        relay_kernel,
+        out_shape=[jax.ShapeDtypeStruct((rows, HEAD), BF16)] * 2,
+        grid=(rows // block,),
+        in_specs=[slim, slim, slim, pl.BlockSpec((block, HEAD), lambda i: (i, 1))],
+        out_specs=[slim, slim],
+        compiler_params=pltpu.CompilerParams(
+            dimension_semantics=("arbitrary",), vmem_limit_bytes=56 * 1024 * 1024
+        ),
+        cost_estimate=pl.CostEstimate(flops=rows * 512, bytes_accessed=rows * 1536, transcendentals=0),
+        name="relay",
+    )(r2f, r2b, t1f, t1b)
 
 
 def spread_kernel(got_ref, out_ref):
@@ -459,23 +495,28 @@
 
     swap = [(0, 1), (1, 0)]
     half = MODEL // 2
-    kept = kept + lax.ppermute(sent, "c", swap).astype(F32)
-    pieces = lax.all_to_all(kept.astype(BF16).reshape(16, half // 16, COLUMNS), ("z", "y"), 0, 0, tiled=True)
-    pieces = lax.all_to_all(spread(pieces), ("z", "y"), 0, 0, tiled=True).reshape(half, COLUMNS)
+    other = lax.ppermute(sent, "c", swap)
+    parts = []
+    count = rows // ROW_PARTS
+    own, s1f, s1b, r2f, r2b = partial_rows(place, grads, weight_in, 0, count)
+    parts.append([own, r2f, r2b, lax.ppermute(s1f, "mp", ring(1)), lax.ppermute(s1b, "mp", ring(3))])
+    kept = (kept + other.astype(F32)).astype(BF16)
+    grads, weight_in, kept = lax.optimization_barrier((grads, weight_in, kept))
+    pieces = lax.all_to_all(kept.reshape(16, half // 16, COLUMNS), ("z", "y"), 0, 0, tiled=True)
+    own, s1f, s1b, r2f, r2b = partial_rows(place, grads, weight_in, count, count)
+    parts.append([own, r2f, r2b, lax.ppermute(s1f, "mp", ring(1)), lax.ppermute(s1b, "mp", ring(3))])
+    pieces = spread(pieces)
+    second_step = [relay(*p[1:]) for p in parts]
+    second_step, pieces = lax.optimization_barrier((second_step, pieces))
+    shares = []
+    for (own, _, _, t1f, t1b), (r2f, r2b) in zip(parts, second_step):
+        shares.append((own, t1f, t1b, lax.ppermute(r2f, "mp", ring(1)), lax.ppermute(r2b, "mp", ring(3))))
+    pieces = lax.all_to_all(pieces, ("z", "y"), 0, 0, tiled=True).reshape(half, COLUMNS)
     other = lax.ppermute(pieces, "c", swap)
     proj_grad, out_grad, bias_grad, gain_grad = weights_out(place, pieces, other)
-
     event_grads = None
-    count = rows // ROW_PARTS
     for n in range(ROW_PARTS):
-        own, ahead, across, behind = partial_rows(place, grads, weight_in, n * count, count)
-        shares = (
-            own,
-            lax.ppermute(ahead, "mp", ring(1)),
-            lax.ppermute(across, "mp", ring(2)),
-            lax.ppermute(behind, "mp", ring(3)),
-        )
-        event_grads = event_rows(lengths, place, shares, upstream, n * count, event_grads)
+        event_grads = event_rows(lengths, place, shares[n], upstream, n * count, event_grads)
     return event_grads, proj_grad, bias_grad, gain_grad.reshape(WIDTH), out_grad
 
 

time: 182 us -> 176 us (0.967)
  waiting for transfers between devices: 49.5 us -> 31.6 us
  starting transfers between devices: 16.5 us -> 23.3 us
  Pallas kernels: 80.5 us -> 85.9 us
  blocking collectives: 28.4 us -> 25.7 us
  local copies, waits for them, and re-layouts: 1.8 us -> 4.14 us
    ppermute x7 -> x9, waiting for transfers between devices: 41.2 us -> 31.6 us  [the longest x2 19.2 us: body(): lax.ppermute(s1f, 'mp', ring(1))]
    all_to_all x1, waiting for transfers between devices: 8.29 us -> 0.01 us  [body(): lax.all_to_all(kept.reshape(16, half // 16, COLUMNS), ('z', 'y'), 0, 0, t...]
    pallas_call x0 -> x2, Pallas kernels: none -> 6.31 us  [relay(): pl.pallas_call(relay_kernel, out_shape=[jax.ShapeDtypeStruct((rows, HEAD)...]
    all_to_all x1, starting transfers between devices: 3.71 us -> 7.85 us  [body(): lax.all_to_all(kept.reshape(16, half // 16, COLUMNS), ('z', 'y'), 0, 0, t...]
    ppermute x7 -> x9, starting transfers between devices: 9.27 us -> 12.3 us  [the longest x2 4.67 us: body(): lax.ppermute(r2b, 'mp', ring(3))]
    all_to_all x1, blocking collectives: 28.4 us -> 25.7 us  [body(): lax.all_to_all(pieces, ('z', 'y'), 0, 0, tiled=True).reshape(half, COLUMNS)]
    unnamed x14 -> x26, local copies, waits for them, and re-layouts: 1.8 us -> 4.14 us
  transfers between devices with their start and end apart: 9 -> 11, of which waited for: 7 -> 5; matrix products, arithmetic and copies ran while one was open for 0% -> 0% of each run, Pallas kernels for 14% -> 18%
where the time goes in v2:
time: 176 us; the launch traced here: 175 us
  Pallas kernels  85.9 us (49%)
  waiting for transfers between devices  31.6 us (18%)
  blocking collectives  25.7 us (15%)
  starting transfers between devices  23.3 us (13%)
  local copies, waits for them, and re-layouts  4.14 us (2%)
  other arithmetic  3.86 us (2%)
    pallas_call x1, Pallas kernels, layer(): pl.pallas_call(functools.partial(layer_kernel, steps), out_shape=[jax.Sha...  48.9 us
    all_to_all x1, blocking collectives, body(): lax.all_to_all(pieces, ('z', 'y'), 0, 0, tiled=True).reshape(half, COLUMNS)  25.7 us
    ppermute x2, waiting for transfers between devices, body(): lax.ppermute(s1f, 'mp', ring(1))  19.2 us
    pallas_call x2, Pallas kernels, partial_rows(): pl.pallas_call(partial_kernel, out_shape=[jax.ShapeDtypeStruct((count, WI...  15.4 us
    pallas_call x2, Pallas kernels, event_rows(): pl.pallas_call(functools.partial(event_kernel, begin, block), out_shape=j...  9.97 us
    ppermute x2, waiting for transfers between devices, body(): lax.ppermute(r2f, 'mp', ring(1))  9.25 us
    all_to_all x1, starting transfers between devices, body(): lax.all_to_all(kept.reshape(16, half // 16, COLUMNS), ('z', 'y'), 0, 0, t...  7.85 us
    pallas_call x2, Pallas kernels, relay(): pl.pallas_call(relay_kernel, out_shape=[jax.ShapeDtypeStruct((rows, HEAD)...  6.31 us
  transfers between devices with their start and end apart: 11, of which 5 were waited for; matrix products, arithmetic and copies ran while one was open for 0% of the time, Pallas kernels for 18%

profile of v2, /device:TPU:1, one launch (start us, length us, event | category | flops | bytes accessed | tf_op | source)
XLA Modules:
  0.0 175.2 jit_solution(13416144662762920683)
XLA Ops:
  0.6 0.6 pad_add_fusion.place_ref
  1.2 48.9 %layer.1 = (bf16[3072,1024]{1,0:T(8,128)(2,1)}, bf16[512,1408]{1,0:T(8,128)(2,1)}, f32[512,1408]{1,0:T(8,128)}, bf16[1024,1024]{1,0:T(8,128)(2,1)}) custom-call(s32[32,48]{1,0:T(8,128)} %lengths_ref.5, s32[3]{0:T(128)} %pad_add_fusion.place_ref, bf16[3072,1024]{1,0:T(8,128)(2,1)} %xp_ref.1, bf16[3072,1024]{1,0:T(8,128)(2,1)} %g_ref.5, ...), custom_call_target="tpu_custom_call" | custom-call | flops 18522046464 | bytes 24576000 | tf_op jit(solution)/shard_map/layer/pallas_call | solution.py:239
  50.1 1.4 collective-permute-start
  51.6 3.1 %collective-permute-done = bf16[512,1408]{1,0:T(8,128)(2,1)S(1)} collective-permute-done((bf16[512,1408]{1,0:T(8,128)(2,1)}, bf16[512,1408]{1,0:T(8,128)(2,1)S(1)}, u32[]{:S(2)}, u32[]{:S(2)}) %collective-permute-start) | collective-permute-done | bytes 1441824 | tf_op jit(solution)/shard_map/ppermute | solution.py:498
  54.6 3.3 %add_convert_fusion = bf16[512,1408]{1,0:T(8,128)(2,1)} fusion(f32[512,1408]{1,0:T(8,128)} %get-tuple-element.37, bf16[512,1408]{1,0:T(8,128)(2,1)S(1)} %collective-permute-done), kind=kLoop, calls=%fused_computation | loop fusion | flops 2162688 | bytes 5767168 | tf_op jit(solution)/shard_map/convert_element_type | solution.py:503
  57.9 7.9 %all-to-all-start = ((bf16[16,32,1408]{2,1,0:T(8,128)(2,1)}), bf16[16,32,1408]{2,1,0:T(8,128)(2,1)S(1)}, u32[]{:S(2)}, u32[]{:S(2)}) async-start(bf16[16,32,1408]{2,1,0:T(8,128)(2,1)} %bitcast.4), calls=%async_computation | async-start | bytes 2883584 | tf_op jit(solution)/shard_map/all_to_all | solution.py:505
  65.8 7.7 %partial_rows.3 = (f32[1536,256]{1,0:T(8,128)}, bf16[1536,256]{1,0:T(8,128)(2,1)}, bf16[1536,256]{1,0:T(8,128)(2,1)}, bf16[1536,128]{1,0:T(8,128)(2,1)}, bf16[1536,128]{1,0:T(8,128)(2,1)}) custom-call(s32[3]{0:T(128)} %pad_add_fusion.place_ref, bf16[3072,1024]{1,0:T(8,128)(2,1)} %get-tuple-element.39.pg_ref, bf16[1024,1024]{1,0:T(8,128)(2,1)} %get-tuple-element.40.w_ref), custom_call_target="tpu_custom_call" | custom-call | flops 3221225472 | bytes 8388608 | tf_op jit(solution)/shard_map/partial_rows/pallas_call | solution.py:317
  73.4 1.3 collective-permute-start.3
  74.7 1.5 collective-permute-start.4
  76.2 7.7 %partial_rows.2 = (f32[1536,256]{1,0:T(8,128)}, bf16[1536,256]{1,0:T(8,128)(2,1)}, bf16[1536,256]{1,0:T(8,128)(2,1)}, bf16[1536,128]{1,0:T(8,128)(2,1)}, bf16[1536,128]{1,0:T(8,128)(2,1)}) custom-call(s32[3]{0:T(128)} %pad_add_fusion.place_ref, bf16[3072,1024]{1,0:T(8,128)(2,1)} %get-tuple-element.39.pg_ref, bf16[1024,1024]{1,0:T(8,128)(2,1)} %get-tuple-element.40.w_ref), custom_call_target="tpu_custom_call" | custom-call | flops 3221225472 | bytes 8388608 | tf_op jit(solution)/shard_map/partial_rows/pallas_call | solution.py:317
  83.9 0.1 collective-permute-start.1
  84.0 2.7 %collective-permute-start.2 = (bf16[1536,256]{1,0:T(8,128)(2,1)}, bf16[1536,256]{1,0:T(8,128)(2,1)S(1)}, u32[]{:S(2)}, u32[]{:S(2)}) collective-permute-start(bf16[1536,256]{1,0:T(8,128)(2,1)} %get-tuple-element.43), channel_id=1, source_target_pairs={{0,3},{1,0},{2,1},{3,2},{4,7},{5,4},{6,5},{7,6},{8,11},{9,8},{10,9... | collective-permute-start | bytes 2359304 | tf_op jit(solution)/shard_map/ppermute | solution.py:507
  86.6 6.7 %collective-permute-done.3.t1f_ref = bf16[1536,256]{1,0:T(8,128)(2,1)S(1)} collective-permute-done((bf16[1536,256]{1,0:T(8,128)(2,1)}, bf16[1536,256]{1,0:T(8,128)(2,1)S(1)}, u32[]{:S(2)}, u32[]{:S(2)}) %collective-permute-start.3) | collective-permute-done | bytes 786464 | tf_op jit(solution)/shard_map/ppermute | solution.py:502
  93.4 0.0 copy-start.1
  93.4 0.0 collective-permute-done.4.t1b_ref
  93.4 0.0 copy-start.2
  93.4 0.9 copy-done.1
  94.3 0.3 copy-done.2
  94.6 3.1 %relay.2 = (bf16[1536,128]{1,0:T(8,128)(2,1)}, bf16[1536,128]{1,0:T(8,128)(2,1)}) custom-call(bf16[1536,128]{1,0:T(8,128)(2,1)} %get-tuple-element.44.r2f_ref, bf16[1536,128]{1,0:T(8,128)(2,1)} %get-tuple-element.45.r2b_ref, bf16[1536,256]{1,0:T(8,128)(2,1)} %copy-done.1, bf16[1536,256]{1,0:T(8,128)(2,1)} %copy-done.2), custom_call_target="tpu_custom_call" | custom-call | flops 786432 | bytes 2359296 | tf_op jit(solution)/shard_map/relay/pallas_call | solution.py:393
  97.7 12.5 %collective-permute-done.1.t1f_ref = bf16[1536,256]{1,0:T(8,128)(2,1)S(1)} collective-permute-done((bf16[1536,256]{1,0:T(8,128)(2,1)}, bf16[1536,256]{1,0:T(8,128)(2,1)S(1)}, u32[]{:S(2)}, u32[]{:S(2)}) %collective-permute-start.1) | collective-permute-done | bytes 786464 | tf_op jit(solution)/shard_map/ppermute | solution.py:507
  110.2 0.0 copy-start.3
  110.2 0.0 collective-permute-done.2.t1b_ref
  110.2 0.0 copy-start.4
  110.2 0.9 copy-done.3
  111.1 0.3 copy-done.4
  111.4 3.2 %relay.3 = (bf16[1536,128]{1,0:T(8,128)(2,1)}, bf16[1536,128]{1,0:T(8,128)(2,1)}) custom-call(bf16[1536,128]{1,0:T(8,128)(2,1)} %get-tuple-element.50.r2f_ref, bf16[1536,128]{1,0:T(8,128)(2,1)} %get-tuple-element.51.r2b_ref, bf16[1536,256]{1,0:T(8,128)(2,1)} %copy-done.3, bf16[1536,256]{1,0:T(8,128)(2,1)} %copy-done.4), custom_call_target="tpu_custom_call" | custom-call | flops 786432 | bytes 2359296 | tf_op jit(solution)/shard_map/relay/pallas_call | solution.py:393
  114.5 0.0 all-to-all-done.got_ref
  114.5 0.2 spread.1
  114.7 0.0 copy-start.12
  114.7 0.0 copy-start.10
  114.8 0.0 copy-start.11
  114.8 0.0 copy-start.9
  114.8 25.7 %all_to_all.10 = bf16[16,32,1408]{2,1,0:T(8,128)(2,1)S(1)} all-to-all(bf16[16,32,1408]{2,1,0:T(8,128)(2,1)S(1)} %spread.1), channel_id=1, replica_groups=mesh['z'=4,'y'=4,'c'=2,'mp'=4] {'z','y'}, dimensions={0} | all-to-all | bytes 2883584 | tf_op jit(solution)/shard_map/all_to_all | solution.py:514
  140.5 3.2 %collective-permute-start.9 = (bf16[512,1408]{1,0:T(8,128)(2,1)S(1)}, bf16[512,1408]{1,0:T(8,128)(2,1)S(1)}, u32[]{:S(2)}, u32[]{:S(2)}) collective-permute-start(bf16[512,1408]{1,0:T(8,128)(2,1)S(1)} %bitcast.7), channel_id=1, source_target_pairs={{0,4},{4,0},{1,5},{5,1},{2,6},{6,2},{3,7},{7,3},{8,12},{12,8},{9,1... | collective-permute-start | bytes 4325384 | tf_op jit(solution)/shard_map/ppermute | solution.py:515
  143.7 0.0 copy-done.12
  143.7 0.7 collective-permute-start.7
  144.4 0.0 copy-done.10
  144.4 2.0 %collective-permute-start.8 = (bf16[1536,128]{1,0:T(8,128)(2,1)S(1)}, bf16[1536,128]{1,0:T(8,128)(2,1)S(1)}, u32[]{:S(2)}, u32[]{:S(2)}) collective-permute-start(bf16[1536,128]{1,0:T(8,128)(2,1)S(1)} %copy-done.10), channel_id=1, source_target_pairs={{0,3},{1,0},{2,1},{3,2},{4,7},{5,4},{6,5},{7,6},{8,11},{9,8},{10,9... | collective-permute-start | bytes 1179656 | tf_op jit(solution)/shard_map/ppermute | solution.py:513
  146.4 0.0 copy-done.11
  146.4 0.0 collective-permute-start.5
  146.4 0.0 copy-done.9
  146.4 2.7 %collective-permute-start.6 = (bf16[1536,128]{1,0:T(8,128)(2,1)S(1)}, bf16[1536,128]{1,0:T(8,128)(2,1)S(1)}, u32[]{:S(2)}, u32[]{:S(2)}) collective-permute-start(bf16[1536,128]{1,0:T(8,128)(2,1)S(1)} %copy-done.9), channel_id=1, source_target_pairs={{0,3},{1,0},{2,1},{3,2},{4,7},{5,4},{6,5},{7,6},{8,11},{9,8},{10,9... | collective-permute-start | bytes 1179656 | tf_op jit(solution)/shard_map/ppermute | solution.py:513
  149.0 6.6 %collective-permute-done.7.t2f_ref = bf16[1536,128]{1,0:T(8,128)(2,1)S(1)} collective-permute-done((bf16[1536,128]{1,0:T(8,128)(2,1)S(1)}, bf16[1536,128]{1,0:T(8,128)(2,1)S(1)}, u32[]{:S(2)}, u32[]{:S(2)}) %collective-permute-start.7) | collective-permute-done | bytes 393248 | tf_op jit(solution)/shard_map/ppermute | solution.py:513
  155.6 0.0 copy-start.5
  155.6 0.0 collective-permute-done.8.t2b_ref
  155.6 0.0 copy-start.6
  155.6 0.8 copy-done.5
  156.4 0.1 copy-done.6
  156.5 4.9 %event_rows.2.refs_0_ = bf16[3072,256]{1,0:T(8,128)(2,1)} custom-call(s32[32,48]{1,0:T(8,128)} %lengths_ref.5, s32[3]{0:T(128)} %pad_add_fusion.place_ref, f32[1536,256]{1,0:T(8,128)} %get-tuple-element.57.own_ref, bf16[1536,256]{1,0:T(8,128)(2,1)} %copy-done.1, bf16[1536,256]{1,0:T(8,128)(2,1)} %copy-done.2, bf16[1536,128]{1,0:T(8,128)(2,1)} %copy-done.5, ...), custom_call_target="tpu_custom_call" | custom-call | flops 3145728 | bytes 4718592 | tf_op jit(solution)/shard_map/event_rows/pallas_call | solution.py:366
  161.4 2.7 %collective-permute-done.5.t2f_ref = bf16[1536,128]{1,0:T(8,128)(2,1)S(1)} collective-permute-done((bf16[1536,128]{1,0:T(8,128)(2,1)S(1)}, bf16[1536,128]{1,0:T(8,128)(2,1)S(1)}, u32[]{:S(2)}, u32[]{:S(2)}) %collective-permute-start.5) | collective-permute-done | bytes 393248 | tf_op jit(solution)/shard_map/ppermute | solution.py:513
  164.1 0.0 copy-start.7
  164.1 0.0 collective-permute-done.6.t2b_ref
  164.1 0.0 copy-start.8
  164.1 0.8 copy-done.7
  164.8 0.1 copy-done.8
  165.0 0.0 copy-start
  165.0 5.1 %event_rows.3 = bf16[3072,256]{1,0:T(8,128)(2,1)} custom-call(s32[32,48]{1,0:T(8,128)} %lengths_ref.5, s32[3]{0:T(128)} %pad_add_fusion.place_ref, f32[1536,256]{1,0:T(8,128)} %get-tuple-element.41.own_ref, bf16[1536,256]{1,0:T(8,128)(2,1)} %copy-done.3, bf16[1536,256]{1,0:T(8,128)(2,1)} %copy-done.4, ...), custom_call_target="tpu_custom_call", output_to_operand_aliasing={{}: (8, {})} | custom-call | flops 3145728 | bytes 4718592 | tf_op jit(solution)/shard_map/event_rows/pallas_call | solution.py:366
  170.1 0.0 collective-permute-done.9.other_ref
  170.1 0.0 copy-done
  170.1 5.2 %weights_out.1 = (f32[1024,4,256]{2,1,0:T(4,128)}, f32[256,1024]{1,0:T(8,128)}, f32[4,256]{1,0:T(4,128)}, f32[1,256]{1,0:T(1,128)}) custom-call(s32[3]{0:T(128)S(1)} %copy-done, bf16[512,1408]{1,0:T(8,128)(2,1)S(1)} %bitcast.8, bf16[512,1408]{1,0:T(8,128)(2,1)S(1)} %collective-permute-done.9.other_ref), custom_call_target="tpu_custom_call" | custom-call | flops 4000000 | bytes 8500000 | tf_op jit(solution)/shard_map/weights_out/pallas_call | solution.py:456
Async XLA Ops:
  50.1 4.5 %collective-permute-start = (bf16[512,1408]{1,0:T(8,128)(2,1)}, bf16[512,1408]{1,0:T(8,128)(2,1)S(1)}, u32[]{:S(2)}, u32[]{:S(2)}) collective-permute-start(bf16[512,1408]{1,0:T(8,128)(2,1)} %get-tuple-element.38), channel_id=1, source_target_pairs={{0,4},{4,0},{1,5},{5,1},{2,6},{6,2},{3,7},{7,3},{8,12},{12,8},{9,1... | collective-permute-start | bytes 4325384 | tf_op jit(solution)/shard_map/ppermute | solution.py:498
  57.9 56.6 %all-to-all-start = ((bf16[16,32,1408]{2,1,0:T(8,128)(2,1)}), bf16[16,32,1408]{2,1,0:T(8,128)(2,1)S(1)}, u32[]{:S(2)}, u32[]{:S(2)}) async-start(bf16[16,32,1408]{2,1,0:T(8,128)(2,1)} %bitcast.4), calls=%async_computation | async-start | bytes 2883584 | tf_op jit(solution)/shard_map/all_to_all | solution.py:505
  73.4 19.9 %collective-permute-start.3 = (bf16[1536,256]{1,0:T(8,128)(2,1)}, bf16[1536,256]{1,0:T(8,128)(2,1)S(1)}, u32[]{:S(2)}, u32[]{:S(2)}) collective-permute-start(bf16[1536,256]{1,0:T(8,128)(2,1)} %get-tuple-element.46), channel_id=1, source_target_pairs={{0,1},{1,2},{2,3},{3,0},{4,5},{5,6},{6,7},{7,4},{8,9},{9,10},{10,1... | collective-permute-start | bytes 2359304 | tf_op jit(solution)/shard_map/ppermute | solution.py:502
  74.7 18.7 %collective-permute-start.4 = (bf16[1536,256]{1,0:T(8,128)(2,1)}, bf16[1536,256]{1,0:T(8,128)(2,1)S(1)}, u32[]{:S(2)}, u32[]{:S(2)}) collective-permute-start(bf16[1536,256]{1,0:T(8,128)(2,1)} %get-tuple-element.47), channel_id=1, source_target_pairs={{0,3},{1,0},{2,1},{3,2},{4,7},{5,4},{6,5},{7,6},{8,11},{9,8},{10,9... | collective-permute-start | bytes 2359304 | tf_op jit(solution)/shard_map/ppermute | solution.py:502
  83.9 26.3 %collective-permute-start.1 = (bf16[1536,256]{1,0:T(8,128)(2,1)}, bf16[1536,256]{1,0:T(8,128)(2,1)S(1)}, u32[]{:S(2)}, u32[]{:S(2)}) collective-permute-start(bf16[1536,256]{1,0:T(8,128)(2,1)} %get-tuple-element.42), channel_id=1, source_target_pairs={{0,1},{1,2},{2,3},{3,0},{4,5},{5,6},{6,7},{7,4},{8,9},{9,10},{10,1... | collective-permute-start | bytes 2359304 | tf_op jit(solution)/shard_map/ppermute | solution.py:507
  84.0 26.3 %collective-permute-start.2 = (bf16[1536,256]{1,0:T(8,128)(2,1)}, bf16[1536,256]{1,0:T(8,128)(2,1)S(1)}, u32[]{:S(2)}, u32[]{:S(2)}) collective-permute-start(bf16[1536,256]{1,0:T(8,128)(2,1)} %get-tuple-element.43), channel_id=1, source_target_pairs={{0,3},{1,0},{2,1},{3,2},{4,7},{5,4},{6,5},{7,6},{8,11},{9,8},{10,9... | collective-permute-start | bytes 2359304 | tf_op jit(solution)/shard_map/ppermute | solution.py:507
  93.4 0.9 copy-start.1
  93.4 1.2 copy-start.2
  110.2 0.9 copy-start.3
  110.2 1.2 copy-start.4
  114.7 28.9 %copy-start.12 = (bf16[1536,128]{1,0:T(8,128)(2,1)S(1)}, bf16[1536,128]{1,0:T(8,128)(2,1)}, u32[]{:S(2)}) copy-start(bf16[1536,128]{1,0:T(8,128)(2,1)} %get-tuple-element.58) | copy-start | bytes 1179652
  114.7 29.6 %copy-start.10 = (bf16[1536,128]{1,0:T(8,128)(2,1)S(1)}, bf16[1536,128]{1,0:T(8,128)(2,1)}, u32[]{:S(2)}) copy-start(bf16[1536,128]{1,0:T(8,128)(2,1)} %get-tuple-element.59) | copy-start | bytes 1179652
  114.8 31.6 %copy-start.11 = (bf16[1536,128]{1,0:T(8,128)(2,1)S(1)}, bf16[1536,128]{1,0:T(8,128)(2,1)}, u32[]{:S(2)}) copy-start(bf16[1536,128]{1,0:T(8,128)(2,1)} %get-tuple-element.55) | copy-start | bytes 1179652
  114.8 31.6 %copy-start.9 = (bf16[1536,128]{1,0:T(8,128)(2,1)S(1)}, bf16[1536,128]{1,0:T(8,128)(2,1)}, u32[]{:S(2)}) copy-start(bf16[1536,128]{1,0:T(8,128)(2,1)} %get-tuple-element.56) | copy-start | bytes 1179652
  140.5 29.6 %collective-permute-start.9 = (bf16[512,1408]{1,0:T(8,128)(2,1)S(1)}, bf16[512,1408]{1,0:T(8,128)(2,1)S(1)}, u32[]{:S(2)}, u32[]{:S(2)}) collective-permute-start(bf16[512,1408]{1,0:T(8,128)(2,1)S(1)} %bitcast.7), channel_id=1, source_target_pairs={{0,4},{4,0},{1,5},{5,1},{2,6},{6,2},{3,7},{7,3},{8,12},{12,8},{9,1... | collective-permute-start | bytes 4325384 | tf_op jit(solution)/shard_map/ppermute | solution.py:515
  143.7 12.0 %collective-permute-start.7 = (bf16[1536,128]{1,0:T(8,128)(2,1)S(1)}, bf16[1536,128]{1,0:T(8,128)(2,1)S(1)}, u32[]{:S(2)}, u32[]{:S(2)}) collective-permute-start(bf16[1536,128]{1,0:T(8,128)(2,1)S(1)} %copy-done.12), channel_id=1, source_target_pairs={{0,1},{1,2},{2,3},{3,0},{4,5},{5,6},{6,7},{7,4},{8,9},{9,10},{10,1... | collective-permute-start | bytes 1179656 | tf_op jit(solution)/shard_map/ppermute | solution.py:513
  144.4 11.3 %collective-permute-start.8 = (bf16[1536,128]{1,0:T(8,128)(2,1)S(1)}, bf16[1536,128]{1,0:T(8,128)(2,1)S(1)}, u32[]{:S(2)}, u32[]{:S(2)}) collective-permute-start(bf16[1536,128]{1,0:T(8,128)(2,1)S(1)} %copy-done.10), channel_id=1, source_target_pairs={{0,3},{1,0},{2,1},{3,2},{4,7},{5,4},{6,5},{7,6},{8,11},{9,8},{10,9... | collective-permute-start | bytes 1179656 | tf_op jit(solution)/shard_map/ppermute | solution.py:513
  146.4 17.7 %collective-permute-start.5 = (bf16[1536,128]{1,0:T(8,128)(2,1)S(1)}, bf16[1536,128]{1,0:T(8,128)(2,1)S(1)}, u32[]{:S(2)}, u32[]{:S(2)}) collective-permute-start(bf16[1536,128]{1,0:T(8,128)(2,1)S(1)} %copy-done.11), channel_id=1, source_target_pairs={{0,1},{1,2},{2,3},{3,0},{4,5},{5,6},{6,7},{7,4},{8,9},{9,10},{10,1... | collective-permute-start | bytes 1179656 | tf_op jit(solution)/shard_map/ppermute | solution.py:513
  146.4 17.7 %collective-permute-start.6 = (bf16[1536,128]{1,0:T(8,128)(2,1)S(1)}, bf16[1536,128]{1,0:T(8,128)(2,1)S(1)}, u32[]{:S(2)}, u32[]{:S(2)}) collective-permute-start(bf16[1536,128]{1,0:T(8,128)(2,1)S(1)} %copy-done.9), channel_id=1, source_target_pairs={{0,3},{1,0},{2,1},{3,2},{4,7},{5,4},{6,5},{7,6},{8,11},{9,8},{10,9... | collective-permute-start | bytes 1179656 | tf_op jit(solution)/shard_map/ppermute | solution.py:513
  155.6 0.8 copy-start.5
  155.6 0.9 copy-start.6
  164.1 0.8 copy-start.7
  164.1 0.9 copy-start.8
  165.0 5.1 %copy-start = (s32[3]{0:T(128)S(1)}, s32[3]{0:T(128)}, u32[]{:S(2)}) copy-start(s32[3]{0:T(128)} %pad_add_fusion.place_ref) | copy-start | bytes 40

commit v3 on v1

--- a/solution.py
+++ b/solution.py
@@ -18,7 +18,6 @@
 MODEL = 1024
 COLUMNS = 5 * WIDTH + 128
 PIECES = 8
-ROW_PARTS = 2
 HISTORY = 3
 F32 = jnp.float32
 BF16 = jnp.bfloat16
@@ -294,78 +293,70 @@
     grads = pg_ref[...]
     me = place_ref[2]
 
-    def chunk(shift):
+    def share(shift):
         start = pl.multiple_of(lax.rem(me + shift, 4) * WIDTH, WIDTH)
         return dot(grads, w_ref[pl.ds(start, WIDTH), :], NT)
 
-    ahead_out[...] = chunk(1).astype(BF16)
-    across_out[...] = chunk(2).astype(BF16)
-    behind_out[...] = chunk(3).astype(BF16)
-    own_out[...] = chunk(0)
-
-
-def partial_rows(place, grads, w, begin, count):
+    ahead_out[...] = share(1).astype(BF16)
+    across_out[...] = share(2).astype(BF16)
+    behind_out[...] = share(3).astype(BF16)
+    own_out[...] = share(0)
+
+
+def partial_rows(place, grads, w):
     block = 512
-    here = pl.BlockSpec((block, WIDTH), lambda i, p: (i, 0))
+    rows = grads.shape[0]
+    wide = pl.BlockSpec((block, WIDTH), lambda i, p: (i, 0))
     return pl.pallas_call(
         partial_kernel,
-        out_shape=[jax.ShapeDtypeStruct((count, WIDTH), F32)] + [jax.ShapeDtypeStruct((count, WIDTH), BF16)] * 3,
+        out_shape=[jax.ShapeDtypeStruct((rows, WIDTH), F32)] + [jax.ShapeDtypeStruct((rows, WIDTH), BF16)] * 3,
         grid_spec=pltpu.PrefetchScalarGridSpec(
             num_scalar_prefetch=1,
-            grid=(count // block,),
+            grid=(rows // block,),
             in_specs=[
-                pl.BlockSpec((block, MODEL), lambda i, p: (begin // block + i, 0)),
+                pl.BlockSpec((block, MODEL), lambda i, p: (i, 0)),
                 pl.BlockSpec(w.shape, lambda i, p: (0, 0)),
             ],
-            out_specs=[here, here, here, here],
+            out_specs=[wide, wide, wide, wide],
         ),
         compiler_params=pltpu.CompilerParams(
             dimension_semantics=("arbitrary",), vmem_limit_bytes=56 * 1024 * 1024
         ),
         cost_estimate=pl.CostEstimate(
-            flops=2 * count * MODEL * MODEL, bytes_accessed=count * 4096 + w.size * 2, transcendentals=0
+            flops=2 * rows * MODEL * MODEL, bytes_accessed=rows * 4608 + w.size * 2, transcendentals=0
         ),
         name="partial_rows",
     )(place, grads, w)
 
 
-def event_kernel(begin, block, lengths_ref, place_ref, own_ref, a_ref, b_ref, c_ref, g_ref, *refs):
-    out_ref = refs[-1]
+def event_kernel(block, lengths_ref, place_ref, own_ref, a_ref, b_ref, c_ref, g_ref, out_ref):
     home = place_ref[0]
     tiles = lax.fori_loop(0, lengths_ref.shape[1], lambda u, t: t + lengths_ref[home, u], jnp.int32(0))
-    row = lax.broadcasted_iota(jnp.int32, (block, WIDTH), 0) + begin + pl.program_id(0) * block
-    g = jnp.where(row < tiles * TILE, g_ref[...].astype(F32), 0.0)
+    row = lax.broadcasted_iota(jnp.int32, (block, WIDTH), 0) + pl.program_id(0) * block
+    base = own_ref[...] + jnp.where(row < tiles * TILE, g_ref[...].astype(F32), 0.0)
     got = a_ref[...].astype(F32) + b_ref[...].astype(F32) + c_ref[...].astype(F32)
-    out_ref[...] = (own_ref[...] + got + g).astype(BF16)
-
-
-def event_rows(lengths, place, shares, g, begin, out):
+    out_ref[...] = (base + got).astype(BF16)
+
+
+def event_rows(lengths, place, shares, g):
     block = 512
-    count = shares[0].shape[0]
-    here = pl.BlockSpec((block, WIDTH), lambda i, f, p: (i, 0))
-    in_specs = [here] * 4 + [pl.BlockSpec((block, WIDTH), lambda i, f, p: (begin // block + i, p[2]))]
-    operands = list(shares) + [g]
-    aliases = {}
-    if out is not None:
-        in_specs.append(pl.BlockSpec(memory_space=pl.ANY))
-        operands.append(out)
-        aliases = {7: 0}
+    rows = g.shape[0]
+    wide = pl.BlockSpec((block, WIDTH), lambda i, f, p: (i, 0))
     return pl.pallas_call(
-        functools.partial(event_kernel, begin, block),
-        out_shape=jax.ShapeDtypeStruct((g.shape[0], WIDTH), BF16),
+        functools.partial(event_kernel, block),
+        out_shape=jax.ShapeDtypeStruct((rows, WIDTH), BF16),
         grid_spec=pltpu.PrefetchScalarGridSpec(
             num_scalar_prefetch=2,
-            grid=(count // block,),
-            in_specs=in_specs,
-            out_specs=pl.BlockSpec((block, WIDTH), lambda i, f, p: (begin // block + i, 0)),
-        ),
-        input_output_aliases=aliases,
+            grid=(rows // block,),
+            in_specs=[wide, wide, wide, wide, pl.BlockSpec((block, WIDTH), lambda i, f, p: (i, p[2]))],
+            out_specs=wide,
+        ),
         compiler_params=pltpu.CompilerParams(
             dimension_semantics=("arbitrary",), vmem_limit_bytes=56 * 1024 * 1024
         ),
-        cost_estimate=pl.CostEstimate(flops=count * 2048, bytes_accessed=count * 3072, transcendentals=0),
+        cost_estimate=pl.CostEstimate(flops=rows * 2048, bytes_accessed=rows * 3584, transcendentals=0),
         name="event_rows",
-    )(lengths, place, *operands)
+    )(lengths, place, *shares, g)
 
 
 def spread_kernel(got_ref, out_ref):
@@ -459,23 +450,16 @@
 
     swap = [(0, 1), (1, 0)]
     half = MODEL // 2
-    kept = kept + lax.ppermute(sent, "c", swap).astype(F32)
-    pieces = lax.all_to_all(kept.astype(BF16).reshape(16, half // 16, COLUMNS), ("z", "y"), 0, 0, tiled=True)
+    other = lax.ppermute(sent, "c", swap)
+    shares = partial_rows(place, grads, weight_in)
+    kept = (kept + other.astype(F32)).astype(BF16)
+    shares, kept = lax.optimization_barrier((shares, kept))
+    shares = [shares[0]] + [lax.ppermute(shares[step], "mp", ring(step)) for step in (1, 2, 3)]
+    pieces = lax.all_to_all(kept.reshape(16, half // 16, COLUMNS), ("z", "y"), 0, 0, tiled=True)
     pieces = lax.all_to_all(spread(pieces), ("z", "y"), 0, 0, tiled=True).reshape(half, COLUMNS)
     other = lax.ppermute(pieces, "c", swap)
     proj_grad, out_grad, bias_grad, gain_grad = weights_out(place, pieces, other)
-
-    event_grads = None
-    count = rows // ROW_PARTS
-    for n in range(ROW_PARTS):
-        own, ahead, across, behind = partial_rows(place, grads, weight_in, n * count, count)
-        shares = (
-            own,
-            lax.ppermute(ahead, "mp", ring(1)),
-            lax.ppermute(across, "mp", ring(2)),
-            lax.ppermute(behind, "mp", ring(3)),
-        )
-        event_grads = event_rows(lengths, place, shares, upstream, n * count, event_grads)
+    event_grads = event_rows(lengths, place, shares, upstream)
     return event_grads, proj_grad, bias_grad, gain_grad.reshape(WIDTH), out_grad
 
 

time: 182 us -> 182 us (level)
  waiting for transfers between devices: 49.5 us -> 62.8 us
  Pallas kernels: 80.5 us -> 74.6 us
  starting transfers between devices: 16.5 us -> 13.5 us
  other arithmetic: 2.76 us -> 0.87 us
    ppermute x7 -> x4, waiting for transfers between devices: 41.2 us -> 48 us  [the longest x3 48 us: body(): lax.ppermute(shares[step], 'mp', ring(step))]
    all_to_all x1, waiting for transfers between devices: 8.29 us -> 14.8 us  [body(): lax.all_to_all(spread(pieces), ('z', 'y'), 0, 0, tiled=True)]
    pallas_call x4 -> x2, Pallas kernels: 25.2 us -> 19.3 us  [the longest x1 12 us: partial_rows(): pl.pallas_call(partial_kernel, out_shape=[jax.ShapeDtypeStruct((rows, WID...]
    ppermute x7 -> x4, starting transfers between devices: 9.27 us -> 6.32 us  [the longest x3 4.89 us: body(): lax.ppermute(shares[step], 'mp', ring(step))]
    convert_element_type x1, other arithmetic: 2.17 us -> 0.25 us  [body(): kept = (kept + other.astype(F32)).astype(BF16)]
  transfers between devices with their start and end apart: 9 -> 6, of which waited for: 7 -> 4; matrix products, arithmetic and copies ran while one was open for 0% -> 0% of each run, Pallas kernels for 14% -> 11%
where the time goes in v3:
time: 182 us; the launch traced here: 181 us
  Pallas kernels  74.6 us (41%)
  waiting for transfers between devices  62.8 us (35%)
  blocking collectives  28.6 us (16%)
  starting transfers between devices  13.5 us (7%)
    pallas_call x1, Pallas kernels, layer(): pl.pallas_call(functools.partial(layer_kernel, steps), out_shape=[jax.Sha...  48.8 us
    ppermute x3, waiting for transfers between devices, body(): lax.ppermute(shares[step], 'mp', ring(step))  48 us
    all_to_all x1, blocking collectives, body(): lax.all_to_all(kept.reshape(16, half // 16, COLUMNS), ('z', 'y'), 0, 0, t...  28.6 us
    all_to_all x1, waiting for transfers between devices, body(): lax.all_to_all(spread(pieces), ('z', 'y'), 0, 0, tiled=True)  14.8 us
    pallas_call x1, Pallas kernels, partial_rows(): pl.pallas_call(partial_kernel, out_shape=[jax.ShapeDtypeStruct((rows, WID...  12 us
    pallas_call x1, Pallas kernels, event_rows(): pl.pallas_call(functools.partial(event_kernel, block), out_shape=jax.Shap...  7.34 us
    pallas_call x1, Pallas kernels, weights_out(): pl.pallas_call(weights_kernel, out_shape=[jax.ShapeDtypeStruct((MODEL, 4,...  5.17 us
    ppermute x3, starting transfers between devices, body(): lax.ppermute(shares[step], 'mp', ring(step))  4.89 us
  transfers between devices with their start and end apart: 6, of which 4 were waited for; matrix products, arithmetic and copies ran while one was open for 0% of the time, Pallas kernels for 11%

profile of v3, /device:TPU:1, one launch (start us, length us, event | category | flops | bytes accessed | tf_op | source)
XLA Modules:
  0.0 181.0 jit_solution(293462475223335775)
XLA Ops:
  0.6 0.6 pad_add_fusion.place_ref
  1.3 48.8 %layer.1 = (bf16[3072,1024]{1,0:T(8,128)(2,1)}, bf16[512,1408]{1,0:T(8,128)(2,1)}, f32[512,1408]{1,0:T(8,128)}, bf16[1024,1024]{1,0:T(8,128)(2,1)}) custom-call(s32[32,48]{1,0:T(8,128)} %lengths_ref.3, s32[3]{0:T(128)} %pad_add_fusion.place_ref, bf16[3072,1024]{1,0:T(8,128)(2,1)} %xp_ref.1, bf16[3072,1024]{1,0:T(8,128)(2,1)} %g_ref.3, ...), custom_call_target="tpu_custom_call" | custom-call | flops 18522046464 | bytes 24576000 | tf_op jit(solution)/shard_map/layer/pallas_call | solution.py:238
  50.0 1.4 collective-permute-start
  51.5 0.0 copy-start.1
  51.5 12.0 %partial_rows.1 = (f32[3072,256]{1,0:T(8,128)}, bf16[3072,256]{1,0:T(8,128)(2,1)}, bf16[3072,256]{1,0:T(8,128)(2,1)}, bf16[3072,256]{1,0:T(8,128)(2,1)}) custom-call(s32[3]{0:T(128)} %pad_add_fusion.place_ref, bf16[3072,1024]{1,0:T(8,128)(2,1)} %get-tuple-element.22.pg_ref, bf16[1024,1024]{1,0:T(8,128)(2,1)} %get-tuple-element.23.w_ref), custom_call_target="tpu_custom_call" | custom-call | flops 6442450944 | bytes 16252928 | tf_op jit(solution)/shard_map/partial_rows/pallas_call | solution.py:310
  63.4 0.0 collective-permute-done
  63.4 0.0 copy-done.1
  63.5 0.2 add_convert_fusion
  63.7 28.6 %all_to_all.10.got_ref = bf16[16,32,1408]{2,1,0:T(8,128)(2,1)S(1)} all-to-all(bf16[16,32,1408]{2,1,0:T(8,128)(2,1)S(1)} %bitcast.9), channel_id=1, replica_groups=mesh['z'=4,'y'=4,'c'=2,'mp'=4] {'z','y'}, dimensions={0} | all-to-all | bytes 2883584 | tf_op jit(solution)/shard_map/all_to_all | solution.py:458
  92.3 1.3 spread.1
  93.6 3.7 %all-to-all-start.1 = ((bf16[16,32,1408]{2,1,0:T(8,128)(2,1)}), bf16[16,32,1408]{2,1,0:T(8,128)(2,1)S(1)}, u32[]{:S(2)}, u32[]{:S(2)}) async-start(bf16[16,32,1408]{2,1,0:T(8,128)(2,1)} %spread.1), calls=%async_computation.1 | async-start | bytes 2883584 | tf_op jit(solution)/shard_map/all_to_all | solution.py:459
  97.3 1.3 collective-permute-start.1
  98.6 2.4 %collective-permute-start.2 = (bf16[3072,256]{1,0:T(8,128)(2,1)}, bf16[3072,256]{1,0:T(8,128)(2,1)}, u32[]{:S(2)}, u32[]{:S(2)}) collective-permute-start(bf16[3072,256]{1,0:T(8,128)(2,1)} %get-tuple-element.32), channel_id=1, source_target_pairs={{0,2},{1,3},{2,0},{3,1},{4,6},{5,7},{6,4},{7,5},{8,10},{9,11},{10,... | collective-permute-start | bytes 4718600 | tf_op jit(solution)/shard_map/ppermute | solution.py:457
  101.1 1.2 collective-permute-start.3
  102.2 14.8 %all-to-all-done.1 = bf16[16,32,1408]{2,1,0:T(8,128)(2,1)S(1)} async-done(((bf16[16,32,1408]{2,1,0:T(8,128)(2,1)}), bf16[16,32,1408]{2,1,0:T(8,128)(2,1)S(1)}, u32[]{:S(2)}, u32[]{:S(2)}) %all-to-all-start.1) | async-done | bytes 1441824 | tf_op jit(solution)/shard_map/all_to_all | solution.py:459
  117.0 0.0 copy-start
  117.0 3.5 %collective-permute-start.4 = (bf16[512,1408]{1,0:T(8,128)(2,1)S(1)}, bf16[512,1408]{1,0:T(8,128)(2,1)S(1)}, u32[]{:S(2)}, u32[]{:S(2)}) collective-permute-start(bf16[512,1408]{1,0:T(8,128)(2,1)S(1)} %bitcast.7), channel_id=1, source_target_pairs={{0,4},{4,0},{1,5},{5,1},{2,6},{6,2},{3,7},{7,3},{8,12},{12,8},{9,1... | collective-permute-start | bytes 4325384 | tf_op jit(solution)/shard_map/ppermute | solution.py:460
  120.5 12.8 %collective-permute-done.1.a_ref = bf16[3072,256]{1,0:T(8,128)(2,1)S(1)} collective-permute-done((bf16[3072,256]{1,0:T(8,128)(2,1)}, bf16[3072,256]{1,0:T(8,128)(2,1)S(1)}, u32[]{:S(2)}, u32[]{:S(2)}) %collective-permute-start.1) | collective-permute-done | bytes 1572896 | tf_op jit(solution)/shard_map/ppermute | solution.py:457
  133.3 0.0 copy-start.2
  133.3 34.8 %collective-permute-done.2.b_ref = bf16[3072,256]{1,0:T(8,128)(2,1)} collective-permute-done((bf16[3072,256]{1,0:T(8,128)(2,1)}, bf16[3072,256]{1,0:T(8,128)(2,1)}, u32[]{:S(2)}, u32[]{:S(2)}) %collective-permute-start.2) | collective-permute-done | bytes 1572896 | tf_op jit(solution)/shard_map/ppermute | solution.py:457
  168.1 0.4 collective-permute-done.3.c_ref
  168.5 0.0 copy-done.2
  168.5 7.3 %event_rows.1 = bf16[3072,256]{1,0:T(8,128)(2,1)} custom-call(s32[32,48]{1,0:T(8,128)} %lengths_ref.3, s32[3]{0:T(128)} %pad_add_fusion.place_ref, f32[3072,256]{1,0:T(8,128)} %get-tuple-element.30.own_ref, bf16[3072,256]{1,0:T(8,128)(2,1)} %copy-done.2, bf16[3072,256]{1,0:T(8,128)(2,1)} %collective-permute-done.2.b_ref, ...), custom_call_target="tpu_custom_call" | custom-call | flops 6291456 | bytes 11010048 | tf_op jit(solution)/shard_map/event_rows/pallas_call | solution.py:345
  175.8 0.0 collective-permute-done.4.other_ref
  175.9 0.0 copy-done
  175.9 5.2 %weights_out.1 = (f32[1024,4,256]{2,1,0:T(4,128)}, f32[256,1024]{1,0:T(8,128)}, f32[4,256]{1,0:T(4,128)}, f32[1,256]{1,0:T(1,128)}) custom-call(s32[3]{0:T(128)S(1)} %copy-done, bf16[512,1408]{1,0:T(8,128)(2,1)S(1)} %bitcast.8, bf16[512,1408]{1,0:T(8,128)(2,1)S(1)} %collective-permute-done.4.other_ref), custom_call_target="tpu_custom_call" | custom-call | flops 4000000 | bytes 8500000 | tf_op jit(solution)/shard_map/weights_out/pallas_call | solution.py:411
Async XLA Ops:
  50.0 13.4 %collective-permute-start = (bf16[512,1408]{1,0:T(8,128)(2,1)}, bf16[512,1408]{1,0:T(8,128)(2,1)S(1)}, u32[]{:S(2)}, u32[]{:S(2)}) collective-permute-start(bf16[512,1408]{1,0:T(8,128)(2,1)} %get-tuple-element.29), channel_id=1, source_target_pairs={{0,4},{4,0},{1,5},{5,1},{2,6},{6,2},{3,7},{7,3},{8,12},{12,8},{9,1... | collective-permute-start | bytes 4325384 | tf_op jit(solution)/shard_map/ppermute | solution.py:453
  51.5 12.0 %copy-start.1 = (f32[512,1408]{1,0:T(8,128)S(1)}, f32[512,1408]{1,0:T(8,128)}, u32[]{:S(2)}) copy-start(f32[512,1408]{1,0:T(8,128)} %get-tuple-element.28) | copy-start | bytes 8650756
  93.6 23.4 %all-to-all-start.1 = ((bf16[16,32,1408]{2,1,0:T(8,128)(2,1)}), bf16[16,32,1408]{2,1,0:T(8,128)(2,1)S(1)}, u32[]{:S(2)}, u32[]{:S(2)}) async-start(bf16[16,32,1408]{2,1,0:T(8,128)(2,1)} %spread.1), calls=%async_computation.1 | async-start | bytes 2883584 | tf_op jit(solution)/shard_map/all_to_all | solution.py:459
  97.3 36.0 %collective-permute-start.1 = (bf16[3072,256]{1,0:T(8,128)(2,1)}, bf16[3072,256]{1,0:T(8,128)(2,1)S(1)}, u32[]{:S(2)}, u32[]{:S(2)}) collective-permute-start(bf16[3072,256]{1,0:T(8,128)(2,1)} %get-tuple-element.31), channel_id=1, source_target_pairs={{0,1},{1,2},{2,3},{3,0},{4,5},{5,6},{6,7},{7,4},{8,9},{9,10},{10,1... | collective-permute-start | bytes 4718600 | tf_op jit(solution)/shard_map/ppermute | solution.py:457
  98.6 69.5 %collective-permute-start.2 = (bf16[3072,256]{1,0:T(8,128)(2,1)}, bf16[3072,256]{1,0:T(8,128)(2,1)}, u32[]{:S(2)}, u32[]{:S(2)}) collective-permute-start(bf16[3072,256]{1,0:T(8,128)(2,1)} %get-tuple-element.32), channel_id=1, source_target_pairs={{0,2},{1,3},{2,0},{3,1},{4,6},{5,7},{6,4},{7,5},{8,10},{9,11},{10,... | collective-permute-start | bytes 4718600 | tf_op jit(solution)/shard_map/ppermute | solution.py:457
  101.1 67.4 %collective-permute-start.3 = (bf16[3072,256]{1,0:T(8,128)(2,1)}, bf16[3072,256]{1,0:T(8,128)(2,1)}, u32[]{:S(2)}, u32[]{:S(2)}) collective-permute-start(bf16[3072,256]{1,0:T(8,128)(2,1)} %get-tuple-element.33), channel_id=1, source_target_pairs={{0,3},{1,0},{2,1},{3,2},{4,7},{5,4},{6,5},{7,6},{8,11},{9,8},{10,9... | collective-permute-start | bytes 4718600 | tf_op jit(solution)/shard_map/ppermute | solution.py:457
  117.0 58.8 %copy-start = (s32[3]{0:T(128)S(1)}, s32[3]{0:T(128)}, u32[]{:S(2)}) copy-start(s32[3]{0:T(128)} %pad_add_fusion.place_ref) | copy-start | bytes 40
  117.0 58.8 %collective-permute-start.4 = (bf16[512,1408]{1,0:T(8,128)(2,1)S(1)}, bf16[512,1408]{1,0:T(8,128)(2,1)S(1)}, u32[]{:S(2)}, u32[]{:S(2)}) collective-permute-start(bf16[512,1408]{1,0:T(8,128)(2,1)S(1)} %bitcast.7), channel_id=1, source_target_pairs={{0,4},{4,0},{1,5},{5,1},{2,6},{6,2},{3,7},{7,3},{8,12},{12,8},{9,1... | collective-permute-start | bytes 4325384 | tf_op jit(solution)/shard_map/ppermute | solution.py:460
  133.3 35.2 %copy-start.2 = (bf16[3072,256]{1,0:T(8,128)(2,1)}, bf16[3072,256]{1,0:T(8,128)(2,1)S(1)}, u32[]{:S(2)}) copy-start(bf16[3072,256]{1,0:T(8,128)(2,1)S(1)} %collective-permute-done.1.a_ref) | copy-start | bytes 4718596

commit v4 on v3

--- a/solution.py
+++ b/solution.py
@@ -19,6 +19,7 @@
 COLUMNS = 5 * WIDTH + 128
 PIECES = 8
 HISTORY = 3
+ROW_PARTS = (1280, 1024, 768)
 F32 = jnp.float32
 BF16 = jnp.bfloat16
 NT = (((1,), (1,)), ((), ()))
@@ -303,9 +304,8 @@
     own_out[...] = share(0)
 
 
-def partial_rows(place, grads, w):
-    block = 512
-    rows = grads.shape[0]
+def partial_rows(place, grads, w, begin, rows):
+    block = 256
     wide = pl.BlockSpec((block, WIDTH), lambda i, p: (i, 0))
     return pl.pallas_call(
         partial_kernel,
@@ -314,7 +314,7 @@
             num_scalar_prefetch=1,
             grid=(rows // block,),
             in_specs=[
-                pl.BlockSpec((block, MODEL), lambda i, p: (i, 0)),
+                pl.BlockSpec((block, MODEL), lambda i, p: (begin // block + i, 0)),
                 pl.BlockSpec(w.shape, lambda i, p: (0, 0)),
             ],
             out_specs=[wide, wide, wide, wide],
@@ -329,34 +329,49 @@
     )(place, grads, w)
 
 
-def event_kernel(block, lengths_ref, place_ref, own_ref, a_ref, b_ref, c_ref, g_ref, out_ref):
+def event_kernel(begin, block, lengths_ref, place_ref, own_ref, a_ref, b_ref, c_ref, g_ref, *refs):
+    out_ref, tiles_ref = refs[-2:]
     home = place_ref[0]
-    tiles = lax.fori_loop(0, lengths_ref.shape[1], lambda u, t: t + lengths_ref[home, u], jnp.int32(0))
-    row = lax.broadcasted_iota(jnp.int32, (block, WIDTH), 0) + pl.program_id(0) * block
-    base = own_ref[...] + jnp.where(row < tiles * TILE, g_ref[...].astype(F32), 0.0)
+
+    @pl.when(pl.program_id(0) == 0)
+    def _():
+        tiles_ref[0] = lax.fori_loop(0, lengths_ref.shape[1], lambda u, t: t + lengths_ref[home, u], jnp.int32(0))
+
+    row = lax.broadcasted_iota(jnp.int32, (block, WIDTH), 0) + begin + pl.program_id(0) * block
+    base = own_ref[...] + jnp.where(row < tiles_ref[0] * TILE, g_ref[...].astype(F32), 0.0)
     got = a_ref[...].astype(F32) + b_ref[...].astype(F32) + c_ref[...].astype(F32)
     out_ref[...] = (base + got).astype(BF16)
 
 
-def event_rows(lengths, place, shares, g):
-    block = 512
-    rows = g.shape[0]
+def event_rows(lengths, place, shares, g, begin, out):
+    block = 256
+    rows = shares[0].shape[0]
     wide = pl.BlockSpec((block, WIDTH), lambda i, f, p: (i, 0))
+    in_specs = [wide, wide, wide, wide]
+    in_specs.append(pl.BlockSpec((block, WIDTH), lambda i, f, p: (begin // block + i, p[2])))
+    operands = list(shares) + [g]
+    aliases = {}
+    if out is not None:
+        in_specs.append(pl.BlockSpec(memory_space=pl.ANY))
+        operands.append(out)
+        aliases = {7: 0}
     return pl.pallas_call(
-        functools.partial(event_kernel, block),
-        out_shape=jax.ShapeDtypeStruct((rows, WIDTH), BF16),
+        functools.partial(event_kernel, begin, block),
+        out_shape=jax.ShapeDtypeStruct((g.shape[0], WIDTH), BF16),
         grid_spec=pltpu.PrefetchScalarGridSpec(
             num_scalar_prefetch=2,
             grid=(rows // block,),
-            in_specs=[wide, wide, wide, wide, pl.BlockSpec((block, WIDTH), lambda i, f, p: (i, p[2]))],
-            out_specs=wide,
-        ),
+            in_specs=in_specs,
+            out_specs=pl.BlockSpec((block, WIDTH), lambda i, f, p: (begin // block + i, 0)),
+            scratch_shapes=[pltpu.SMEM((1,), jnp.int32)],
+        ),
+        input_output_aliases=aliases,
         compiler_params=pltpu.CompilerParams(
             dimension_semantics=("arbitrary",), vmem_limit_bytes=56 * 1024 * 1024
         ),
         cost_estimate=pl.CostEstimate(flops=rows * 2048, bytes_accessed=rows * 3584, transcendentals=0),
         name="event_rows",
-    )(lengths, place, *shares, g)
+    )(lengths, place, *operands)
 
 
 def spread_kernel(got_ref, out_ref):
@@ -374,42 +389,56 @@
     )(pieces)
 
 
-def weights_kernel(place_ref, mine_ref, other_ref, pw_out, ow_out, bias_out, gain_out):
-    i, k = pl.program_id(0), pl.program_id(1)
-    own = place_ref[1] == i
-
-    def write(ref):
-        values = ref[...].astype(F32) * (1.0 / 32.0)
-        for p in range(4):
-            pw_out[:, p, :] = values[:, p * WIDTH : (p + 1) * WIDTH]
-        ow_out[...] = values[:, 4 * WIDTH : 5 * WIDTH].T
-        for p in range(5 * WIDTH // 128):
-            block, at = divmod(32 * p, values.shape[0])
-
-            @pl.when((i == 0) & (k == block))
-            def _():
-                lanes = slice(p % 2 * 128, p % 2 * 128 + 128)
-                small = values[at : at + 1, 5 * WIDTH :]
-                if p < 8:
-                    bias_out[p // 2 : p // 2 + 1, lanes] = small
-                else:
-                    gain_out[:, lanes] = small
-
-    @pl.when(own)
-    def _():
-        write(mine_ref)
-
-    @pl.when(jnp.logical_not(own))
-    def _():
-        write(other_ref)
-
-
-def weights_out(place, mine, other):
-    half = MODEL // 2
+def weights_kernel(other, place_ref, got_ref, *refs):
+    pw_out, ow_out, bias_out, gain_out = refs[-4:]
+    k = pl.program_id(0)
+    core = place_ref[1]
+    first_half = (1 - core if other else core) == 0
+    values = got_ref[...].astype(F32) * (1.0 / 32.0)
+    for p in range(4):
+        pw_out[:, p, :] = values[:, p * WIDTH : (p + 1) * WIDTH]
+    ow_out[...] = values[:, 4 * WIDTH : 5 * WIDTH].T
+    if other:
+
+        @pl.when(k == 0)
+        def _():
+            bias_out[...] = refs[2][...]
+            gain_out[...] = refs[3][...]
+
+    for p in range(5 * WIDTH // 128):
+        block, at = divmod(32 * p, values.shape[0])
+
+        @pl.when(first_half & (k == block))
+        def _():
+            lanes = slice(p % 2 * 128, p % 2 * 128 + 128)
+            small = values[at : at + 1, 5 * WIDTH :]
+            if p < 8:
+                bias_out[p // 2 : p // 2 + 1, lanes] = small
+            else:
+                gain_out[:, lanes] = small
+
+
+def weights_out(place, got, earlier):
+    other = earlier is not None
     block = 128
-    per = half // block
+    per = got.shape[0] // block
+
+    def half(p):
+        return (1 - p[1] if other else p[1]) * per
+
+    small_specs = [
+        pl.BlockSpec((4, WIDTH), lambda k, p: (0, 0)),
+        pl.BlockSpec((1, WIDTH), lambda k, p: (0, 0)),
+    ]
+    in_specs = [pl.BlockSpec((block, COLUMNS), lambda k, p: (k, 0))]
+    operands = [got]
+    aliases = {}
+    if other:
+        in_specs += [pl.BlockSpec(memory_space=pl.ANY)] * 2 + small_specs
+        operands += list(earlier)
+        aliases = {2: 0, 3: 1}
     return pl.pallas_call(
-        weights_kernel,
+        functools.partial(weights_kernel, other),
         out_shape=[
             jax.ShapeDtypeStruct((MODEL, 4, WIDTH), F32),
             jax.ShapeDtypeStruct((WIDTH, MODEL), F32),
@@ -418,24 +447,21 @@
         ],
         grid_spec=pltpu.PrefetchScalarGridSpec(
             num_scalar_prefetch=1,
-            grid=(2, per),
-            in_specs=[
-                pl.BlockSpec((block, COLUMNS), lambda i, k, c: (k, 0)),
-                pl.BlockSpec((block, COLUMNS), lambda i, k, c: (k, 0)),
-            ],
+            grid=(per,),
+            in_specs=in_specs,
             out_specs=[
-                pl.BlockSpec((block, 4, WIDTH), lambda i, k, c: (i * per + k, 0, 0)),
-                pl.BlockSpec((WIDTH, block), lambda i, k, c: (0, i * per + k)),
-                pl.BlockSpec((4, WIDTH), lambda i, k, c: (0, 0)),
-                pl.BlockSpec((1, WIDTH), lambda i, k, c: (0, 0)),
-            ],
-        ),
+                pl.BlockSpec((block, 4, WIDTH), lambda k, p: (half(p) + k, 0, 0)),
+                pl.BlockSpec((WIDTH, block), lambda k, p: (0, half(p) + k)),
+            ]
+            + small_specs,
+        ),
+        input_output_aliases=aliases,
         compiler_params=pltpu.CompilerParams(
-            dimension_semantics=("arbitrary", "arbitrary"), vmem_limit_bytes=40 * 1024 * 1024
-        ),
-        cost_estimate=pl.CostEstimate(flops=4000000, bytes_accessed=8500000, transcendentals=0),
+            dimension_semantics=("arbitrary",), vmem_limit_bytes=40 * 1024 * 1024
+        ),
+        cost_estimate=pl.CostEstimate(flops=2000000, bytes_accessed=4200000, transcendentals=0),
         name="weights_out",
-    )(place, mine, other)
+    )(place, *operands)
 
 
 def ring(step):
@@ -451,15 +477,27 @@
     swap = [(0, 1), (1, 0)]
     half = MODEL // 2
     other = lax.ppermute(sent, "c", swap)
-    shares = partial_rows(place, grads, weight_in)
+    begins = [sum(ROW_PARTS[:n]) for n in range(len(ROW_PARTS))]
+    one, two, three = (partial_rows(place, grads, weight_in, b, n) for b, n in zip(begins, ROW_PARTS))
+
+    def send(shares):
+        return [shares[0]] + [lax.ppermute(shares[step], "mp", ring(step)) for step in (1, 2, 3)]
+
     kept = (kept + other.astype(F32)).astype(BF16)
-    shares, kept = lax.optimization_barrier((shares, kept))
-    shares = [shares[0]] + [lax.ppermute(shares[step], "mp", ring(step)) for step in (1, 2, 3)]
+    one, two, three, kept = lax.optimization_barrier((one, two, three, kept))
+    one = send(one)
     pieces = lax.all_to_all(kept.reshape(16, half // 16, COLUMNS), ("z", "y"), 0, 0, tiled=True)
-    pieces = lax.all_to_all(spread(pieces), ("z", "y"), 0, 0, tiled=True).reshape(half, COLUMNS)
+    one, two, three, pieces = lax.optimization_barrier((one, two, three, spread(pieces)))
+    two = send(two)
+    pieces = lax.all_to_all(pieces, ("z", "y"), 0, 0, tiled=True).reshape(half, COLUMNS)
+    two, three, pieces = lax.optimization_barrier((two, three, pieces))
+    three = send(three)
+    event_grads = event_rows(lengths, place, one, upstream, begins[0], None)
     other = lax.ppermute(pieces, "c", swap)
-    proj_grad, out_grad, bias_grad, gain_grad = weights_out(place, pieces, other)
-    event_grads = event_rows(lengths, place, shares, upstream)
+    weights = weights_out(place, pieces, None)
+    event_grads = event_rows(lengths, place, two, upstream, begins[1], event_grads)
+    proj_grad, out_grad, bias_grad, gain_grad = weights_out(place, other, weights)
+    event_grads = event_rows(lengths, place, three, upstream, begins[2], event_grads)
     return event_grads, proj_grad, bias_grad, gain_grad.reshape(WIDTH), out_grad
 
 

time: 182 us -> 180 us (0.989)
  blocking collectives: 28.6 us -> 0 us
  Pallas kernels: 74.6 us -> 91.9 us
  starting transfers between devices: 13.5 us -> 29.1 us
  waiting for transfers between devices: 62.8 us -> 53.5 us
    all_to_all x1 -> x0, blocking collectives: 28.6 us -> none  [body(): lax.all_to_all(kept.reshape(16, half // 16, COLUMNS), ('z', 'y'), 0, 0, t...]
    ppermute x3 -> x9, waiting for transfers between devices: 48 us -> 34.8 us  [send(): lax.ppermute(shares[step], 'mp', ring(step))]
    all_to_all x1 -> x2, starting transfers between devices: 3.7 us -> 14.1 us  [the longest x1 7.85 us: body(): lax.all_to_all(kept.reshape(16, half // 16, COLUMNS), ('z', 'y'), 0, 0, t...]
    pallas_call x1 -> x3, Pallas kernels: 12 us -> 20.6 us  [partial_rows(): pl.pallas_call(partial_kernel, out_shape=[jax.ShapeDtypeStruct((rows, WID...]
    pallas_call x2 -> x5, Pallas kernels: 12.5 us -> 21 us  [the longest x3 14.5 us: event_rows(): pl.pallas_call(functools.partial(event_kernel, begin, block), out_shape=j...]
    ppermute x3 -> x9, starting transfers between devices: 4.89 us -> 11.8 us  [send(): lax.ppermute(shares[step], 'mp', ring(step))]
    all_to_all x1 -> x2, waiting for transfers between devices: 14.8 us -> 18.7 us  [the longest x1 18.7 us: body(): lax.all_to_all(kept.reshape(16, half // 16, COLUMNS), ('z', 'y'), 0, 0, t...]
  transfers between devices with their start and end apart: 6 -> 13, of which waited for: 4 -> 6; matrix products, arithmetic and copies ran while one was open for 0% -> 0% of each run, Pallas kernels for 11% -> 22%
where the time goes in v4:
time: 180 us; the launch traced here: 179 us
  Pallas kernels  91.9 us (51%)
  waiting for transfers between devices  53.5 us (30%)
  starting transfers between devices  29.1 us (16%)
  other arithmetic  1.94 us (1%)
    pallas_call x1, Pallas kernels, layer(): pl.pallas_call(functools.partial(layer_kernel, steps), out_shape=[jax.Sha...  48.9 us
    ppermute x9, waiting for transfers between devices, send(): lax.ppermute(shares[step], 'mp', ring(step))  34.8 us
    pallas_call x3, Pallas kernels, partial_rows(): pl.pallas_call(partial_kernel, out_shape=[jax.ShapeDtypeStruct((rows, WID...  20.6 us
    all_to_all x1, waiting for transfers between devices, body(): lax.all_to_all(kept.reshape(16, half // 16, COLUMNS), ('z', 'y'), 0, 0, t...  18.7 us
    pallas_call x3, Pallas kernels, event_rows(): pl.pallas_call(functools.partial(event_kernel, begin, block), out_shape=j...  14.5 us
    ppermute x9, starting transfers between devices, send(): lax.ppermute(shares[step], 'mp', ring(step))  11.8 us
    all_to_all x1, starting transfers between devices, body(): lax.all_to_all(kept.reshape(16, half // 16, COLUMNS), ('z', 'y'), 0, 0, t...  7.85 us
    pallas_call x2, Pallas kernels, weights_out(): pl.pallas_call(functools.partial(weights_kernel, other), out_shape=[jax.S...  6.54 us
  transfers between devices with their start and end apart: 13, of which 6 were waited for; matrix products, arithmetic and copies ran while one was open for 0% of the time, Pallas kernels for 22%

profile of v4, /device:TPU:1, one launch (start us, length us, event | category | flops | bytes accessed | tf_op | source)
XLA Modules:
  0.0 178.8 jit_solution(14557644420251629957)
XLA Ops:
  0.6 0.6 pad_add_fusion.place_ref
  1.2 48.9 %layer.1 = (bf16[3072,1024]{1,0:T(8,128)(2,1)}, bf16[512,1408]{1,0:T(8,128)(2,1)}, f32[512,1408]{1,0:T(8,128)}, bf16[1024,1024]{1,0:T(8,128)(2,1)}) custom-call(s32[32,48]{1,0:T(8,128)} %lengths_ref.7, s32[3]{0:T(128)} %pad_add_fusion.place_ref, bf16[3072,1024]{1,0:T(8,128)(2,1)} %xp_ref.1, bf16[3072,1024]{1,0:T(8,128)(2,1)} %g_ref.7, ...), custom_call_target="tpu_custom_call" | custom-call | flops 18522046464 | bytes 24576000 | tf_op jit(solution)/shard_map/layer/pallas_call | solution.py:239
  50.1 1.4 collective-permute-start
  51.6 5.9 %partial_rows.5 = (f32[768,256]{1,0:T(8,128)}, bf16[768,256]{1,0:T(8,128)(2,1)}, bf16[768,256]{1,0:T(8,128)(2,1)}, bf16[768,256]{1,0:T(8,128)(2,1)}) custom-call(s32[3]{0:T(128)} %pad_add_fusion.place_ref, bf16[3072,1024]{1,0:T(8,128)(2,1)} %get-tuple-element.64.pg_ref, bf16[1024,1024]{1,0:T(8,128)(2,1)} %get-tuple-element.65.w_ref), custom_call_target="tpu_custom_call" | custom-call | flops 1610612736 | bytes 5636096 | tf_op jit(solution)/shard_map/partial_rows/pallas_call | solution.py:310
  57.5 6.7 %partial_rows.4 = (f32[1024,256]{1,0:T(8,128)}, bf16[1024,256]{1,0:T(8,128)(2,1)}, bf16[1024,256]{1,0:T(8,128)(2,1)}, bf16[1024,256]{1,0:T(8,128)(2,1)}) custom-call(s32[3]{0:T(128)} %pad_add_fusion.place_ref, bf16[3072,1024]{1,0:T(8,128)(2,1)} %get-tuple-element.64.pg_ref, bf16[1024,1024]{1,0:T(8,128)(2,1)} %get-tuple-element.65.w_ref), custom_call_target="tpu_custom_call" | custom-call | flops 2147483648 | bytes 6815744 | tf_op jit(solution)/shard_map/partial_rows/pallas_call | solution.py:310
  64.2 0.0 copy-start.2
  64.2 8.0 %partial_rows.3 = (f32[1280,256]{1,0:T(8,128)}, bf16[1280,256]{1,0:T(8,128)(2,1)}, bf16[1280,256]{1,0:T(8,128)(2,1)}, bf16[1280,256]{1,0:T(8,128)(2,1)}) custom-call(s32[3]{0:T(128)} %pad_add_fusion.place_ref, bf16[3072,1024]{1,0:T(8,128)(2,1)} %get-tuple-element.64.pg_ref, bf16[1024,1024]{1,0:T(8,128)(2,1)} %get-tuple-element.65.w_ref), custom_call_target="tpu_custom_call" | custom-call | flops 2684354560 | bytes 7995392 | tf_op jit(solution)/shard_map/partial_rows/pallas_call | solution.py:310
  72.2 0.0 collective-permute-done
  72.2 0.0 copy-done.2
  72.2 1.3 add_convert_fusion
  73.6 7.9 %all-to-all-start = ((bf16[16,32,1408]{2,1,0:T(8,128)(2,1)}), bf16[16,32,1408]{2,1,0:T(8,128)(2,1)S(1)}, u32[]{:S(2)}, u32[]{:S(2)}) async-start(bf16[16,32,1408]{2,1,0:T(8,128)(2,1)} %bitcast.4), calls=%async_computation | async-start | bytes 2883584 | tf_op jit(solution)/shard_map/all_to_all | solution.py:489
  81.4 1.3 collective-permute-start.1
  82.7 2.4 %collective-permute-start.2 = (bf16[1280,256]{1,0:T(8,128)(2,1)}, bf16[1280,256]{1,0:T(8,128)(2,1)S(1)}, u32[]{:S(2)}, u32[]{:S(2)}) collective-permute-start(bf16[1280,256]{1,0:T(8,128)(2,1)} %get-tuple-element.82), channel_id=1, source_target_pairs={{0,2},{1,3},{2,0},{3,1},{4,6},{5,7},{6,4},{7,5},{8,10},{9,11},{10,... | collective-permute-start | bytes 1966088 | tf_op jit(solution)/shard_map/ppermute | solution.py:484
  85.2 1.2 collective-permute-start.3
  86.3 18.7 %all-to-all-done.got_ref = bf16[16,32,1408]{2,1,0:T(8,128)(2,1)S(1)} async-done(((bf16[16,32,1408]{2,1,0:T(8,128)(2,1)}), bf16[16,32,1408]{2,1,0:T(8,128)(2,1)S(1)}, u32[]{:S(2)}, u32[]{:S(2)}) %all-to-all-start) | async-done | bytes 1441824 | tf_op jit(solution)/shard_map/all_to_all | solution.py:489
  105.0 1.3 spread.1
  106.3 0.0 collective-permute-done.1.a_ref
  106.3 0.0 copy-start.3
  106.3 7.7 %collective-permute-done.2.b_ref = bf16[1280,256]{1,0:T(8,128)(2,1)S(1)} collective-permute-done((bf16[1280,256]{1,0:T(8,128)(2,1)}, bf16[1280,256]{1,0:T(8,128)(2,1)S(1)}, u32[]{:S(2)}, u32[]{:S(2)}) %collective-permute-start.2) | collective-permute-done | bytes 655392 | tf_op jit(solution)/shard_map/ppermute | solution.py:484
  114.0 0.0 copy-start.4
  114.0 0.0 collective-permute-done.3.c_ref
  114.0 0.0 copy-start.5
  114.0 6.3 %all-to-all-start.1 = ((bf16[16,32,1408]{2,1,0:T(8,128)(2,1)}), bf16[16,32,1408]{2,1,0:T(8,128)(2,1)S(1)}, u32[]{:S(2)}, u32[]{:S(2)}) async-start(bf16[16,32,1408]{2,1,0:T(8,128)(2,1)} %spread.1), calls=%async_computation.1 | async-start | bytes 2883584 | tf_op jit(solution)/shard_map/all_to_all | solution.py:492
  120.3 1.3 collective-permute-start.4
  121.6 2.9 %collective-permute-start.5 = (bf16[1024,256]{1,0:T(8,128)(2,1)}, bf16[1024,256]{1,0:T(8,128)(2,1)S(1)}, u32[]{:S(2)}, u32[]{:S(2)}) collective-permute-start(bf16[1024,256]{1,0:T(8,128)(2,1)} %get-tuple-element.95), channel_id=1, source_target_pairs={{0,2},{1,3},{2,0},{3,1},{4,6},{5,7},{6,4},{7,5},{8,10},{9,11},{10,... | collective-permute-start | bytes 1572872 | tf_op jit(solution)/shard_map/ppermute | solution.py:484
  124.4 0.1 collective-permute-start.6
  124.5 9.4 %collective-permute-done.4.a_ref = bf16[1024,256]{1,0:T(8,128)(2,1)S(1)} collective-permute-done((bf16[1024,256]{1,0:T(8,128)(2,1)}, bf16[1024,256]{1,0:T(8,128)(2,1)S(1)}, u32[]{:S(2)}, u32[]{:S(2)}) %collective-permute-start.4) | collective-permute-done | bytes 524320 | tf_op jit(solution)/shard_map/ppermute | solution.py:484
  134.0 0.0 copy-start.6
  134.0 13.1 %collective-permute-done.5.b_ref = bf16[1024,256]{1,0:T(8,128)(2,1)S(1)} collective-permute-done((bf16[1024,256]{1,0:T(8,128)(2,1)}, bf16[1024,256]{1,0:T(8,128)(2,1)S(1)}, u32[]{:S(2)}, u32[]{:S(2)}) %collective-permute-start.5) | collective-permute-done | bytes 524320 | tf_op jit(solution)/shard_map/ppermute | solution.py:484
  147.1 0.0 copy-done.6
  147.1 0.0 copy-start.7
  147.1 0.8 copy-done.7
  147.9 0.0 collective-permute-done.6.c_ref
  147.9 0.0 all-to-all-done.1
  147.9 0.0 copy-start
  147.9 1.7 collective-permute-start.10
  149.7 0.0 collective-permute-start.7
  149.7 2.3 %collective-permute-start.8 = (bf16[768,256]{1,0:T(8,128)(2,1)}, bf16[768,256]{1,0:T(8,128)(2,1)S(1)}, u32[]{:S(2)}, u32[]{:S(2)}) collective-permute-start(bf16[768,256]{1,0:T(8,128)(2,1)} %get-tuple-element.104), channel_id=1, source_target_pairs={{0,2},{1,3},{2,0},{3,1},{4,6},{5,7},{6,4},{7,5},{8,10},{9,11},{10,... | collective-permute-start | bytes 1179656 | tf_op jit(solution)/shard_map/ppermute | solution.py:484
  151.9 0.4 collective-permute-start.9
  152.4 0.0 copy-done.3
  152.4 0.0 copy-done.4
  152.4 0.0 copy-done.5
  152.4 5.5 %event_rows.3.refs_0_ = bf16[3072,256]{1,0:T(8,128)(2,1)} custom-call(s32[32,48]{1,0:T(8,128)} %lengths_ref.7, s32[3]{0:T(128)} %pad_add_fusion.place_ref, f32[1280,256]{1,0:T(8,128)} %get-tuple-element.110.own_ref, bf16[1280,256]{1,0:T(8,128)(2,1)} %copy-done.3, bf16[1280,256]{1,0:T(8,128)(2,1)} %copy-done.4, bf16[1280,256]{1,0:T(8,128)(2,1)} %copy-done.5, ...), custom_call_target="tpu_custom_call" | custom-call | flops 2621440 | bytes 4587520 | tf_op jit(solution)/shard_map/event_rows/pallas_call | solution.py:358
  157.9 0.0 copy-done
  157.9 3.3 %weights_out.2 = (f32[1024,4,256]{2,1,0:T(4,128)}, f32[256,1024]{1,0:T(8,128)}, f32[4,256]{1,0:T(4,128)S(1)}, f32[1,256]{1,0:T(1,128)S(1)}) custom-call(s32[3]{0:T(128)S(1)} %copy-done, bf16[512,1408]{1,0:T(8,128)(2,1)S(1)} %bitcast.8), custom_call_target="tpu_custom_call" | custom-call | flops 2000000 | bytes 4200000 | tf_op jit(solution)/shard_map/weights_out/pallas_call | solution.py:440
  161.1 4.8 %event_rows.4.refs_0_ = bf16[3072,256]{1,0:T(8,128)(2,1)} custom-call(s32[32,48]{1,0:T(8,128)} %lengths_ref.7, s32[3]{0:T(128)} %pad_add_fusion.place_ref, f32[1024,256]{1,0:T(8,128)} %get-tuple-element.106.own_ref, bf16[1024,256]{1,0:T(8,128)(2,1)} %copy-done.6, bf16[1024,256]{1,0:T(8,128)(2,1)} %copy-done.7, ...), custom_call_target="tpu_custom_call", output_to_operand_aliasing={{}: (7, {})} | custom-call | flops 2097152 | bytes 3670016 | tf_op jit(solution)/shard_map/event_rows/pallas_call | solution.py:358
  165.9 0.0 copy-start.1
  165.9 0.0 collective-permute-done.7.a_ref
  165.9 0.0 copy-start.8
  165.9 3.9 %collective-permute-done.8.b_ref = bf16[768,256]{1,0:T(8,128)(2,1)S(1)} collective-permute-done((bf16[768,256]{1,0:T(8,128)(2,1)}, bf16[768,256]{1,0:T(8,128)(2,1)S(1)}, u32[]{:S(2)}, u32[]{:S(2)}) %collective-permute-start.8) | collective-permute-done | bytes 393248 | tf_op jit(solution)/shard_map/ppermute | solution.py:484
  169.8 0.0 copy-start.9
  169.8 0.7 collective-permute-done.9.c_ref
  170.5 0.0 copy-done.8
  170.5 0.1 copy-done.9
  170.6 0.0 copy-start.10
  170.6 0.8 copy-done.10
  171.3 4.2 %event_rows.5 = bf16[3072,256]{1,0:T(8,128)(2,1)} custom-call(s32[32,48]{1,0:T(8,128)} %lengths_ref.7, s32[3]{0:T(128)} %pad_add_fusion.place_ref, f32[768,256]{1,0:T(8,128)} %get-tuple-element.102.own_ref, bf16[768,256]{1,0:T(8,128)(2,1)} %copy-done.8, bf16[768,256]{1,0:T(8,128)(2,1)} %copy-done.9, ...), custom_call_target="tpu_custom_call", output_to_operand_aliasing={{}: (7, {})} | custom-call | flops 1572864 | bytes 2752512 | tf_op jit(solution)/shard_map/event_rows/pallas_call | solution.py:358
  175.5 0.0 collective-permute-done.10.got_ref
  175.5 0.0 copy-done.1
  175.5 3.3 %weights_out.3 = (f32[1024,4,256]{2,1,0:T(4,128)}, f32[256,1024]{1,0:T(8,128)}, f32[4,256]{1,0:T(4,128)}, f32[1,256]{1,0:T(1,128)}) custom-call(s32[3]{0:T(128)S(1)} %copy-done.1, bf16[512,1408]{1,0:T(8,128)(2,1)S(1)} %collective-permute-done.10.got_ref, f32[1024,4,256]{2,1,0:T(4,128)} %get-tuple-element.115.refs_0_, ...), custom_call_target="tpu_custom_call", output_to_operand_aliasing={{0}: (2, {}), {1}: (3, {})} | custom-call | flops 2000000 | bytes 4200000 | tf_op jit(solution)/shard_map/weights_out/pallas_call | solution.py:440
Async XLA Ops:
  50.1 22.1 %collective-permute-start = (bf16[512,1408]{1,0:T(8,128)(2,1)}, bf16[512,1408]{1,0:T(8,128)(2,1)S(1)}, u32[]{:S(2)}, u32[]{:S(2)}) collective-permute-start(bf16[512,1408]{1,0:T(8,128)(2,1)} %get-tuple-element.79), channel_id=1, source_target_pairs={{0,4},{4,0},{1,5},{5,1},{2,6},{6,2},{3,7},{7,3},{8,12},{12,8},{9,1... | collective-permute-start | bytes 4325384 | tf_op jit(solution)/shard_map/ppermute | solution.py:479
  64.2 8.0 %copy-start.2 = (f32[512,1408]{1,0:T(8,128)S(1)}, f32[512,1408]{1,0:T(8,128)}, u32[]{:S(2)}) copy-start(f32[512,1408]{1,0:T(8,128)} %get-tuple-element.78) | copy-start | bytes 8650756
  73.6 31.4 %all-to-all-start = ((bf16[16,32,1408]{2,1,0:T(8,128)(2,1)}), bf16[16,32,1408]{2,1,0:T(8,128)(2,1)S(1)}, u32[]{:S(2)}, u32[]{:S(2)}) async-start(bf16[16,32,1408]{2,1,0:T(8,128)(2,1)} %bitcast.4), calls=%async_computation | async-start | bytes 2883584 | tf_op jit(solution)/shard_map/all_to_all | solution.py:489
  81.4 24.9 %collective-permute-start.1 = (bf16[1280,256]{1,0:T(8,128)(2,1)}, bf16[1280,256]{1,0:T(8,128)(2,1)S(1)}, u32[]{:S(2)}, u32[]{:S(2)}) collective-permute-start(bf16[1280,256]{1,0:T(8,128)(2,1)} %get-tuple-element.81), channel_id=1, source_target_pairs={{0,1},{1,2},{2,3},{3,0},{4,5},{5,6},{6,7},{7,4},{8,9},{9,10},{10,1... | collective-permute-start | bytes 1966088 | tf_op jit(solution)/shard_map/ppermute | solution.py:484
  82.7 31.3 %collective-permute-start.2 = (bf16[1280,256]{1,0:T(8,128)(2,1)}, bf16[1280,256]{1,0:T(8,128)(2,1)S(1)}, u32[]{:S(2)}, u32[]{:S(2)}) collective-permute-start(bf16[1280,256]{1,0:T(8,128)(2,1)} %get-tuple-element.82), channel_id=1, source_target_pairs={{0,2},{1,3},{2,0},{3,1},{4,6},{5,7},{6,4},{7,5},{8,10},{9,11},{10,... | collective-permute-start | bytes 1966088 | tf_op jit(solution)/shard_map/ppermute | solution.py:484
  85.2 28.8 %collective-permute-start.3 = (bf16[1280,256]{1,0:T(8,128)(2,1)}, bf16[1280,256]{1,0:T(8,128)(2,1)S(1)}, u32[]{:S(2)}, u32[]{:S(2)}) collective-permute-start(bf16[1280,256]{1,0:T(8,128)(2,1)} %get-tuple-element.83), channel_id=1, source_target_pairs={{0,3},{1,0},{2,1},{3,2},{4,7},{5,4},{6,5},{7,6},{8,11},{9,8},{10,9... | collective-permute-start | bytes 1966088 | tf_op jit(solution)/shard_map/ppermute | solution.py:484
  106.3 46.1 %copy-start.3 = (bf16[1280,256]{1,0:T(8,128)(2,1)}, bf16[1280,256]{1,0:T(8,128)(2,1)S(1)}, u32[]{:S(2)}) copy-start(bf16[1280,256]{1,0:T(8,128)(2,1)S(1)} %collective-permute-done.1.a_ref) | copy-start | bytes 1966084
  114.0 38.4 %copy-start.4 = (bf16[1280,256]{1,0:T(8,128)(2,1)}, bf16[1280,256]{1,0:T(8,128)(2,1)S(1)}, u32[]{:S(2)}) copy-start(bf16[1280,256]{1,0:T(8,128)(2,1)S(1)} %collective-permute-done.2.b_ref) | copy-start | bytes 1966084
  114.0 38.4 %copy-start.5 = (bf16[1280,256]{1,0:T(8,128)(2,1)}, bf16[1280,256]{1,0:T(8,128)(2,1)S(1)}, u32[]{:S(2)}) copy-start(bf16[1280,256]{1,0:T(8,128)(2,1)S(1)} %collective-permute-done.3.c_ref) | copy-start | bytes 1966084
  114.0 33.9 %all-to-all-start.1 = ((bf16[16,32,1408]{2,1,0:T(8,128)(2,1)}), bf16[16,32,1408]{2,1,0:T(8,128)(2,1)S(1)}, u32[]{:S(2)}, u32[]{:S(2)}) async-start(bf16[16,32,1408]{2,1,0:T(8,128)(2,1)} %spread.1), calls=%async_computation.1 | async-start | bytes 2883584 | tf_op jit(solution)/shard_map/all_to_all | solution.py:492
  120.3 13.7 %collective-permute-start.4 = (bf16[1024,256]{1,0:T(8,128)(2,1)}, bf16[1024,256]{1,0:T(8,128)(2,1)S(1)}, u32[]{:S(2)}, u32[]{:S(2)}) collective-permute-start(bf16[1024,256]{1,0:T(8,128)(2,1)} %get-tuple-element.94), channel_id=1, source_target_pairs={{0,1},{1,2},{2,3},{3,0},{4,5},{5,6},{6,7},{7,4},{8,9},{9,10},{10,1... | collective-permute-start | bytes 1572872 | tf_op jit(solution)/shard_map/ppermute | solution.py:484
  121.6 25.5 %collective-permute-start.5 = (bf16[1024,256]{1,0:T(8,128)(2,1)}, bf16[1024,256]{1,0:T(8,128)(2,1)S(1)}, u32[]{:S(2)}, u32[]{:S(2)}) collective-permute-start(bf16[1024,256]{1,0:T(8,128)(2,1)} %get-tuple-element.95), channel_id=1, source_target_pairs={{0,2},{1,3},{2,0},{3,1},{4,6},{5,7},{6,4},{7,5},{8,10},{9,11},{10,... | collective-permute-start | bytes 1572872 | tf_op jit(solution)/shard_map/ppermute | solution.py:484
  124.4 23.5 %collective-permute-start.6 = (bf16[1024,256]{1,0:T(8,128)(2,1)}, bf16[1024,256]{1,0:T(8,128)(2,1)}, u32[]{:S(2)}, u32[]{:S(2)}) collective-permute-start(bf16[1024,256]{1,0:T(8,128)(2,1)} %get-tuple-element.96), channel_id=1, source_target_pairs={{0,3},{1,0},{2,1},{3,2},{4,7},{5,4},{6,5},{7,6},{8,11},{9,8},{10,9... | collective-permute-start | bytes 1572872 | tf_op jit(solution)/shard_map/ppermute | solution.py:484
  134.0 13.2 %copy-start.6 = (bf16[1024,256]{1,0:T(8,128)(2,1)}, bf16[1024,256]{1,0:T(8,128)(2,1)S(1)}, u32[]{:S(2)}) copy-start(bf16[1024,256]{1,0:T(8,128)(2,1)S(1)} %collective-permute-done.4.a_ref) | copy-start | bytes 1572868
  147.1 0.8 copy-start.7
  147.9 10.0 %copy-start = (s32[3]{0:T(128)S(1)}, s32[3]{0:T(128)}, u32[]{:S(2)}) copy-start(s32[3]{0:T(128)} %pad_add_fusion.place_ref) | copy-start | bytes 40
  147.9 27.6 %collective-permute-start.10 = (bf16[512,1408]{1,0:T(8,128)(2,1)S(1)}, bf16[512,1408]{1,0:T(8,128)(2,1)S(1)}, u32[]{:S(2)}, u32[]{:S(2)}) collective-permute-start(bf16[512,1408]{1,0:T(8,128)(2,1)S(1)} %bitcast.7), channel_id=1, source_target_pairs={{0,4},{4,0},{1,5},{5,1},{2,6},{6,2},{3,7},{7,3},{8,12},{12,8},{9,1... | collective-permute-start | bytes 4325384 | tf_op jit(solution)/shard_map/ppermute | solution.py:496
  149.7 16.3 %collective-permute-start.7 = (bf16[768,256]{1,0:T(8,128)(2,1)}, bf16[768,256]{1,0:T(8,128)(2,1)S(1)}, u32[]{:S(2)}, u32[]{:S(2)}) collective-permute-start(bf16[768,256]{1,0:T(8,128)(2,1)} %get-tuple-element.103), channel_id=1, source_target_pairs={{0,1},{1,2},{2,3},{3,0},{4,5},{5,6},{6,7},{7,4},{8,9},{9,10},{10,1... | collective-permute-start | bytes 1179656 | tf_op jit(solution)/shard_map/ppermute | solution.py:484
  149.7 20.1 %collective-permute-start.8 = (bf16[768,256]{1,0:T(8,128)(2,1)}, bf16[768,256]{1,0:T(8,128)(2,1)S(1)}, u32[]{:S(2)}, u32[]{:S(2)}) collective-permute-start(bf16[768,256]{1,0:T(8,128)(2,1)} %get-tuple-element.104), channel_id=1, source_target_pairs={{0,2},{1,3},{2,0},{3,1},{4,6},{5,7},{6,4},{7,5},{8,10},{9,11},{10,... | collective-permute-start | bytes 1179656 | tf_op jit(solution)/shard_map/ppermute | solution.py:484
  151.9 18.6 %collective-permute-start.9 = (bf16[768,256]{1,0:T(8,128)(2,1)}, bf16[768,256]{1,0:T(8,128)(2,1)S(1)}, u32[]{:S(2)}, u32[]{:S(2)}) collective-permute-start(bf16[768,256]{1,0:T(8,128)(2,1)} %get-tuple-element.105), channel_id=1, source_target_pairs={{0,3},{1,0},{2,1},{3,2},{4,7},{5,4},{6,5},{7,6},{8,11},{9,8},{10,9... | collective-permute-start | bytes 1179656 | tf_op jit(solution)/shard_map/ppermute | solution.py:484
  165.9 9.6 %copy-start.1 = (s32[3]{0:T(128)S(1)}, s32[3]{0:T(128)}, u32[]{:S(2)}) copy-start(s32[3]{0:T(128)} %pad_add_fusion.place_ref) | copy-start | bytes 40
  165.9 4.6 %copy-start.8 = (bf16[768,256]{1,0:T(8,128)(2,1)}, bf16[768,256]{1,0:T(8,128)(2,1)S(1)}, u32[]{:S(2)}) copy-start(bf16[768,256]{1,0:T(8,128)(2,1)S(1)} %collective-permute-done.7.a_ref) | copy-start | bytes 1179652
  169.8 0.7 copy-start.9
  170.6 0.8 copy-start.10

commit v5 on v4

--- a/solution.py
+++ b/solution.py
@@ -19,7 +19,6 @@
 COLUMNS = 5 * WIDTH + 128
 PIECES = 8
 HISTORY = 3
-ROW_PARTS = (1280, 1024, 768)
 F32 = jnp.float32
 BF16 = jnp.bfloat16
 NT = (((1,), (1,)), ((), ()))
@@ -290,88 +289,65 @@
     )(lengths, place, x, g, x, w, wo, bias, gain)
 
 
-def partial_kernel(place_ref, pg_ref, w_ref, own_out, ahead_out, across_out, behind_out):
+def partial_kernel(pg_ref, w_ref, out_ref):
     grads = pg_ref[...]
-    me = place_ref[2]
-
-    def share(shift):
-        start = pl.multiple_of(lax.rem(me + shift, 4) * WIDTH, WIDTH)
-        return dot(grads, w_ref[pl.ds(start, WIDTH), :], NT)
-
-    ahead_out[...] = share(1).astype(BF16)
-    across_out[...] = share(2).astype(BF16)
-    behind_out[...] = share(3).astype(BF16)
-    own_out[...] = share(0)
-
-
-def partial_rows(place, grads, w, begin, rows):
-    block = 256
-    wide = pl.BlockSpec((block, WIDTH), lambda i, p: (i, 0))
+    for d in range(4):
+        cols = slice(d * WIDTH, (d + 1) * WIDTH)
+        out_ref[:, cols] = dot(grads, w_ref[cols, :], NT).astype(BF16)
+
+
+def partial_rows(grads, w):
+    block = 512
+    rows = grads.shape[0]
+    wide = pl.BlockSpec((block, MODEL), lambda i: (i, 0))
     return pl.pallas_call(
         partial_kernel,
-        out_shape=[jax.ShapeDtypeStruct((rows, WIDTH), F32)] + [jax.ShapeDtypeStruct((rows, WIDTH), BF16)] * 3,
-        grid_spec=pltpu.PrefetchScalarGridSpec(
-            num_scalar_prefetch=1,
-            grid=(rows // block,),
-            in_specs=[
-                pl.BlockSpec((block, MODEL), lambda i, p: (begin // block + i, 0)),
-                pl.BlockSpec(w.shape, lambda i, p: (0, 0)),
-            ],
-            out_specs=[wide, wide, wide, wide],
-        ),
+        out_shape=jax.ShapeDtypeStruct((rows, MODEL), BF16),
+        grid=(rows // block,),
+        in_specs=[wide, pl.BlockSpec(w.shape, lambda i: (0, 0))],
+        out_specs=wide,
         compiler_params=pltpu.CompilerParams(
             dimension_semantics=("arbitrary",), vmem_limit_bytes=56 * 1024 * 1024
         ),
         cost_estimate=pl.CostEstimate(
-            flops=2 * rows * MODEL * MODEL, bytes_accessed=rows * 4608 + w.size * 2, transcendentals=0
+            flops=2 * rows * MODEL * MODEL, bytes_accessed=rows * 4096 + w.size * 2, transcendentals=0
         ),
         name="partial_rows",
-    )(place, grads, w)
-
-
-def event_kernel(begin, block, lengths_ref, place_ref, own_ref, a_ref, b_ref, c_ref, g_ref, *refs):
-    out_ref, tiles_ref = refs[-2:]
+    )(grads, w)
+
+
+def event_kernel(block, lengths_ref, place_ref, got_ref, g_ref, out_ref, tiles_ref):
     home = place_ref[0]
 
     @pl.when(pl.program_id(0) == 0)
     def _():
         tiles_ref[0] = lax.fori_loop(0, lengths_ref.shape[1], lambda u, t: t + lengths_ref[home, u], jnp.int32(0))
 
-    row = lax.broadcasted_iota(jnp.int32, (block, WIDTH), 0) + begin + pl.program_id(0) * block
-    base = own_ref[...] + jnp.where(row < tiles_ref[0] * TILE, g_ref[...].astype(F32), 0.0)
-    got = a_ref[...].astype(F32) + b_ref[...].astype(F32) + c_ref[...].astype(F32)
-    out_ref[...] = (base + got).astype(BF16)
-
-
-def event_rows(lengths, place, shares, g, begin, out):
-    block = 256
-    rows = shares[0].shape[0]
+    row = lax.broadcasted_iota(jnp.int32, (block, WIDTH), 0) + pl.program_id(0) * block
+    g = jnp.where(row < tiles_ref[0] * TILE, g_ref[...].astype(F32), 0.0)
+    out_ref[...] = (got_ref[...].astype(F32) + g).astype(BF16)
+
+
+def event_rows(lengths, place, got, g):
+    block = 768
+    rows = g.shape[0]
     wide = pl.BlockSpec((block, WIDTH), lambda i, f, p: (i, 0))
-    in_specs = [wide, wide, wide, wide]
-    in_specs.append(pl.BlockSpec((block, WIDTH), lambda i, f, p: (begin // block + i, p[2])))
-    operands = list(shares) + [g]
-    aliases = {}
-    if out is not None:
-        in_specs.append(pl.BlockSpec(memory_space=pl.ANY))
-        operands.append(out)
-        aliases = {7: 0}
     return pl.pallas_call(
-        functools.partial(event_kernel, begin, block),
-        out_shape=jax.ShapeDtypeStruct((g.shape[0], WIDTH), BF16),
+        functools.partial(event_kernel, block),
+        out_shape=jax.ShapeDtypeStruct((rows, WIDTH), BF16),
         grid_spec=pltpu.PrefetchScalarGridSpec(
             num_scalar_prefetch=2,
             grid=(rows // block,),
-            in_specs=in_specs,
-            out_specs=pl.BlockSpec((block, WIDTH), lambda i, f, p: (begin // block + i, 0)),
+            in_specs=[wide, pl.BlockSpec((block, WIDTH), lambda i, f, p: (i, p[2]))],
+            out_specs=wide,
             scratch_shapes=[pltpu.SMEM((1,), jnp.int32)],
         ),
-        input_output_aliases=aliases,
         compiler_params=pltpu.CompilerParams(
             dimension_semantics=("arbitrary",), vmem_limit_bytes=56 * 1024 * 1024
         ),
-        cost_estimate=pl.CostEstimate(flops=rows * 2048, bytes_accessed=rows * 3584, transcendentals=0),
+        cost_estimate=pl.CostEstimate(flops=rows * 1024, bytes_accessed=rows * 1536, transcendentals=0),
         name="event_rows",
-    )(lengths, place, *operands)
+    )(lengths, place, got, g)
 
 
 def spread_kernel(got_ref, out_ref):
@@ -464,10 +440,6 @@
     )(place, *operands)
 
 
-def ring(step):
-    return [(i, (i + step) % 4) for i in range(4)]
-
-
 def body(events, upstream, proj_weight, proj_bias, norm_gain, out_weight, lengths, owners):
     rows = events.shape[0]
     place = jnp.stack([lax.axis_index(DP), lax.axis_index("c"), lax.axis_index("mp")]).astype(jnp.int32)
@@ -477,27 +449,15 @@
     swap = [(0, 1), (1, 0)]
     half = MODEL // 2
     other = lax.ppermute(sent, "c", swap)
-    begins = [sum(ROW_PARTS[:n]) for n in range(len(ROW_PARTS))]
-    one, two, three = (partial_rows(place, grads, weight_in, b, n) for b, n in zip(begins, ROW_PARTS))
-
-    def send(shares):
-        return [shares[0]] + [lax.ppermute(shares[step], "mp", ring(step)) for step in (1, 2, 3)]
-
+    shares = partial_rows(grads, weight_in)
     kept = (kept + other.astype(F32)).astype(BF16)
-    one, two, three, kept = lax.optimization_barrier((one, two, three, kept))
-    one = send(one)
+    got = lax.psum_scatter(shares, "mp", scatter_dimension=1, tiled=True)
     pieces = lax.all_to_all(kept.reshape(16, half // 16, COLUMNS), ("z", "y"), 0, 0, tiled=True)
-    one, two, three, pieces = lax.optimization_barrier((one, two, three, spread(pieces)))
-    two = send(two)
-    pieces = lax.all_to_all(pieces, ("z", "y"), 0, 0, tiled=True).reshape(half, COLUMNS)
-    two, three, pieces = lax.optimization_barrier((two, three, pieces))
-    three = send(three)
-    event_grads = event_rows(lengths, place, one, upstream, begins[0], None)
+    pieces = lax.all_to_all(spread(pieces), ("z", "y"), 0, 0, tiled=True).reshape(half, COLUMNS)
     other = lax.ppermute(pieces, "c", swap)
     weights = weights_out(place, pieces, None)
-    event_grads = event_rows(lengths, place, two, upstream, begins[1], event_grads)
     proj_grad, out_grad, bias_grad, gain_grad = weights_out(place, other, weights)
-    event_grads = event_rows(lengths, place, three, upstream, begins[2], event_grads)
+    event_grads = event_rows(lengths, place, got, upstream)
     return event_grads, proj_grad, bias_grad, gain_grad.reshape(WIDTH), out_grad
 
 

time: 180 us -> 148 us (0.82)
  blocking collectives: 0 us -> 52.1 us
  waiting for transfers between devices: 53.5 us -> 4.77 us
  starting transfers between devices: 29.1 us -> 3.43 us
  Pallas kernels: 91.9 us -> 72.1 us
  between operations: 0.72 us -> 14.1 us
    all_to_all x0 -> x2, blocking collectives: none -> 52.1 us  [the longest x1 28.4 us: body(): lax.all_to_all(kept.reshape(16, half // 16, COLUMNS), ('z', 'y'), 0, 0, t...]
    ppermute x9 -> x0, waiting for transfers between devices: 34.8 us -> none  [send(): lax.ppermute(shares[step], 'mp', ring(step))]
    all_to_all x2 -> x0, waiting for transfers between devices: 18.7 us -> none  [the longest x1 18.7 us: body(): lax.all_to_all(kept.reshape(16, half // 16, COLUMNS), ('z', 'y'), 0, 0, t...]
    pallas_call x6 -> x2, Pallas kernels: 35.1 us -> 16.5 us  [the longest x1 11.5 us: partial_rows(): pl.pallas_call(partial_kernel, out_shape=jax.ShapeDtypeStruct((rows, MODE...]
    all_to_all x2 -> x0, starting transfers between devices: 14.1 us -> none  [the longest x1 7.85 us: body(): lax.all_to_all(kept.reshape(16, half // 16, COLUMNS), ('z', 'y'), 0, 0, t...]
    ppermute x9 -> x0, starting transfers between devices: 11.8 us -> none  [send(): lax.ppermute(shares[step], 'mp', ring(step))]
    ppermute x1, waiting for transfers between devices: 0.01 us -> 3.06 us  [body(): other = lax.ppermute(sent, 'c', swap)]
  transfers between devices with their start and end apart: 13 -> 3, of which waited for: 6 -> 2; matrix products, arithmetic and copies ran while one was open for 0% -> 0% of each run, Pallas kernels for 22% -> 5%
where the time goes in v5:
time: 148 us; the launch traced here: 147 us
  Pallas kernels  72.1 us (49%)
  blocking collectives  52.1 us (35%)
  between operations  14.1 us (10%)
  waiting for transfers between devices  4.77 us (3%)
  starting transfers between devices  3.43 us (2%)
    pallas_call x1, Pallas kernels, layer(): pl.pallas_call(functools.partial(layer_kernel, steps), out_shape=[jax.Sha...  48.8 us
    all_to_all x1, blocking collectives, body(): lax.all_to_all(kept.reshape(16, half // 16, COLUMNS), ('z', 'y'), 0, 0, t...  28.4 us
    all_to_all x1, blocking collectives, body(): lax.all_to_all(spread(pieces), ('z', 'y'), 0, 0, tiled=True)  23.6 us
    pallas_call x1, Pallas kernels, partial_rows(): pl.pallas_call(partial_kernel, out_shape=jax.ShapeDtypeStruct((rows, MODE...  11.5 us
    pallas_call x2, Pallas kernels, weights_out(): pl.pallas_call(functools.partial(weights_kernel, other), out_shape=[jax.S...  6.54 us
    pallas_call x1, Pallas kernels, event_rows(): pl.pallas_call(functools.partial(event_kernel, block), out_shape=jax.Shap...  5.03 us
    ppermute x1, waiting for transfers between devices, body(): other = lax.ppermute(sent, 'c', swap)  3.06 us
  transfers between devices with their start and end apart: 3, of which 2 were waited for; matrix products, arithmetic and copies ran while one was open for 0% of the time, Pallas kernels for 5%

profile of v5, /device:TPU:1, one launch (start us, length us, event | category | flops | bytes accessed | tf_op | source)
XLA Modules:
  0.0 147.4 jit_solution(5735850997630398148)
XLA Ops:
  7.2 0.0 reduce-scatter.2.cloned.1.call-start
  7.2 0.6 pad_add_fusion.place_ref
  7.8 48.8 %layer.1 = (bf16[3072,1024]{1,0:T(8,128)(2,1)}, bf16[512,1408]{1,0:T(8,128)(2,1)}, f32[512,1408]{1,0:T(8,128)}, bf16[1024,1024]{1,0:T(8,128)(2,1)}) custom-call(s32[32,48]{1,0:T(8,128)} %lengths_ref.3, s32[3]{0:T(128)} %pad_add_fusion.place_ref, bf16[3072,1024]{1,0:T(8,128)(2,1)} %xp_ref.1, bf16[3072,1024]{1,0:T(8,128)(2,1)} %g_ref.3, ...), custom_call_target="tpu_custom_call" | custom-call | flops 18522046464 | bytes 24576000 | tf_op jit(solution)/shard_map/layer/pallas_call | solution.py:238
  56.7 11.5 %partial_rows.1 = bf16[3072,1024]{1,0:T(8,128)(2,1)} custom-call(bf16[3072,1024]{1,0:T(8,128)(2,1)} %get-tuple-element.17.pg_ref, bf16[1024,1024]{1,0:T(8,128)(2,1)} %get-tuple-element.18.w_ref), custom_call_target="tpu_custom_call" | custom-call | flops 6442450944 | bytes 14680064 | tf_op jit(solution)/shard_map/partial_rows/pallas_call | solution.py:303
  68.1 0.0 copy-start.1
  68.1 0.0 reduce-scatter.2.cloned.1.call-update
  68.2 1.5 %collective-permute-start = (bf16[512,1408]{1,0:T(8,128)(2,1)}, bf16[512,1408]{1,0:T(8,128)(2,1)S(1)}, u32[]{:S(2)}, u32[]{:S(2)}) collective-permute-start(bf16[512,1408]{1,0:T(8,128)(2,1)} %get-tuple-element.20), channel_id=1, source_target_pairs={{0,4},{4,0},{1,5},{5,1},{2,6},{6,2},{3,7},{7,3},{8,12},{12,8},{9,1... | collective-permute-start | bytes 4325384 | tf_op jit(solution)/shard_map/ppermute | solution.py:451
  69.7 3.1 %collective-permute-done = bf16[512,1408]{1,0:T(8,128)(2,1)S(1)} collective-permute-done((bf16[512,1408]{1,0:T(8,128)(2,1)}, bf16[512,1408]{1,0:T(8,128)(2,1)S(1)}, u32[]{:S(2)}, u32[]{:S(2)}) %collective-permute-start) | collective-permute-done | bytes 1441824 | tf_op jit(solution)/shard_map/ppermute | solution.py:451
  72.7 0.0 copy-done.1
  72.7 0.4 add_convert_fusion
  73.1 28.4 %all_to_all.10.got_ref = bf16[16,32,1408]{2,1,0:T(8,128)(2,1)S(1)} all-to-all(bf16[16,32,1408]{2,1,0:T(8,128)(2,1)S(1)} %bitcast.9), channel_id=1, replica_groups=mesh['z'=4,'y'=4,'c'=2,'mp'=4] {'z','y'}, dimensions={0} | all-to-all | bytes 2883584 | tf_op jit(solution)/shard_map/all_to_all | solution.py:455
  101.5 0.2 spread.1
  101.7 0.0 copy-start
  101.7 23.6 %all_to_all.11 = bf16[16,32,1408]{2,1,0:T(8,128)(2,1)S(1)} all-to-all(bf16[16,32,1408]{2,1,0:T(8,128)(2,1)S(1)} %spread.1), channel_id=1, replica_groups=mesh['z'=4,'y'=4,'c'=2,'mp'=4] {'z','y'}, dimensions={0} | all-to-all | bytes 2883584 | tf_op jit(solution)/shard_map/all_to_all | solution.py:456
  125.4 1.9 %collective-permute-start.1 = (bf16[512,1408]{1,0:T(8,128)(2,1)S(1)}, bf16[512,1408]{1,0:T(8,128)(2,1)S(1)}, u32[]{:S(2)}, u32[]{:S(2)}) collective-permute-start(bf16[512,1408]{1,0:T(8,128)(2,1)S(1)} %bitcast.7), channel_id=1, source_target_pairs={{0,4},{4,0},{1,5},{5,1},{2,6},{6,2},{3,7},{7,3},{8,12},{12,8},{9,1... | collective-permute-start | bytes 4325384 | tf_op jit(solution)/shard_map/ppermute | solution.py:457
  127.3 0.0 copy-done
  127.3 3.3 %weights_out.2 = (f32[1024,4,256]{2,1,0:T(4,128)}, f32[256,1024]{1,0:T(8,128)}, f32[4,256]{1,0:T(4,128)S(1)}, f32[1,256]{1,0:T(1,128)S(1)}) custom-call(s32[3]{0:T(128)S(1)} %copy-done, bf16[512,1408]{1,0:T(8,128)(2,1)S(1)} %bitcast.8), custom_call_target="tpu_custom_call" | custom-call | flops 2000000 | bytes 4200000 | tf_op jit(solution)/shard_map/weights_out/pallas_call | solution.py:416
  130.5 0.0 collective-permute-done.1.got_ref
  130.5 3.3 %weights_out.3 = (f32[1024,4,256]{2,1,0:T(4,128)}, f32[256,1024]{1,0:T(8,128)}, f32[4,256]{1,0:T(4,128)}, f32[1,256]{1,0:T(1,128)}) custom-call(s32[3]{0:T(128)S(1)} %copy-done, bf16[512,1408]{1,0:T(8,128)(2,1)S(1)} %collective-permute-done.1.got_ref, f32[1024,4,256]{2,1,0:T(4,128)} %get-tuple-element.21.refs_0_, ...), custom_call_target="tpu_custom_call", output_to_operand_aliasing={{0}: (2, {}), {1}: (3, {})} | custom-call | flops 2000000 | bytes 4200000 | tf_op jit(solution)/shard_map/weights_out/pallas_call | solution.py:416
  133.8 1.7 %reduce-scatter.2.cloned.1.call-done.got_ref = bf16[3072,256]{1,0:T(8,128)(2,1)} async-done(((bf16[3072,1024]{1,0:T(8,128)(2,1)}), bf16[3072,256]{1,0:T(8,128)(2,1)}) %reduce-scatter.2.cloned.1.call-update) | async-done | bytes 1572880 | tf_op jit(solution)/shard_map/reduce_scatter | solution.py:454
  135.5 5.0 %event_rows.1 = bf16[3072,256]{1,0:T(8,128)(2,1)} custom-call(s32[32,48]{1,0:T(8,128)} %lengths_ref.3, s32[3]{0:T(128)} %pad_add_fusion.place_ref, bf16[3072,256]{1,0:T(8,128)(2,1)} %reduce-scatter.2.cloned.1.call-done.got_ref, bf16[3072,1024]{1,0:T(8,128)(2,1)} %g_ref.3), custom_call_target="tpu_custom_call" | custom-call | flops 3145728 | bytes 4718592 | tf_op jit(solution)/shard_map/event_rows/pallas_call | solution.py:335
Async XLA Ops:
  7.2 128.3 %reduce-scatter.2.cloned.1.call-start = ((), (), s32[]{:S(2)}) async-start(), calls=%async_computation.3 | async-start | bytes 7864320 | tf_op jit(solution)/shard_map/reduce_scatter | solution.py:454
  68.1 4.6 %copy-start.1 = (f32[512,1408]{1,0:T(8,128)S(1)}, f32[512,1408]{1,0:T(8,128)}, u32[]{:S(2)}) copy-start(f32[512,1408]{1,0:T(8,128)} %get-tuple-element.19) | copy-start | bytes 8650756
  68.2 4.6 %collective-permute-start = (bf16[512,1408]{1,0:T(8,128)(2,1)}, bf16[512,1408]{1,0:T(8,128)(2,1)S(1)}, u32[]{:S(2)}, u32[]{:S(2)}) collective-permute-start(bf16[512,1408]{1,0:T(8,128)(2,1)} %get-tuple-element.20), channel_id=1, source_target_pairs={{0,4},{4,0},{1,5},{5,1},{2,6},{6,2},{3,7},{7,3},{8,12},{12,8},{9,1... | collective-permute-start | bytes 4325384 | tf_op jit(solution)/shard_map/ppermute | solution.py:451
  101.7 25.5 %copy-start = (s32[3]{0:T(128)S(1)}, s32[3]{0:T(128)}, u32[]{:S(2)}) copy-start(s32[3]{0:T(128)} %pad_add_fusion.place_ref) | copy-start | bytes 40
  125.4 5.1 %collective-permute-start.1 = (bf16[512,1408]{1,0:T(8,128)(2,1)S(1)}, bf16[512,1408]{1,0:T(8,128)(2,1)S(1)}, u32[]{:S(2)}, u32[]{:S(2)}) collective-permute-start(bf16[512,1408]{1,0:T(8,128)(2,1)S(1)} %bitcast.7), channel_id=1, source_target_pairs={{0,4},{4,0},{1,5},{5,1},{2,6},{6,2},{3,7},{7,3},{8,12},{12,8},{9,1... | collective-permute-start | bytes 4325384 | tf_op jit(solution)/shard_map/ppermute | solution.py:457
Sparse Core Ops, SparseCore 0:
  68.3 67.1 reduce-scatter.1

commit v6 on v5

--- a/solution.py
+++ b/solution.py
@@ -289,65 +289,47 @@
     )(lengths, place, x, g, x, w, wo, bias, gain)
 
 
-def partial_kernel(pg_ref, w_ref, out_ref):
+def partial_kernel(block, lengths_ref, place_ref, pg_ref, w_ref, g_ref, out_ref, tiles_ref):
+    home, me = place_ref[0], place_ref[2]
+
+    @pl.when(pl.program_id(0) == 0)
+    def _():
+        tiles_ref[0] = lax.fori_loop(0, lengths_ref.shape[1], lambda u, t: t + lengths_ref[home, u], jnp.int32(0))
+
+    row = lax.broadcasted_iota(jnp.int32, (block, WIDTH), 0) + pl.program_id(0) * block
     grads = pg_ref[...]
     for d in range(4):
         cols = slice(d * WIDTH, (d + 1) * WIDTH)
-        out_ref[:, cols] = dot(grads, w_ref[cols, :], NT).astype(BF16)
-
-
-def partial_rows(grads, w):
-    block = 512
+        g = jnp.where(row < jnp.where(me == d, tiles_ref[0] * TILE, 0), g_ref[...].astype(F32), 0.0)
+        out_ref[:, cols] = (dot(grads, w_ref[cols, :], NT) + g).astype(BF16)
+
+
+def partial_rows(lengths, place, grads, w, g):
+    block = 1024
     rows = grads.shape[0]
-    wide = pl.BlockSpec((block, MODEL), lambda i: (i, 0))
+    here = pl.BlockSpec((block, MODEL), lambda i, f, p: (i, 0))
     return pl.pallas_call(
-        partial_kernel,
+        functools.partial(partial_kernel, block),
         out_shape=jax.ShapeDtypeStruct((rows, MODEL), BF16),
-        grid=(rows // block,),
-        in_specs=[wide, pl.BlockSpec(w.shape, lambda i: (0, 0))],
-        out_specs=wide,
-        compiler_params=pltpu.CompilerParams(
-            dimension_semantics=("arbitrary",), vmem_limit_bytes=56 * 1024 * 1024
-        ),
-        cost_estimate=pl.CostEstimate(
-            flops=2 * rows * MODEL * MODEL, bytes_accessed=rows * 4096 + w.size * 2, transcendentals=0
-        ),
-        name="partial_rows",
-    )(grads, w)
-
-
-def event_kernel(block, lengths_ref, place_ref, got_ref, g_ref, out_ref, tiles_ref):
-    home = place_ref[0]
-
-    @pl.when(pl.program_id(0) == 0)
-    def _():
-        tiles_ref[0] = lax.fori_loop(0, lengths_ref.shape[1], lambda u, t: t + lengths_ref[home, u], jnp.int32(0))
-
-    row = lax.broadcasted_iota(jnp.int32, (block, WIDTH), 0) + pl.program_id(0) * block
-    g = jnp.where(row < tiles_ref[0] * TILE, g_ref[...].astype(F32), 0.0)
-    out_ref[...] = (got_ref[...].astype(F32) + g).astype(BF16)
-
-
-def event_rows(lengths, place, got, g):
-    block = 768
-    rows = g.shape[0]
-    wide = pl.BlockSpec((block, WIDTH), lambda i, f, p: (i, 0))
-    return pl.pallas_call(
-        functools.partial(event_kernel, block),
-        out_shape=jax.ShapeDtypeStruct((rows, WIDTH), BF16),
         grid_spec=pltpu.PrefetchScalarGridSpec(
             num_scalar_prefetch=2,
             grid=(rows // block,),
-            in_specs=[wide, pl.BlockSpec((block, WIDTH), lambda i, f, p: (i, p[2]))],
-            out_specs=wide,
+            in_specs=[
+                here,
+                pl.BlockSpec(w.shape, lambda i, f, p: (0, 0)),
+                pl.BlockSpec((block, WIDTH), lambda i, f, p: (i, p[2])),
+            ],
+            out_specs=here,
             scratch_shapes=[pltpu.SMEM((1,), jnp.int32)],
         ),
         compiler_params=pltpu.CompilerParams(
             dimension_semantics=("arbitrary",), vmem_limit_bytes=56 * 1024 * 1024
         ),
-        cost_estimate=pl.CostEstimate(flops=rows * 1024, bytes_accessed=rows * 1536, transcendentals=0),
-        name="event_rows",
-    )(lengths, place, got, g)
+        cost_estimate=pl.CostEstimate(
+            flops=2 * rows * MODEL * MODEL, bytes_accessed=rows * 4608 + w.size * 2, transcendentals=0
+        ),
+        name="partial_rows",
+    )(lengths, place, grads, w, g)
 
 
 def spread_kernel(got_ref, out_ref):
@@ -449,15 +431,14 @@
     swap = [(0, 1), (1, 0)]
     half = MODEL // 2
     other = lax.ppermute(sent, "c", swap)
-    shares = partial_rows(grads, weight_in)
+    shares = partial_rows(lengths, place, grads, weight_in, upstream)
+    event_grads = lax.psum_scatter(shares, "mp", scatter_dimension=1, tiled=True)
     kept = (kept + other.astype(F32)).astype(BF16)
-    got = lax.psum_scatter(shares, "mp", scatter_dimension=1, tiled=True)
     pieces = lax.all_to_all(kept.reshape(16, half // 16, COLUMNS), ("z", "y"), 0, 0, tiled=True)
     pieces = lax.all_to_all(spread(pieces), ("z", "y"), 0, 0, tiled=True).reshape(half, COLUMNS)
     other = lax.ppermute(pieces, "c", swap)
     weights = weights_out(place, pieces, None)
     proj_grad, out_grad, bias_grad, gain_grad = weights_out(place, other, weights)
-    event_grads = event_rows(lengths, place, got, upstream)
     return event_grads, proj_grad, bias_grad, gain_grad.reshape(WIDTH), out_grad
 
 

time: 148 us -> 143 us (0.966)
  Pallas kernels: 72.1 us -> 67.4 us
    pallas_call x2 -> x1, Pallas kernels: 16.5 us -> 11.9 us  [partial_rows(): pl.pallas_call(functools.partial(partial_kernel, block), out_shape=jax.Sh...]
where the time goes in v6:
time: 143 us
  Pallas kernels  67.4 us (47%)
  blocking collectives  52.1 us (36%)
  between operations  14.1 us (10%)
  waiting for transfers between devices  4.78 us (3%)
  starting transfers between devices  3.42 us (2%)
    pallas_call x1, Pallas kernels, layer(): pl.pallas_call(functools.partial(layer_kernel, steps), out_shape=[jax.Sha...  48.8 us
    all_to_all x1, blocking collectives, body(): lax.all_to_all(kept.reshape(16, half // 16, COLUMNS), ('z', 'y'), 0, 0, t...  28.4 us
    all_to_all x1, blocking collectives, body(): lax.all_to_all(spread(pieces), ('z', 'y'), 0, 0, tiled=True)  23.6 us
    pallas_call x1, Pallas kernels, partial_rows(): pl.pallas_call(functools.partial(partial_kernel, block), out_shape=jax.Sh...  11.9 us
    pallas_call x2, Pallas kernels, weights_out(): pl.pallas_call(functools.partial(weights_kernel, other), out_shape=[jax.S...  6.54 us
    ppermute x1, waiting for transfers between devices, body(): other = lax.ppermute(sent, 'c', swap)  3.06 us
  transfers between devices with their start and end apart: 3, of which 2 were waited for; matrix products, arithmetic and copies ran while one was open for 0% of the time, Pallas kernels for 5%

profile of v6, /device:TPU:1, one launch (start us, length us, event | category | flops | bytes accessed | tf_op | source)
XLA Modules:
  0.0 142.7 jit_solution(4817111195461271671)
XLA Ops:
  7.2 0.0 reduce-scatter.2.cloned.1.call-start
  7.2 0.6 pad_add_fusion.place_ref
  7.8 48.8 %layer.1 = (bf16[3072,1024]{1,0:T(8,128)(2,1)}, bf16[512,1408]{1,0:T(8,128)(2,1)}, f32[512,1408]{1,0:T(8,128)}, bf16[1024,1024]{1,0:T(8,128)(2,1)}) custom-call(s32[32,48]{1,0:T(8,128)} %lengths_ref.3, s32[3]{0:T(128)} %pad_add_fusion.place_ref, bf16[3072,1024]{1,0:T(8,128)(2,1)} %xp_ref.1, bf16[3072,1024]{1,0:T(8,128)(2,1)} %g_ref.3, ...), custom_call_target="tpu_custom_call" | custom-call | flops 18522046464 | bytes 24576000 | tf_op jit(solution)/shard_map/layer/pallas_call | solution.py:238
  56.6 11.9 %partial_rows.1 = bf16[3072,1024]{1,0:T(8,128)(2,1)} custom-call(s32[32,48]{1,0:T(8,128)} %lengths_ref.3, s32[3]{0:T(128)} %pad_add_fusion.place_ref, bf16[3072,1024]{1,0:T(8,128)(2,1)} %get-tuple-element.17.pg_ref, bf16[1024,1024]{1,0:T(8,128)(2,1)} %get-tuple-element.18.w_ref, bf16[3072,1024]{1,0:T(8,128)(2,1)} %g_ref.3), custom_call_target="tpu_custom_call" | custom-call | flops 6442450944 | bytes 16252928 | tf_op jit(solution)/shard_map/partial_rows/pallas_call | solution.py:311
  68.5 0.0 copy-start.1
  68.5 0.0 reduce-scatter.2.cloned.1.call-update
  68.5 1.5 %collective-permute-start = (bf16[512,1408]{1,0:T(8,128)(2,1)}, bf16[512,1408]{1,0:T(8,128)(2,1)S(1)}, u32[]{:S(2)}, u32[]{:S(2)}) collective-permute-start(bf16[512,1408]{1,0:T(8,128)(2,1)} %get-tuple-element.20), channel_id=1, source_target_pairs={{0,4},{4,0},{1,5},{5,1},{2,6},{6,2},{3,7},{7,3},{8,12},{12,8},{9,1... | collective-permute-start | bytes 4325384 | tf_op jit(solution)/shard_map/ppermute | solution.py:433
  70.0 3.1 %collective-permute-done = bf16[512,1408]{1,0:T(8,128)(2,1)S(1)} collective-permute-done((bf16[512,1408]{1,0:T(8,128)(2,1)}, bf16[512,1408]{1,0:T(8,128)(2,1)S(1)}, u32[]{:S(2)}, u32[]{:S(2)}) %collective-permute-start) | collective-permute-done | bytes 1441824 | tf_op jit(solution)/shard_map/ppermute | solution.py:433
  73.1 0.0 copy-done.1
  73.1 0.4 add_convert_fusion
  73.5 28.4 %all_to_all.10.got_ref = bf16[16,32,1408]{2,1,0:T(8,128)(2,1)S(1)} all-to-all(bf16[16,32,1408]{2,1,0:T(8,128)(2,1)S(1)} %bitcast.9), channel_id=1, replica_groups=mesh['z'=4,'y'=4,'c'=2,'mp'=4] {'z','y'}, dimensions={0} | all-to-all | bytes 2883584 | tf_op jit(solution)/shard_map/all_to_all | solution.py:437
  101.9 0.2 spread.1
  102.1 0.0 copy-start
  102.1 23.6 %all_to_all.11 = bf16[16,32,1408]{2,1,0:T(8,128)(2,1)S(1)} all-to-all(bf16[16,32,1408]{2,1,0:T(8,128)(2,1)S(1)} %spread.1), channel_id=1, replica_groups=mesh['z'=4,'y'=4,'c'=2,'mp'=4] {'z','y'}, dimensions={0} | all-to-all | bytes 2883584 | tf_op jit(solution)/shard_map/all_to_all | solution.py:438
  125.7 1.9 %collective-permute-start.1 = (bf16[512,1408]{1,0:T(8,128)(2,1)S(1)}, bf16[512,1408]{1,0:T(8,128)(2,1)S(1)}, u32[]{:S(2)}, u32[]{:S(2)}) collective-permute-start(bf16[512,1408]{1,0:T(8,128)(2,1)S(1)} %bitcast.7), channel_id=1, source_target_pairs={{0,4},{4,0},{1,5},{5,1},{2,6},{6,2},{3,7},{7,3},{8,12},{12,8},{9,1... | collective-permute-start | bytes 4325384 | tf_op jit(solution)/shard_map/ppermute | solution.py:439
  127.6 0.0 copy-done
  127.6 3.3 %weights_out.2 = (f32[1024,4,256]{2,1,0:T(4,128)}, f32[256,1024]{1,0:T(8,128)}, f32[4,256]{1,0:T(4,128)S(1)}, f32[1,256]{1,0:T(1,128)S(1)}) custom-call(s32[3]{0:T(128)S(1)} %copy-done, bf16[512,1408]{1,0:T(8,128)(2,1)S(1)} %bitcast.8), custom_call_target="tpu_custom_call" | custom-call | flops 2000000 | bytes 4200000 | tf_op jit(solution)/shard_map/weights_out/pallas_call | solution.py:398
  130.9 0.0 collective-permute-done.1.got_ref
  130.9 3.3 %weights_out.3 = (f32[1024,4,256]{2,1,0:T(4,128)}, f32[256,1024]{1,0:T(8,128)}, f32[4,256]{1,0:T(4,128)}, f32[1,256]{1,0:T(1,128)}) custom-call(s32[3]{0:T(128)S(1)} %copy-done, bf16[512,1408]{1,0:T(8,128)(2,1)S(1)} %collective-permute-done.1.got_ref, f32[1024,4,256]{2,1,0:T(4,128)} %get-tuple-element.21.refs_0_, ...), custom_call_target="tpu_custom_call", output_to_operand_aliasing={{0}: (2, {}), {1}: (3, {})} | custom-call | flops 2000000 | bytes 4200000 | tf_op jit(solution)/shard_map/weights_out/pallas_call | solution.py:398
  134.2 1.7 %reduce-scatter.2.cloned.1.call-done = bf16[3072,256]{1,0:T(8,128)(2,1)} async-done(((bf16[3072,1024]{1,0:T(8,128)(2,1)}), bf16[3072,256]{1,0:T(8,128)(2,1)}) %reduce-scatter.2.cloned.1.call-update) | async-done | bytes 1572880 | tf_op jit(solution)/shard_map/reduce_scatter | solution.py:435
Async XLA Ops:
  7.2 128.7 %reduce-scatter.2.cloned.1.call-start = ((), (), s32[]{:S(2)}) async-start(), calls=%async_computation.3 | async-start | bytes 7864320 | tf_op jit(solution)/shard_map/reduce_scatter | solution.py:435
  68.5 4.6 %copy-start.1 = (f32[512,1408]{1,0:T(8,128)S(1)}, f32[512,1408]{1,0:T(8,128)}, u32[]{:S(2)}) copy-start(f32[512,1408]{1,0:T(8,128)} %get-tuple-element.19) | copy-start | bytes 8650756
  68.5 4.6 %collective-permute-start = (bf16[512,1408]{1,0:T(8,128)(2,1)}, bf16[512,1408]{1,0:T(8,128)(2,1)S(1)}, u32[]{:S(2)}, u32[]{:S(2)}) collective-permute-start(bf16[512,1408]{1,0:T(8,128)(2,1)} %get-tuple-element.20), channel_id=1, source_target_pairs={{0,4},{4,0},{1,5},{5,1},{2,6},{6,2},{3,7},{7,3},{8,12},{12,8},{9,1... | collective-permute-start | bytes 4325384 | tf_op jit(solution)/shard_map/ppermute | solution.py:433
  102.1 25.5 %copy-start = (s32[3]{0:T(128)S(1)}, s32[3]{0:T(128)}, u32[]{:S(2)}) copy-start(s32[3]{0:T(128)} %pad_add_fusion.place_ref) | copy-start | bytes 40
  125.7 5.1 %collective-permute-start.1 = (bf16[512,1408]{1,0:T(8,128)(2,1)S(1)}, bf16[512,1408]{1,0:T(8,128)(2,1)S(1)}, u32[]{:S(2)}, u32[]{:S(2)}) collective-permute-start(bf16[512,1408]{1,0:T(8,128)(2,1)S(1)} %bitcast.7), channel_id=1, source_target_pairs={{0,4},{4,0},{1,5},{5,1},{2,6},{6,2},{3,7},{7,3},{8,12},{12,8},{9,1... | collective-permute-start | bytes 4325384 | tf_op jit(solution)/shard_map/ppermute | solution.py:439
Sparse Core Ops, SparseCore 0:
  68.7 67.1 reduce-scatter.1

commit v7 on v6

--- a/solution.py
+++ b/solution.py
@@ -301,7 +301,7 @@
     for d in range(4):
         cols = slice(d * WIDTH, (d + 1) * WIDTH)
         g = jnp.where(row < jnp.where(me == d, tiles_ref[0] * TILE, 0), g_ref[...].astype(F32), 0.0)
-        out_ref[:, cols] = (dot(grads, w_ref[cols, :], NT) + g).astype(BF16)
+        out_ref[d] = (dot(grads, w_ref[cols, :], NT) + g).astype(BF16)
 
 
 def partial_rows(lengths, place, grads, w, g):
@@ -310,7 +310,7 @@
     here = pl.BlockSpec((block, MODEL), lambda i, f, p: (i, 0))
     return pl.pallas_call(
         functools.partial(partial_kernel, block),
-        out_shape=jax.ShapeDtypeStruct((rows, MODEL), BF16),
+        out_shape=jax.ShapeDtypeStruct((4, rows, WIDTH), BF16),
         grid_spec=pltpu.PrefetchScalarGridSpec(
             num_scalar_prefetch=2,
             grid=(rows // block,),
@@ -319,7 +319,7 @@
                 pl.BlockSpec(w.shape, lambda i, f, p: (0, 0)),
                 pl.BlockSpec((block, WIDTH), lambda i, f, p: (i, p[2])),
             ],
-            out_specs=here,
+            out_specs=pl.BlockSpec((4, block, WIDTH), lambda i, f, p: (0, i, 0)),
             scratch_shapes=[pltpu.SMEM((1,), jnp.int32)],
         ),
         compiler_params=pltpu.CompilerParams(
@@ -432,7 +432,7 @@
     half = MODEL // 2
     other = lax.ppermute(sent, "c", swap)
     shares = partial_rows(lengths, place, grads, weight_in, upstream)
-    event_grads = lax.psum_scatter(shares, "mp", scatter_dimension=1, tiled=True)
+    event_grads = lax.psum_scatter(shares, "mp", scatter_dimension=0, tiled=False)
     kept = (kept + other.astype(F32)).astype(BF16)
     pieces = lax.all_to_all(kept.reshape(16, half // 16, COLUMNS), ("z", "y"), 0, 0, tiled=True)
     pieces = lax.all_to_all(spread(pieces), ("z", "y"), 0, 0, tiled=True).reshape(half, COLUMNS)

time: 143 us -> 143 us (level)
  no operation moved by 1% of the time
where the time goes in v7:
time: 143 us
  Pallas kernels  67.4 us (47%)
  blocking collectives  52.1 us (36%)
  between operations  14.1 us (10%)
  waiting for transfers between devices  4.78 us (3%)
  starting transfers between devices  3.42 us (2%)
    pallas_call x1, Pallas kernels, layer(): pl.pallas_call(functools.partial(layer_kernel, steps), out_shape=[jax.Sha...  48.8 us
    all_to_all x1, blocking collectives, body(): lax.all_to_all(kept.reshape(16, half // 16, COLUMNS), ('z', 'y'), 0, 0, t...  28.4 us
    all_to_all x1, blocking collectives, body(): lax.all_to_all(spread(pieces), ('z', 'y'), 0, 0, tiled=True)  23.6 us
    pallas_call x1, Pallas kernels, partial_rows(): pl.pallas_call(functools.partial(partial_kernel, block), out_shape=jax.Sh...  11.9 us
    pallas_call x2, Pallas kernels, weights_out(): pl.pallas_call(functools.partial(weights_kernel, other), out_shape=[jax.S...  6.54 us
    ppermute x1, waiting for transfers between devices, body(): other = lax.ppermute(sent, 'c', swap)  3.06 us
  transfers between devices with their start and end apart: 3, of which 2 were waited for; matrix products, arithmetic and copies ran while one was open for 0% of the time, Pallas kernels for 5%

profile of v7, /device:TPU:1, one launch (start us, length us, event | category | flops | bytes accessed | tf_op | source)
XLA Modules:
  0.0 142.7 jit_solution(4015032946503209872)
XLA Ops:
  7.2 0.0 reduce-scatter.2.cloned.1.call-start
  7.2 0.6 pad_add_fusion.place_ref
  7.8 48.8 %layer.1 = (bf16[3072,1024]{1,0:T(8,128)(2,1)}, bf16[512,1408]{1,0:T(8,128)(2,1)}, f32[512,1408]{1,0:T(8,128)}, bf16[1024,1024]{1,0:T(8,128)(2,1)}) custom-call(s32[32,48]{1,0:T(8,128)} %lengths_ref.3, s32[3]{0:T(128)} %pad_add_fusion.place_ref, bf16[3072,1024]{1,0:T(8,128)(2,1)} %xp_ref.1, bf16[3072,1024]{1,0:T(8,128)(2,1)} %g_ref.3, ...), custom_call_target="tpu_custom_call" | custom-call | flops 18522046464 | bytes 24576000 | tf_op jit(solution)/shard_map/layer/pallas_call | solution.py:238
  56.6 11.9 %partial_rows.1 = bf16[4,3072,256]{2,1,0:T(8,128)(2,1)} custom-call(s32[32,48]{1,0:T(8,128)} %lengths_ref.3, s32[3]{0:T(128)} %pad_add_fusion.place_ref, bf16[3072,1024]{1,0:T(8,128)(2,1)} %get-tuple-element.17.pg_ref, bf16[1024,1024]{1,0:T(8,128)(2,1)} %get-tuple-element.18.w_ref, bf16[3072,1024]{1,0:T(8,128)(2,1)} %g_ref.3), custom_call_target="tpu_custom_call" | custom-call | flops 6442450944 | bytes 16252928 | tf_op jit(solution)/shard_map/partial_rows/pallas_call | solution.py:311
  68.5 0.0 copy-start.1
  68.5 0.0 reduce-scatter.2.cloned.1.call-update
  68.5 1.5 %collective-permute-start = (bf16[512,1408]{1,0:T(8,128)(2,1)}, bf16[512,1408]{1,0:T(8,128)(2,1)S(1)}, u32[]{:S(2)}, u32[]{:S(2)}) collective-permute-start(bf16[512,1408]{1,0:T(8,128)(2,1)} %get-tuple-element.20), channel_id=1, source_target_pairs={{0,4},{4,0},{1,5},{5,1},{2,6},{6,2},{3,7},{7,3},{8,12},{12,8},{9,1... | collective-permute-start | bytes 4325384 | tf_op jit(solution)/shard_map/ppermute | solution.py:433
  70.0 3.1 %collective-permute-done = bf16[512,1408]{1,0:T(8,128)(2,1)S(1)} collective-permute-done((bf16[512,1408]{1,0:T(8,128)(2,1)}, bf16[512,1408]{1,0:T(8,128)(2,1)S(1)}, u32[]{:S(2)}, u32[]{:S(2)}) %collective-permute-start) | collective-permute-done | bytes 1441824 | tf_op jit(solution)/shard_map/ppermute | solution.py:433
  73.1 0.0 copy-done.1
  73.1 0.4 add_convert_fusion
  73.4 28.4 %all_to_all.10.got_ref = bf16[16,32,1408]{2,1,0:T(8,128)(2,1)S(1)} all-to-all(bf16[16,32,1408]{2,1,0:T(8,128)(2,1)S(1)} %bitcast.10), channel_id=1, replica_groups=mesh['z'=4,'y'=4,'c'=2,'mp'=4] {'z','y'}, dimensions={0} | all-to-all | bytes 2883584 | tf_op jit(solution)/shard_map/all_to_all | solution.py:437
  101.9 0.2 spread.1
  102.1 0.0 copy-start
  102.1 23.6 %all_to_all.11 = bf16[16,32,1408]{2,1,0:T(8,128)(2,1)S(1)} all-to-all(bf16[16,32,1408]{2,1,0:T(8,128)(2,1)S(1)} %spread.1), channel_id=1, replica_groups=mesh['z'=4,'y'=4,'c'=2,'mp'=4] {'z','y'}, dimensions={0} | all-to-all | bytes 2883584 | tf_op jit(solution)/shard_map/all_to_all | solution.py:438
  125.7 1.9 %collective-permute-start.1 = (bf16[512,1408]{1,0:T(8,128)(2,1)S(1)}, bf16[512,1408]{1,0:T(8,128)(2,1)S(1)}, u32[]{:S(2)}, u32[]{:S(2)}) collective-permute-start(bf16[512,1408]{1,0:T(8,128)(2,1)S(1)} %bitcast.8), channel_id=1, source_target_pairs={{0,4},{4,0},{1,5},{5,1},{2,6},{6,2},{3,7},{7,3},{8,12},{12,8},{9,1... | collective-permute-start | bytes 4325384 | tf_op jit(solution)/shard_map/ppermute | solution.py:439
  127.6 0.0 copy-done
  127.6 3.3 %weights_out.2 = (f32[1024,4,256]{2,1,0:T(4,128)}, f32[256,1024]{1,0:T(8,128)}, f32[4,256]{1,0:T(4,128)S(1)}, f32[1,256]{1,0:T(1,128)S(1)}) custom-call(s32[3]{0:T(128)S(1)} %copy-done, bf16[512,1408]{1,0:T(8,128)(2,1)S(1)} %bitcast.9), custom_call_target="tpu_custom_call" | custom-call | flops 2000000 | bytes 4200000 | tf_op jit(solution)/shard_map/weights_out/pallas_call | solution.py:398
  130.9 0.0 collective-permute-done.1.got_ref
  130.9 3.3 %weights_out.3 = (f32[1024,4,256]{2,1,0:T(4,128)}, f32[256,1024]{1,0:T(8,128)}, f32[4,256]{1,0:T(4,128)}, f32[1,256]{1,0:T(1,128)}) custom-call(s32[3]{0:T(128)S(1)} %copy-done, bf16[512,1408]{1,0:T(8,128)(2,1)S(1)} %collective-permute-done.1.got_ref, f32[1024,4,256]{2,1,0:T(4,128)} %get-tuple-element.21.refs_0_, ...), custom_call_target="tpu_custom_call", output_to_operand_aliasing={{0}: (2, {}), {1}: (3, {})} | custom-call | flops 2000000 | bytes 4200000 | tf_op jit(solution)/shard_map/weights_out/pallas_call | solution.py:398
  134.2 1.7 %reduce-scatter.2.cloned.1.call-done = bf16[1,3072,256]{2,1,0:T(8,128)(2,1)} async-done(((bf16[4,3072,256]{2,1,0:T(8,128)(2,1)}), bf16[1,3072,256]{2,1,0:T(8,128)(2,1)}) %reduce-scatter.2.cloned.1.call-update) | async-done | bytes 1572880 | tf_op jit(solution)/shard_map/reduce_scatter | solution.py:435
Async XLA Ops:
  7.2 128.7 %reduce-scatter.2.cloned.1.call-start = ((), (), s32[]{:S(2)}) async-start(), calls=%async_computation.3 | async-start | bytes 7864320 | tf_op jit(solution)/shard_map/reduce_scatter | solution.py:435
  68.5 4.6 %copy-start.1 = (f32[512,1408]{1,0:T(8,128)S(1)}, f32[512,1408]{1,0:T(8,128)}, u32[]{:S(2)}) copy-start(f32[512,1408]{1,0:T(8,128)} %get-tuple-element.19) | copy-start | bytes 8650756
  68.5 4.6 %collective-permute-start = (bf16[512,1408]{1,0:T(8,128)(2,1)}, bf16[512,1408]{1,0:T(8,128)(2,1)S(1)}, u32[]{:S(2)}, u32[]{:S(2)}) collective-permute-start(bf16[512,1408]{1,0:T(8,128)(2,1)} %get-tuple-element.20), channel_id=1, source_target_pairs={{0,4},{4,0},{1,5},{5,1},{2,6},{6,2},{3,7},{7,3},{8,12},{12,8},{9,1... | collective-permute-start | bytes 4325384 | tf_op jit(solution)/shard_map/ppermute | solution.py:433
  102.1 25.5 %copy-start = (s32[3]{0:T(128)S(1)}, s32[3]{0:T(128)}, u32[]{:S(2)}) copy-start(s32[3]{0:T(128)} %pad_add_fusion.place_ref) | copy-start | bytes 40
  125.7 5.1 %collective-permute-start.1 = (bf16[512,1408]{1,0:T(8,128)(2,1)S(1)}, bf16[512,1408]{1,0:T(8,128)(2,1)S(1)}, u32[]{:S(2)}, u32[]{:S(2)}) collective-permute-start(bf16[512,1408]{1,0:T(8,128)(2,1)S(1)} %bitcast.8), channel_id=1, source_target_pairs={{0,4},{4,0},{1,5},{5,1},{2,6},{6,2},{3,7},{7,3},{8,12},{12,8},{9,1... | collective-permute-start | bytes 4325384 | tf_op jit(solution)/shard_map/ppermute | solution.py:439
Sparse Core Ops, SparseCore 0:
  68.6 67.1 reduce-scatter.1
